TPU v7x, 512 devices: a whole 4x4x16 slice. The times are simulated.
512 devices in a mesh: dp: 32 (over y_lo, z), mp: 16 (over x, y_hi, core).
Axes of the slice: x: 4, y: 4 (y_hi: 2, y_lo: 2; y = y_hi * 2 + y_lo), z: 16, core: 2. Of those that a mesh axis runs over, the one named last changes fastest.
Arguments:
- tokens_home: bfloat16 [49152, 4608], P('dp', 'mp'), may hold values from -7 to 7
- q_weight: bfloat16 [4608, 2048], P(None, 'mp'), may hold values from -2 to 2
- kv_weight: bfloat16 [4608, 2048], P(None, 'mp'), may hold values from -2 to 2
- pair_tokens: int32 [128, 2], replicated, may hold values from 1 to 383, as said below
- pair_target: int32 [128], replicated, may hold values from 0 to 31, as said below
- margins: float32 [128], replicated, may hold values from -20 to 20
- grad_attended: bfloat16 [16384, 2048], P('dp', 'mp'), may hold values from -48 to 48
Outputs:
- attended: bfloat16 [16384, 2048], P('dp', 'mp')
- grad_home: bfloat16 [49152, 4608], P('dp', 'mp')
Inputs may be any that keep to these rules, and one draw needn't show every extreme that they name: `pair_tokens`: each pair has 1 or more chosen and 1 or more rejected tokens and at most 384 tokens in all; the pairs of one home replica hold at most 1536 tokens together, and the pairs processed by one replica hold exactly 512 tokens together. `pair_target`: replica s sends exactly one of its 4 pairs to each of the replicas s, s + 1, ..., s + 3, counted modulo the number of replicas; which of its pairs goes where varies.
All inputs are finite; a program needn't handle non-finite values.
Results may differ from a plain program's by a relative error of at most 0.022.
Values may be sent and summed in bfloat16 or wider, within the bound.
No kernel may reach another device: no remote copies, remote signals or barrier semaphores. Data moves between devices by JAX's collectives and lax.ppermute only.
A program may use at most 64 MiB of HBM per device.

v0:
```python
import jax
import jax.numpy as jnp
from jax import lax
from jax.sharding import PartitionSpec as P

SPREAD = 4
RECV = 512
CAP = 384
HOME = 1536


BETA = 0.1
SOFT_CAP = 50.0
ROPE_BASE = 10000.0
QUERY_SCALE = 1.0 / 12.0


def shifted(value, axis, steps):
    count = lax.axis_size(axis)
    pairs = [(source, (source + steps) % count) for source in range(count)]
    return lax.ppermute(value, axis, pairs)


def from_partner(value, axis, apart):
    mask = 2**apart
    pairs = [(source, source ^ mask) for source in range(lax.axis_size(axis))]
    return lax.ppermute(value, axis, pairs)


def rotate(values, position, heading):
    half_size = values.shape[-1] // 2
    frequency = jnp.exp(-jnp.log(ROPE_BASE) * jnp.arange(half_size).astype(jnp.float32) / half_size)
    angles = position.astype(jnp.float32)[:, None] * frequency[None, :]
    cosine = jnp.cos(angles)
    sine_part = heading * jnp.sin(angles)
    leading = values[..., :half_size]
    trailing = values[..., half_size:]
    return jnp.concatenate(
        [leading * cosine - trailing * sine_part, trailing * cosine + leading * sine_part], axis=-1
    )


def route(slot_rows, heading):
    slot_count = slot_rows.shape[0]
    delivered = [slot_rows[0]]
    for offset in range(1, slot_count):
        delivered.append(shifted(slot_rows[offset], "dp", heading * offset))
    return jnp.stack(delivered)


def body(tokens_home, q_weight, kv_weight, pair_tokens, pair_target, margins, grad_attended):
    replicas = lax.axis_size("dp")
    replica = lax.axis_index("dp")
    width_local = tokens_home.shape[1]
    slot_ids = jnp.arange(SPREAD, dtype=jnp.int32)
    tokens = pair_tokens.reshape(replicas, SPREAD, 2)
    target = pair_target.reshape(replicas, SPREAD)
    mine_tokens = tokens[replica]
    mine_offset = jnp.mod(target[replica] - replica, replicas)
    mine_sizes = mine_tokens[:, 0] + mine_tokens[:, 1]
    mine_start = jnp.cumsum(mine_sizes) - mine_sizes
    by_offset = (mine_offset[None, :] == slot_ids[:, None]).astype(jnp.int32)
    send_start = jnp.sum(by_offset * mine_start[None, :], axis=1)
    send_size = jnp.sum(by_offset * mine_sizes[None, :], axis=1)
    slot_place = jnp.arange(CAP, dtype=jnp.int32)
    home_index = jnp.clip(send_start[:, None] + slot_place[None, :], 0, HOME - 1)
    slot_live = slot_place[None, :] < send_size[:, None]
    outbound = jnp.take(tokens_home, home_index.reshape(-1), axis=0).reshape(
        SPREAD, CAP, width_local
    )
    outbound = jnp.where(slot_live[:, :, None], outbound, jnp.zeros_like(outbound))
    arrived = route(outbound, 1)
    anchor = jnp.mod(replica - slot_ids, replicas)
    from_anchor = (target[anchor] == replica).astype(jnp.int32)
    anchor_tokens = tokens[anchor]
    chosen_in = jnp.sum(from_anchor * anchor_tokens[:, :, 0], axis=1)
    sizes_in = chosen_in + jnp.sum(from_anchor * anchor_tokens[:, :, 1], axis=1)
    margin_in = jnp.sum(
        from_anchor.astype(jnp.float32) * margins.reshape(replicas, SPREAD)[anchor], axis=1
    )
    starts_in = jnp.cumsum(sizes_in) - sizes_in
    row_ids = jnp.arange(RECV, dtype=jnp.int32)
    slot_of = jnp.sum((row_ids[:, None] >= starts_in[None, :]).astype(jnp.int32), axis=1) - 1
    row_slot = (slot_of[:, None] == slot_ids[None, :]).astype(jnp.int32)
    start_row = jnp.sum(row_slot * starts_in[None, :], axis=1)
    chosen_row = jnp.sum(row_slot * chosen_in[None, :], axis=1)
    margin_row = jnp.sum(row_slot.astype(jnp.float32) * margin_in[None, :], axis=1)
    within_pair = row_ids - start_row
    rejected_row = (within_pair >= chosen_row).astype(jnp.int32)
    position = within_pair - rejected_row * chosen_row
    segment = 2 * slot_of + rejected_row
    moved_rows = jnp.take(
        arrived.reshape(SPREAD * CAP, width_local), slot_of * CAP + within_pair, axis=0
    )
    piece = lax.all_gather(moved_rows, "mp", axis=1, tiled=True)
    proj_q = jnp.dot(piece, q_weight, preferred_element_type=jnp.float32)
    proj_kv = jnp.dot(piece, kv_weight, preferred_element_type=jnp.float32)
    holds_key = jnp.mod(lax.axis_index("mp"), 2) == 0
    queries = (QUERY_SCALE * rotate(proj_q, position, 1.0)).astype(jnp.bfloat16)
    own_part = jnp.where(holds_key, rotate(proj_kv, position, 1.0), proj_kv).astype(jnp.bfloat16)
    partner = from_partner(own_part, "mp", 0)
    key_rows = jnp.where(holds_key, own_part, partner)
    values = jnp.where(holds_key, partner, own_part)
    contract_last = (((1,), (1,)), ((), ()))
    contract_first = (((0,), (0,)), ((), ()))
    scores = lax.dot_general(queries, key_rows, contract_last, preferred_element_type=jnp.float32)
    capped = SOFT_CAP * jnp.tanh(scores / SOFT_CAP)
    allowed = (segment[:, None] == segment[None, :]) & (position[None, :] <= position[:, None])
    exponent = jnp.where(allowed, jnp.exp(capped), 0.0)
    weights = exponent / jnp.sum(exponent, axis=1, keepdims=True)
    prob_rows = weights.astype(jnp.bfloat16)
    attended = jnp.dot(prob_rows, values, preferred_element_type=jnp.float32).astype(jnp.bfloat16)
    coef_row = (
        BETA * jax.nn.sigmoid(-BETA * margin_row) * (2 * rejected_row - 1).astype(jnp.float32)
    )
    upstream = (coef_row[:, None] * grad_attended.astype(jnp.float32)).astype(jnp.bfloat16)
    dprobs = lax.dot_general(upstream, values, contract_last, preferred_element_type=jnp.float32)
    delta_row = jnp.sum(weights * dprobs, axis=1, keepdims=True)
    dscores = (weights * (dprobs - delta_row) * (1.0 - jnp.square(capped / SOFT_CAP))).astype(
        jnp.bfloat16
    )
    dquery = jnp.dot(dscores, key_rows, preferred_element_type=jnp.float32)
    dquery = (QUERY_SCALE * rotate(dquery, position, -1.0)).astype(jnp.bfloat16)
    dkey_part = rotate(
        lax.dot_general(dscores, queries, contract_first, preferred_element_type=jnp.float32),
        position,
        -1.0,
    )
    dvalue_part = lax.dot_general(
        prob_rows, upstream, contract_first, preferred_element_type=jnp.float32
    )
    handed = jnp.where(holds_key, dvalue_part, dkey_part)
    received = from_partner(handed.astype(jnp.bfloat16), "mp", 0).astype(handed.dtype)
    own_grad = (jnp.where(holds_key, dkey_part, dvalue_part) + received).astype(jnp.bfloat16)
    partial_sum = lax.dot_general(
        dquery, q_weight, contract_last, preferred_element_type=jnp.float32
    ) + lax.dot_general(own_grad, kv_weight, contract_last, preferred_element_type=jnp.float32)
    summed = lax.psum_scatter(
        partial_sum.astype(jnp.bfloat16), "mp", scatter_dimension=1, tiled=True
    )
    back_index = jnp.clip(starts_in[:, None] + slot_place[None, :], 0, RECV - 1)
    back_live = slot_place[None, :] < sizes_in[:, None]
    returning = jnp.take(summed, back_index.reshape(-1), axis=0).reshape(SPREAD, CAP, width_local)
    returning = jnp.where(back_live[:, :, None], returning, jnp.zeros_like(returning))
    homeward = route(returning, -1)
    places = jnp.arange(HOME, dtype=jnp.int32)
    pair_at = jnp.sum((places[:, None] >= mine_start[None, :]).astype(jnp.int32), axis=1) - 1
    pair_hot = (pair_at[:, None] == slot_ids[None, :]).astype(jnp.int32)
    start_home = jnp.sum(pair_hot * mine_start[None, :], axis=1)
    offset_home = jnp.sum(pair_hot * mine_offset[None, :], axis=1)
    home_live = places < jnp.sum(mine_sizes)
    flat_index = jnp.where(home_live, offset_home * CAP + places - start_home, 0)
    grad_home = jnp.take(homeward.reshape(SPREAD * CAP, width_local), flat_index, axis=0)
    grad_home = jnp.where(home_live[:, None], grad_home, jnp.zeros_like(grad_home))
    return (attended, grad_home)


def solution(mesh):
    return jax.shard_map(
        body,
        mesh=mesh,
        in_specs=(P("dp", "mp"), P(None, "mp"), P(None, "mp"), P(), P(), P(), P("dp", "mp")),
        out_specs=(P("dp", "mp"), P("dp", "mp")),
        check_vma=False,
    )
```

profile of v0, /device:TPU:6, one launch (start us, length us, event | category | flops | bytes accessed | tf_op | source)
XLA Modules:
  0.0 334.4 jit_solution(10592844408114828122)
XLA Ops:
  11.1 1.6 copy.29
  14.0 4.8 %gather_fusion.5 = bf16[1536,288]{1,0:T(8,128)(2,1)S(1)} fusion(bf16[1536,288]{1,0:T(8,128)(2,1)S(1)} %copy.29, s32[2048]{0:T(1024)} %pad_clamp_fusion.2), kind=kCustom, calls=%fused_computation.clone | custom fusion | bytes 1775616 | tf_op jit(solution)/shard_map/jit(_take)/gather | solution.py:68
  18.8 1.0 broadcast_select_fusion
  20.2 6.5 %collective-permute-start.2 = (bf16[384,288]{1,0:T(8,128)(2,1)S(1)}, bf16[384,288]{1,0:T(8,128)(2,1)S(1)}, u32[]{:S(2)}, u32[]{:S(2)}) collective-permute-start(bf16[384,288]{1,0:T(8,128)(2,1)S(1)} %get-tuple-element.34), channel_id=1, source_target_pairs={{0,48},{16,64},{32,80},{48,96},{64,112},{80,128},{96,144},{112,160... | collective-permute-start | bytes 663560 | tf_op jit(solution)/shard_map/ppermute | solution.py:21
  26.8 6.4 %collective-permute-start.1 = (bf16[384,288]{1,0:T(8,128)(2,1)S(1)}, bf16[384,288]{1,0:T(8,128)(2,1)S(1)}, u32[]{:S(2)}, u32[]{:S(2)}) collective-permute-start(bf16[384,288]{1,0:T(8,128)(2,1)S(1)} %get-tuple-element.35), channel_id=1, source_target_pairs={{0,32},{16,48},{32,64},{48,80},{64,96},{80,112},{96,128},{112,144}... | collective-permute-start | bytes 663560 | tf_op jit(solution)/shard_map/ppermute | solution.py:21
  33.2 3.8 %collective-permute-start = (bf16[384,288]{1,0:T(8,128)(2,1)S(1)}, bf16[384,288]{1,0:T(8,128)(2,1)S(1)}, u32[]{:S(2)}, u32[]{:S(2)}) collective-permute-start(bf16[384,288]{1,0:T(8,128)(2,1)S(1)} %get-tuple-element.36), channel_id=1, source_target_pairs={{0,16},{16,32},{32,48},{48,64},{64,80},{80,96},{96,112},{112,128},... | collective-permute-start | bytes 663560 | tf_op jit(solution)/shard_map/ppermute | solution.py:21
  41.2 11.7 %collective-permute-done.2 = bf16[384,288]{1,0:T(8,128)(2,1)S(1)} collective-permute-done((bf16[384,288]{1,0:T(8,128)(2,1)S(1)}, bf16[384,288]{1,0:T(8,128)(2,1)S(1)}, u32[]{:S(2)}, u32[]{:S(2)}) %collective-permute-start.2) | collective-permute-done | bytes 221216 | tf_op jit(solution)/shard_map/ppermute | solution.py:21
  52.9 12.4 %collective-permute-done.1 = bf16[384,288]{1,0:T(8,128)(2,1)S(1)} collective-permute-done((bf16[384,288]{1,0:T(8,128)(2,1)S(1)}, bf16[384,288]{1,0:T(8,128)(2,1)S(1)}, u32[]{:S(2)}, u32[]{:S(2)}) %collective-permute-start.1) | collective-permute-done | bytes 221216 | tf_op jit(solution)/shard_map/ppermute | solution.py:21
  65.3 6.1 %collective-permute-done = bf16[384,288]{1,0:T(8,128)(2,1)S(1)} collective-permute-done((bf16[384,288]{1,0:T(8,128)(2,1)S(1)}, bf16[384,288]{1,0:T(8,128)(2,1)S(1)}, u32[]{:S(2)}, u32[]{:S(2)}) %collective-permute-start) | collective-permute-done | bytes 221216 | tf_op jit(solution)/shard_map/ppermute | solution.py:21
  71.7 1.9 gather_fusion.2
  73.8 0.9 copy.30
  74.8 70.7 %all-gather.2.cloned.1.call-done = bf16[512,4608]{0,1:T(8,128)(2,1)} async-done(((bf16[512,288]{0,1:T(8,128)(2,1)}), bf16[512,4608]{0,1:T(8,128)(2,1)}) %all-gather.2.cloned.1.call-update) | async-done | bytes 4718608 | tf_op jit(solution)/shard_map/all_gather | solution.py:95
  145.5 3.7 %fusion.66 = f32[512,128]{0,1:T(8,128)S(1)} fusion(bf16[512,4608]{0,1:T(8,128)(2,1)} %all-gather.2.cloned.1.call-done, bf16[4608,128]{1,0:T(8,128)(2,1)} %param.11), kind=kOutput, calls=%fused_computation.154 | convolution fusion | flops 603979776 | bytes 6160384 | tf_op jit(solution)/shard_map/dot_general | solution.py:97
  149.8 2.1 collective-permute-start.3
  152.0 0.9 fusion.65
  157.2 2.4 collective-permute-start.4
  159.6 1.4 fusion.34
  161.0 3.5 %add_convert_fusion = bf16[512,4608]{0,1:T(8,128)(2,1)} fusion(f32[512,4608]{0,1:T(8,128)S(1)} %fusion.34, bf16[4608,128]{1,0:T(8,128)(2,1)S(1)} %copy-done.1, bf16[512,128]{0,1:T(8,128)(2,1)S(1)} %collective-permute-done.4, f32[512,128]{0,1:T(8,128)S(1)} %get-tuple-element.58, f32[512,64]{0,1:T(8,128)S(1)} %get-tuple-element.38, ...), kind=kOutput, calls=%fused_computation.7 | convolution fusion | flops 609026048 | bytes 15990785 | tf_op jit(solution)/shard_map/dot_general | solution.py:137
  165.6 1.3 compare_and_fusion
  167.0 102.7 %reduce-scatter.2.cloned.1.call-done = bf16[512,288]{0,1:T(8,128)(2,1)} async-done(((bf16[512,4608]{0,1:T(8,128)(2,1)}), bf16[512,288]{0,1:T(8,128)(2,1)}) %reduce-scatter.2.cloned.1.call-update) | async-done | bytes 294928 | tf_op jit(solution)/shard_map/reduce_scatter | solution.py:138
  269.7 1.2 copy.33
  270.9 4.7 %gather_fusion.4 = bf16[1536,288]{1,0:T(8,128)(2,1)S(1)} fusion(bf16[512,288]{1,0:T(8,128)(2,1)S(1)} %copy.33, s32[2048]{0:T(1024)S(1)} %pad_clamp_fusion.1), kind=kCustom, calls=%fused_computation.6 | custom fusion | bytes 1775616 | tf_op jit(solution)/shard_map/jit(_take)/gather | solution.py:143
  276.4 7.7 %collective-permute-start.7 = (bf16[384,288]{1,0:T(8,128)(2,1)S(1)}, bf16[384,288]{1,0:T(8,128)(2,1)S(1)}, u32[]{:S(2)}, u32[]{:S(2)}) collective-permute-start(bf16[384,288]{1,0:T(8,128)(2,1)S(1)} %get-tuple-element.30), channel_id=1, source_target_pairs={{0,464},{16,480},{32,496},{48,0},{64,16},{80,32},{96,48},{112,64},... | collective-permute-start | bytes 663560 | tf_op jit(solution)/shard_map/ppermute | solution.py:21
  284.2 5.3 %collective-permute-start.6 = (bf16[384,288]{1,0:T(8,128)(2,1)S(1)}, bf16[384,288]{1,0:T(8,128)(2,1)S(1)}, u32[]{:S(2)}, u32[]{:S(2)}) collective-permute-start(bf16[384,288]{1,0:T(8,128)(2,1)S(1)} %get-tuple-element.31), channel_id=1, source_target_pairs={{0,480},{16,496},{32,0},{48,16},{64,32},{80,48},{96,64},{112,80},{... | collective-permute-start | bytes 663560 | tf_op jit(solution)/shard_map/ppermute | solution.py:21
  289.4 3.3 collective-permute-start.5
  292.8 1.3 convolution_convert_fusion
  294.0 12.4 %collective-permute-done.7 = bf16[384,288]{1,0:T(8,128)(2,1)S(1)} collective-permute-done((bf16[384,288]{1,0:T(8,128)(2,1)S(1)}, bf16[384,288]{1,0:T(8,128)(2,1)S(1)}, u32[]{:S(2)}, u32[]{:S(2)}) %collective-permute-start.7) | collective-permute-done | bytes 221216 | tf_op jit(solution)/shard_map/ppermute | solution.py:21
  306.4 8.4 %collective-permute-done.6 = bf16[384,288]{1,0:T(8,128)(2,1)S(1)} collective-permute-done((bf16[384,288]{1,0:T(8,128)(2,1)S(1)}, bf16[384,288]{1,0:T(8,128)(2,1)S(1)}, u32[]{:S(2)}, u32[]{:S(2)}) %collective-permute-start.6) | collective-permute-done | bytes 221216 | tf_op jit(solution)/shard_map/ppermute | solution.py:21
  314.8 5.2 %collective-permute-done.5 = bf16[384,288]{1,0:T(8,128)(2,1)S(1)} collective-permute-done((bf16[384,288]{1,0:T(8,128)(2,1)S(1)}, bf16[384,288]{1,0:T(8,128)(2,1)S(1)}, u32[]{:S(2)}, u32[]{:S(2)}) %collective-permute-start.5) | collective-permute-done | bytes 221216 | tf_op jit(solution)/shard_map/ppermute | solution.py:21
  320.3 4.7 %gather_fusion.6 = bf16[1536,288]{1,0:T(8,128)(2,1)S(1)} fusion(bf16[1536,288]{1,0:T(8,128)(2,1)S(1)} %bitcast.54, s32[2048]{0:T(1024)S(1)} %pad_clamp_fusion), kind=kCustom, calls=%fused_computation.1.clone | custom fusion | bytes 1775616 | tf_op jit(solution)/shard_map/jit(_take)/gather | solution.py:153
  325.1 1.1 select_select_fusion
  326.2 1.3 copy.34
  (113 shorter events, 17.1 us)
Async XLA Ops:
  7.2 144.8 %copy-start = (bf16[4608,128]{1,0:T(8,128)(2,1)S(1)}, bf16[4608,128]{1,0:T(8,128)(2,1)}, u32[]{:S(2)}) copy-start(bf16[4608,128]{1,0:T(8,128)(2,1)} %param.10) | copy-start | bytes 3538948
  7.2 138.3 %all-gather.2.cloned.1.call-start = ((), (), s32[]{:S(2)}) async-start(), calls=%async_computation.1 | async-start | bytes 5013504 | tf_op jit(solution)/shard_map/all_gather | solution.py:95
  8.1 2.4 copy-start.4
  9.6 0.5 copy-start.13
  9.8 0.5 copy-start.11
  18.8 1.0 copy-start.10
  20.1 16.9 %copy-start.5 = (s32[32,4,2]{1,0,2:T(8,128)S(1)}, s32[32,4,2]{1,0,2:T(8,128)}, u32[]{:S(2)}) copy-start(s32[32,4,2]{1,0,2:T(8,128)} %copy-done.4) | copy-start | bytes 3076
  20.1 17.0 %copy-start.17 = (f32[128]{0:T(128)S(1)}, f32[128]{0:T(128)}, u32[]{:S(2)}) copy-start(f32[128]{0:T(128)} %param.14) | copy-start | bytes 1540
  20.2 32.6 %collective-permute-start.2 = (bf16[384,288]{1,0:T(8,128)(2,1)S(1)}, bf16[384,288]{1,0:T(8,128)(2,1)S(1)}, u32[]{:S(2)}, u32[]{:S(2)}) collective-permute-start(bf16[384,288]{1,0:T(8,128)(2,1)S(1)} %get-tuple-element.34), channel_id=1, source_target_pairs={{0,48},{16,64},{32,80},{48,96},{64,112},{80,128},{96,144},{112,160... | collective-permute-start | bytes 663560 | tf_op jit(solution)/shard_map/ppermute | solution.py:21
  26.8 38.5 %collective-permute-start.1 = (bf16[384,288]{1,0:T(8,128)(2,1)S(1)}, bf16[384,288]{1,0:T(8,128)(2,1)S(1)}, u32[]{:S(2)}, u32[]{:S(2)}) collective-permute-start(bf16[384,288]{1,0:T(8,128)(2,1)S(1)} %get-tuple-element.35), channel_id=1, source_target_pairs={{0,32},{16,48},{32,64},{48,80},{64,96},{80,112},{96,128},{112,144}... | collective-permute-start | bytes 663560 | tf_op jit(solution)/shard_map/ppermute | solution.py:21
  33.2 38.2 %collective-permute-start = (bf16[384,288]{1,0:T(8,128)(2,1)S(1)}, bf16[384,288]{1,0:T(8,128)(2,1)S(1)}, u32[]{:S(2)}, u32[]{:S(2)}) collective-permute-start(bf16[384,288]{1,0:T(8,128)(2,1)S(1)} %get-tuple-element.36), channel_id=1, source_target_pairs={{0,16},{16,32},{32,48},{48,64},{64,80},{80,96},{96,112},{112,128},... | collective-permute-start | bytes 663560 | tf_op jit(solution)/shard_map/ppermute | solution.py:21
  39.2 32.2 %copy-start.18 = (s32[4]{0:T(128)}, s32[4]{0:T(128)S(1)}, u32[]{:S(2)}) copy-start(s32[4]{0:T(128)S(1)} %add.247) | copy-start | bytes 52
  39.4 0.6 copy-start.8
  71.7 2.0 copy-start.16
  74.7 195.0 %reduce-scatter.2.cloned.1.call-start = ((), (), s32[]{:S(2)}) async-start(), calls=%async_computation.2 | async-start | bytes 5013504 | tf_op jit(solution)/shard_map/reduce_scatter | solution.py:138
  145.5 6.5 %copy-start.20 = (bf16[512,4608]{0,1:T(8,128)(2,1)S(1)}, bf16[512,4608]{0,1:T(8,128)(2,1)}, u32[]{:S(2)}) copy-start(bf16[512,4608]{0,1:T(8,128)(2,1)} %all-gather.2.cloned.1.call-done) | copy-start | bytes 14155780
  149.8 3.6 %collective-permute-start.3 = (bf16[512,128]{0,1:T(8,128)(2,1)S(1)}, bf16[512,128]{0,1:T(8,128)(2,1)S(1)}, u32[]{:S(2)}, u32[]{:S(2)}) collective-permute-start(bf16[512,128]{0,1:T(8,128)(2,1)S(1)} %fusion.4), channel_id=1, source_target_pairs={{0,1},{1,0},{2,3},{3,2},{4,5},{5,4},{6,7},{7,6},{8,9},{9,8},{10,11... | collective-permute-start | bytes 393224 | tf_op jit(solution)/shard_map/ppermute | solution.py:27
  153.4 0.7 copy-start.15
  153.5 0.9 copy-start.21
  154.1 2.6 copy-start.2
  157.2 3.8 %collective-permute-start.4 = (bf16[512,128]{0,1:T(8,128)(2,1)S(1)}, bf16[512,128]{0,1:T(8,128)(2,1)S(1)}, u32[]{:S(2)}, u32[]{:S(2)}) collective-permute-start(bf16[512,128]{0,1:T(8,128)(2,1)S(1)} %get-tuple-element.57), channel_id=1, source_target_pairs={{0,1},{1,0},{2,3},{3,2},{4,5},{5,4},{6,7},{7,6},{8,9},{9,8},{10,11... | collective-permute-start | bytes 393224 | tf_op jit(solution)/shard_map/ppermute | solution.py:27
  159.6 1.4 copy-start.1
  164.6 0.7 copy-start.9
  164.6 0.8 copy-start.12
  164.6 0.9 copy-start.14
  164.6 2.3 copy-start.19
  276.3 16.5 %copy-start.3 = (f32[512,512]{0,1:T(8,128)S(1)}, f32[512,512]{0,1:T(8,128)}, u32[]{:S(2)}) copy-start(f32[512,512]{0,1:T(8,128)} %copy-done.2) | copy-start | bytes 3145732
  276.4 30.0 %collective-permute-start.7 = (bf16[384,288]{1,0:T(8,128)(2,1)S(1)}, bf16[384,288]{1,0:T(8,128)(2,1)S(1)}, u32[]{:S(2)}, u32[]{:S(2)}) collective-permute-start(bf16[384,288]{1,0:T(8,128)(2,1)S(1)} %get-tuple-element.30), channel_id=1, source_target_pairs={{0,464},{16,480},{32,496},{48,0},{64,16},{80,32},{96,48},{112,64},... | collective-permute-start | bytes 663560 | tf_op jit(solution)/shard_map/ppermute | solution.py:21
  284.2 30.6 %collective-permute-start.6 = (bf16[384,288]{1,0:T(8,128)(2,1)S(1)}, bf16[384,288]{1,0:T(8,128)(2,1)S(1)}, u32[]{:S(2)}, u32[]{:S(2)}) collective-permute-start(bf16[384,288]{1,0:T(8,128)(2,1)S(1)} %get-tuple-element.31), channel_id=1, source_target_pairs={{0,480},{16,496},{32,0},{48,16},{64,32},{80,48},{96,64},{112,80},{... | collective-permute-start | bytes 663560 | tf_op jit(solution)/shard_map/ppermute | solution.py:21
  289.4 30.6 %collective-permute-start.5 = (bf16[384,288]{1,0:T(8,128)(2,1)S(1)}, bf16[384,288]{1,0:T(8,128)(2,1)S(1)}, u32[]{:S(2)}, u32[]{:S(2)}) collective-permute-start(bf16[384,288]{1,0:T(8,128)(2,1)S(1)} %get-tuple-element.32), channel_id=1, source_target_pairs={{0,496},{16,0},{32,16},{48,32},{64,48},{80,64},{96,80},{112,96},{1... | collective-permute-start | bytes 663560 | tf_op jit(solution)/shard_map/ppermute | solution.py:21
  320.3 4.7 %copy-start.6 = (pred[1536]{0:T(1024)(128)(4,1)S(1)}, pred[1536]{0:T(1024)(128)(4,1)}, u32[]{:S(2)}) copy-start(pred[1536]{0:T(1024)(128)(4,1)} %get-tuple-element.19) | copy-start | bytes 4612
  320.3 4.7 %copy-start.7 = (pred[1536]{0:T(1024)(128)(4,1)S(1)}, pred[1536]{0:T(1024)(128)(4,1)}, u32[]{:S(2)}) copy-start(pred[1536]{0:T(1024)(128)(4,1)} %get-tuple-element.59) | copy-start | bytes 4612
Sparse Core Ops, SparseCore 0:
  74.8 70.6 all-gather.1
  164.7 104.9 reduce-scatter.1
where the time goes:
time: 337 us; the launch traced here: 334 us
  waiting for transfers between devices  230 us (68%)
  starting transfers between devices  37.7 us (11%)
  local copies, waits for them, and re-layouts  26.8 us (8%)
  between operations  14.7 us (4%)
  matrix products  13 us (4%)
  other arithmetic  12.6 us (4%)
    reduce_scatter x1, waiting for transfers between devices, body(): lax.psum_scatter(partial_sum.astype(jnp.bfloat16), 'mp', scatter_dimensio...  103 us
    all_gather x1, waiting for transfers between devices, body(): piece = lax.all_gather(moved_rows, 'mp', axis=1, tiled=True)  70.7 us
    ppermute x6, waiting for transfers between devices, shifted(): return lax.ppermute(value, axis, pairs)  56.2 us
    ppermute x6, starting transfers between devices, shifted(): return lax.ppermute(value, axis, pairs)  33.1 us
  transfers between devices with their start and end apart: 10, of which 8 were waited for; matrix products, arithmetic and copies ran while one was open for 3% of the time, Pallas kernels for 0%

commit v1 on v0

v1 whole, which is shorter than its diff:
```python
import functools

import jax
import jax.numpy as jnp
import numpy as np
from jax import lax
from jax.experimental import pallas as pl
from jax.experimental.pallas import tpu as pltpu
from jax.sharding import PartitionSpec as P

SPREAD = 4
RECV = 512
CAP = 384
HOME = 1536
TAIL = RECV - CAP
HEAD = 128
HALF = 64
WINDOW = 512

BETA = 0.1
SOFT_CAP = 50.0
ROPE_BASE = 10000.0
QUERY_SCALE = 1.0 / 12.0

F32 = jnp.float32
BF16 = jnp.bfloat16

VMEM = pl.BlockSpec(memory_space=pltpu.VMEM)
SMEM = pl.BlockSpec(memory_space=pltpu.SMEM)
NN = (((1,), (0,)), ((), ()))
NT = (((1,), (1,)), ((), ()))
TN = (((0,), (0,)), ((), ()))


def dot(a, b, dims):
    return lax.dot_general(a, b, dims, preferred_element_type=F32)


def call(kernel, outs, in_specs, args, flops, scratch=(), limit=24):
    moved = sum(int(np.prod(o.shape)) * o.dtype.itemsize for o in outs)
    moved += sum(int(np.prod(a.shape)) * a.dtype.itemsize for a in args)
    return pl.pallas_call(
        kernel,
        out_shape=outs,
        in_specs=in_specs,
        out_specs=[VMEM] * len(outs),
        scratch_shapes=list(scratch),
        compiler_params=pltpu.CompilerParams(vmem_limit_bytes=limit << 20),
        cost_estimate=pl.CostEstimate(flops=flops, bytes_accessed=moved, transcendentals=0),
    )(*args)


def sds(shape, dtype):
    return jax.ShapeDtypeStruct(shape, dtype)


def pair_at(tokens, target, home, replica):
    start, running = jnp.int32(0), jnp.int32(0)
    chosen, rejected, index = jnp.int32(0), jnp.int32(0), jnp.int32(0)
    for p in range(SPREAD):
        i = home * SPREAD + p
        hit = target[i] == replica
        c, r = tokens[i, 0], tokens[i, 1]
        start = jnp.where(hit, running, start)
        chosen = jnp.where(hit, c, chosen)
        rejected = jnp.where(hit, r, rejected)
        index = jnp.where(hit, i, index)
        running = running + c + r
    return start, chosen, rejected, index


def around(index, count):
    return lax.rem(index + count, count)


def outgoing(tokens, target, replicas, replica, offset):
    there = around(replica + offset, replicas)
    start, chosen, rejected, _ = pair_at(tokens, target, replica, there)
    place = jnp.int32(0)
    for nearer in range(offset):
        _, c, r, _ = pair_at(tokens, target, around(there - nearer, replicas), there)
        place = place + c + r
    return start, chosen + rejected, place


def window_of(start):
    first = jnp.minimum((start // 16) * 16, HOME - WINDOW)
    return pl.multiple_of(first, 16)


def pack_kernel(replicas, offsets, tokens, target, home, *outs):
    replica = lax.axis_index("dp")
    for offset, out in zip(offsets, outs):
        start, size, place = outgoing(tokens, target, replicas, replica, offset)
        first = window_of(start)
        skip = RECV - out.shape[1]
        column = lax.broadcasted_iota(jnp.int32, (1, out.shape[1]), 1) + skip
        live = (column >= place) & (column < place + size)
        source = jnp.where(live, column - place + start - first, -1)
        row = lax.broadcasted_iota(jnp.int32, (WINDOW, out.shape[1]), 0)
        pick = (row == source).astype(F32).astype(BF16)
        rows = home[pl.ds(first, WINDOW), :]
        out[...] = dot(rows, pick, TN).astype(BF16)


def weights_kernel(q, kv, own, away):
    core = lax.rem(lax.axis_index("mp"), 2)
    for block in range(q.shape[0]):
        own[block, :, :HEAD] = q[block, core]
        own[block, :, HEAD:] = kv[block, core]
        away[block, :, :HEAD] = q[block, 1 - core]
        away[block, :, HEAD:] = kv[block, 1 - core]


def tables_kernel(replicas, tokens, target, margins, frequency, grad, cosine, sine, begin, upstream):
    replica = lax.axis_index("dp")
    row = lax.broadcasted_iota(jnp.int32, (1, RECV), 1)
    first = jnp.zeros((1, RECV), jnp.int32)
    margin = jnp.zeros((1, RECV), F32)
    sign = jnp.zeros((1, RECV), F32)
    place = jnp.int32(0)
    for offset in range(SPREAD):
        home = around(replica - offset, replicas)
        _, chosen, rejected, index = pair_at(tokens, target, home, replica)
        first = jnp.where(row >= place, place, first)
        margin = jnp.where(row >= place, margins[index], margin)
        sign = jnp.where(row >= place, -1.0, sign)
        first = jnp.where(row >= place + chosen, place + chosen, first)
        sign = jnp.where(row >= place + chosen, 1.0, sign)
        place = place + chosen + rejected
    begin[...] = jnp.broadcast_to(first, begin.shape)
    coef = BETA * sign / (1.0 + jnp.exp(BETA * margin))
    upstream[...] = (grad[...].astype(F32).T * coef).astype(BF16)
    angle = (row - first).astype(F32) * frequency[:, :1]
    cosine[...] = jnp.cos(angle)
    sine[...] = jnp.sin(angle)


def block_index(relative):
    place = lax.axis_index("mp")
    x, y = place // 4, lax.rem(place // 2, 2)
    near, far = x + 1 - 2 * lax.rem(x, 2), 3 - x
    across = far + 1 - 2 * lax.rem(far, 2)
    return (x, near, far, across)[relative % 4] * 2 + (y if relative < 4 else 1 - y)


def project_kernel(own, away, *refs):
    pieces, (keep, send) = refs[:-2], refs[-2:]
    mine = jnp.zeros((2 * HEAD, RECV), F32)
    other = jnp.zeros((2 * HEAD, RECV), F32)
    for relative, piece in enumerate(pieces):
        block = block_index(relative)
        mine = mine + dot(own[block], piece[...], TN)
        other = other + dot(away[block], piece[...], TN)
    keep[: 2 * HEAD] = mine
    keep[2 * HEAD :] = other[HEAD:]
    send[: 2 * HEAD] = other
    send[2 * HEAD :] = mine[HEAD:]


def turn(value, cosine, sine):
    low, high = value[:HALF], value[HALF:]
    return jnp.concatenate([low * cosine - high * sine, high * cosine + low * sine], axis=0)


def attention_kernel(kept, got, cosine, sine, begin, upstream, attended, send, held):
    first_core = lax.rem(lax.axis_index("mp"), 2) == 0
    cos, sin = cosine[...], sine[...]
    total = kept[...] + got[...]
    own, other = total[HEAD : 2 * HEAD], total[2 * HEAD :]
    query = (QUERY_SCALE * turn(total[:HEAD], cos, sin)).astype(BF16)
    key = turn(jnp.where(first_core, own, other), cos, sin).astype(BF16)
    value = jnp.where(first_core, other, own).astype(BF16)
    scores = dot(key, query, TN)
    bent = jnp.tanh(scores / SOFT_CAP)
    key_row = lax.broadcasted_iota(jnp.int32, (RECV, RECV), 0)
    query_row = lax.broadcasted_iota(jnp.int32, (RECV, RECV), 1)
    allowed = (key_row <= query_row) & (key_row >= begin[:1, :])
    exponent = jnp.where(allowed, jnp.exp(SOFT_CAP * bent), 0.0)
    weights = exponent * (1.0 / jnp.sum(exponent, axis=0, keepdims=True))
    probs = weights.astype(BF16)
    attended[...] = dot(value, probs, NN).T.astype(BF16)
    up = upstream[...]
    dprobs = dot(value, up, TN)
    delta = jnp.sum(weights * dprobs, axis=0, keepdims=True)
    dscores = (weights * (dprobs - delta) * (1.0 - bent * bent)).astype(BF16)
    dquery = QUERY_SCALE * turn(dot(key, dscores, NN), cos, -sin)
    dkey = turn(dot(query, dscores, NT), cos, -sin)
    dvalue = dot(up, probs, NT)
    down, dother = jnp.where(first_core, dkey, dvalue), jnp.where(first_core, dvalue, dkey)
    send[:HEAD] = dquery.astype(BF16)
    send[HEAD : 2 * HEAD] = down.astype(BF16)
    send[2 * HEAD :] = dother.astype(BF16)
    held[:HEAD] = down
    held[HEAD:] = dother


def spread_kernel(own, away, sent, held, got, *outs):
    down = (held[:HEAD] + got[2 * HEAD :].astype(F32)).astype(BF16)
    dother = (held[HEAD:] + got[HEAD : 2 * HEAD].astype(F32)).astype(BF16)
    mine = jnp.concatenate([sent[:HEAD], down], axis=0)
    other = jnp.concatenate([got[:HEAD], dother], axis=0)
    for relative, out in enumerate(outs):
        block = block_index(relative)
        out[...] = (dot(own[block], mine, NN) + dot(away[block], other, NN)).astype(BF16)


def unpack_kernel(replicas, tokens, target, *refs):
    pieces, (home, total) = refs[:-2], refs[-2:]
    replica = lax.axis_index("dp")
    total[...] = jnp.zeros_like(total)
    for offset, piece in enumerate(pieces):
        start, size, place = outgoing(tokens, target, replicas, replica, offset)
        first = window_of(start)
        skip = RECV - piece.shape[1]
        row = lax.broadcasted_iota(jnp.int32, (WINDOW, piece.shape[1]), 0)
        column = lax.broadcasted_iota(jnp.int32, (1, piece.shape[1]), 1) + skip
        live = (column >= place) & (column < place + size)
        source = jnp.where(live, column - place + start - first, -1)
        pick = (row == source).astype(F32).astype(BF16)
        total[pl.ds(first, WINDOW), :] += dot(pick, piece[...], NT)
    home[...] = total[...].astype(BF16)


def along(value, steps):
    count = lax.axis_size("dp")
    return lax.ppermute(value, "dp", [(s, (s + steps) % count) for s in range(count)])


def swap(value, change):
    count = lax.axis_size("mp")
    pairs = []
    for source in range(count):
        x, y, core = source // 4, source // 2 % 2, source % 2
        x, y, core = change(x, y, core)
        pairs.append((source, x * 4 + y * 2 + core))
    return lax.ppermute(value, "mp", pairs)


def to_core(value):
    return swap(value, lambda x, y, core: (x, y, 1 - core))


def to_y(value):
    return swap(value, lambda x, y, core: (x, 1 - y, core))


def to_near(value):
    return swap(value, lambda x, y, core: (x ^ 1, y, core))


def to_far(value):
    return swap(value, lambda x, y, core: (3 - x, y, core))


def body(tokens_home, q_weight, kv_weight, pair_tokens, pair_target, margins, grad_attended):
    replicas = lax.axis_size("dp")
    blocks = lax.axis_size("mp") // 2
    width = tokens_home.shape[1]
    table = (pair_tokens, pair_target)

    def pack(offsets):
        outs = [sds((width, CAP if o == SPREAD - 1 else RECV), BF16) for o in offsets]
        return call(
            functools.partial(pack_kernel, replicas, offsets),
            outs,
            [SMEM, SMEM, VMEM],
            (*table, tokens_home),
            2 * len(offsets) * width * WINDOW * RECV,
        )

    (third,) = pack((3,))
    bucket = along(third, 1)
    second, first, zeroth = pack((2, 1, 0))
    own_w, away_w = call(
        weights_kernel,
        [sds((blocks, width, 2 * HEAD), BF16)] * 2,
        [VMEM, VMEM],
        (q_weight.reshape(blocks, 2, width, HEAD), kv_weight.reshape(blocks, 2, width, HEAD)),
        1000,
    )
    other_w = to_core(away_w)
    frequency = np.exp(-np.log(ROPE_BASE) * np.arange(HALF) / HALF).astype(np.float32)
    frequency = jnp.asarray(np.broadcast_to(frequency[:, None], (HALF, HEAD)))
    cosine, sine, begin, upstream = call(
        functools.partial(tables_kernel, replicas),
        [sds((HALF, RECV), F32), sds((HALF, RECV), F32), sds((8, RECV), jnp.int32), sds((HEAD, RECV), BF16)],
        [SMEM, SMEM, SMEM, VMEM, VMEM],
        (*table, margins, frequency, grad_attended),
        1000,
    )
    bucket = jnp.pad(bucket, ((0, 0), (TAIL, 0))) + second
    bucket = along(bucket, 1) + first
    moved = along(bucket, 1) + zeroth

    other_y = to_y(moved)
    near = to_near(moved)
    far = to_far(moved)
    across = to_far(near)
    far_y = to_far(other_y)
    near_y = to_near(other_y)
    across_y = to_near(far_y)
    pieces = (moved, near, far, across, other_y, near_y, far_y, across_y)
    keep, send = call(
        project_kernel,
        [sds((3 * HEAD, RECV), F32)] * 2,
        [VMEM] * 10,
        (own_w, other_w, *pieces),
        2 * blocks * width * 4 * HEAD * RECV,
    )
    got = to_core(send)
    attended, send, held = call(
        attention_kernel,
        [sds((RECV, HEAD), BF16), sds((3 * HEAD, RECV), BF16), sds((2 * HEAD, RECV), F32)],
        [VMEM] * 6,
        (keep, got, cosine, sine, begin, upstream),
        14 * HEAD * RECV * RECV,
    )
    got = to_core(send)
    parts = call(
        spread_kernel,
        [sds((width, RECV), BF16)] * 8,
        [VMEM] * 5,
        (own_w, other_w, send, held, got),
        2 * blocks * width * 4 * HEAD * RECV,
    )
    mine, near, far, across, mine_y, near_y, far_y, across_y = parts

    def plus(*terms):
        return sum(t.astype(F32) for t in terms).astype(BF16)

    forward_y = plus(far_y, to_near(across_y))
    forward = plus(near, to_far(across))
    here_y = plus(mine_y, to_near(near_y), to_far(forward_y))
    here = plus(mine, to_far(far), to_near(forward), to_y(here_y))

    back1 = along(here, -1)
    back2 = along(back1, -1)
    back3 = along(back2[:, TAIL:], -1)
    (grad_home,) = call(
        functools.partial(unpack_kernel, replicas),
        [sds((HOME, width), BF16)],
        [SMEM, SMEM] + [VMEM] * 4,
        (*table, here, back1, back2, back3),
        2 * SPREAD * width * WINDOW * RECV,
        scratch=[pltpu.VMEM((HOME, width), F32)],
    )
    return (attended, grad_home)


def solution(mesh):
    return jax.shard_map(
        body,
        mesh=mesh,
        in_specs=(P("dp", "mp"), P(None, "mp"), P(None, "mp"), P(), P(), P(), P("dp", "mp")),
        out_specs=(P("dp", "mp"), P("dp", "mp")),
        check_vma=False,
    )
```

time: 337 us -> 163 us (0.48)
  waiting for transfers between devices: 230 us -> 65.9 us
  starting transfers between devices: 37.7 us -> 72 us
  local copies, waits for them, and re-layouts: 26.8 us -> 3.9 us
  Pallas kernels: 0 us -> 16.2 us
  between operations: 14.7 us -> 1.02 us
  matrix products: 13 us -> 0 us
  other arithmetic: 12.6 us -> 0.64 us
    reduce_scatter x1 -> x0, waiting for transfers between devices: 103 us -> none  [body(): lax.psum_scatter(partial_sum.astype(jnp.bfloat16), 'mp', scatter_dimensio...]
    all_gather x1 -> x0, waiting for transfers between devices: 70.7 us -> none  [body(): piece = lax.all_gather(moved_rows, 'mp', axis=1, tiled=True)]
    ppermute x8 -> x23, starting transfers between devices: 37.6 us -> 72 us  [the longest x17 50.8 us: swap(): return lax.ppermute(value, 'mp', pairs)]
    gather x7 -> x0, local copies, waits for them, and re-layouts: 17.9 us -> none  [the longest x1 4.84 us: body(): jnp.take(tokens_home, home_index.reshape(-1), axis=0)]
    pallas_call x0 -> x8, Pallas kernels: none -> 16.2 us  [call(): pl.pallas_call(kernel, out_shape=outs, in_specs=in_specs, out_specs=[VMEM...]
    dot_general x10 -> x0, matrix products: 13 us -> none  [the longest x1 3.71 us: body(): proj_kv = jnp.dot(piece, kv_weight, preferred_element_type=jnp.float32)]
    ppermute x8 -> x23, waiting for transfers between devices: 56.2 us -> 65.9 us  [the longest x6 43.9 us: along(): lax.ppermute(value, 'dp', [(s, (s + steps) % count) for s in range(count)])]
  transfers between devices with their start and end apart: 10 -> 23, of which waited for: 8 -> 15; matrix products, arithmetic and copies ran while one was open for 3% -> 0% of each run, Pallas kernels for 0% -> 3%
where the time goes in v1:
time: 163 us; the launch traced here: 160 us
  starting transfers between devices  72 us (44%)
  waiting for transfers between devices  65.9 us (40%)
  Pallas kernels  16.2 us (10%)
  local copies, waits for them, and re-layouts  3.9 us (2%)
    ppermute x17, starting transfers between devices, swap(): return lax.ppermute(value, 'mp', pairs)  50.8 us
    ppermute x6, waiting for transfers between devices, along(): lax.ppermute(value, 'dp', [(s, (s + steps) % count) for s in range(count)])  43.9 us
    ppermute x17, waiting for transfers between devices, swap(): return lax.ppermute(value, 'mp', pairs)  22 us
    ppermute x6, starting transfers between devices, along(): lax.ppermute(value, 'dp', [(s, (s + steps) % count) for s in range(count)])  21.2 us
    pallas_call x8, Pallas kernels, call(): pl.pallas_call(kernel, out_shape=outs, in_specs=in_specs, out_specs=[VMEM...  16.2 us
    unnamed x15, local copies, waits for them, and re-layouts  3.8 us
  transfers between devices with their start and end apart: 23, of which 15 were waited for; matrix products, arithmetic and copies ran while one was open for 0% of the time, Pallas kernels for 3%

profile of v1, /device:TPU:6, one launch (start us, length us, event | category | flops | bytes accessed | tf_op | source)
XLA Modules:
  0.0 159.7 jit_solution(3717558005318669681)
XLA Ops:
  5.1 3.8 %collective-permute-start.1 = (bf16[288,384]{1,0:T(8,128)(2,1)S(1)}, bf16[288,384]{1,0:T(8,128)(2,1)S(1)}, u32[]{:S(2)}, u32[]{:S(2)}) collective-permute-start(bf16[288,384]{1,0:T(8,128)(2,1)S(1)} %shard_map.96), channel_id=1, source_target_pairs={{0,16},{16,32},{32,48},{48,64},{64,80},{80,96},{96,112},{112,128},... | collective-permute-start | bytes 663560 | tf_op jit(solution)/shard_map/ppermute | solution.py:227
  9.0 2.3 %shard_map.97 = (bf16[288,512]{1,0:T(8,128)(2,1)S(1)}, bf16[288,512]{1,0:T(8,128)(2,1)S(1)}, bf16[288,512]{1,0:T(8,128)(2,1)S(1)}) custom-call(s32[128,2]{1,0:T(8,128)S(1)} %copy.10.tokens, s32[128]{0:T(128)S(1)} %copy-done.3, bf16[1536,288]{1,0:T(8,128)(2,1)S(1)} %copy.11.home), custom_call_target="tpu_custom_call" | custom-call | flops 452984832 | bytes 1771008 | tf_op jit(solution)/shard_map/pallas_call | solution.py:42
  11.3 11.7 %collective-permute-done.1 = bf16[288,384]{1,0:T(8,128)(2,1)S(1)} collective-permute-done((bf16[288,384]{1,0:T(8,128)(2,1)S(1)}, bf16[288,384]{1,0:T(8,128)(2,1)S(1)}, u32[]{:S(2)}, u32[]{:S(2)}) %collective-permute-start.1) | collective-permute-done | bytes 221216 | tf_op jit(solution)/shard_map/ppermute | solution.py:227
  24.9 10.3 %collective-permute-done.2 = bf16[288,512]{1,0:T(8,128)(2,1)S(1)} collective-permute-done((bf16[288,512]{1,0:T(8,128)(2,1)S(1)}, bf16[288,512]{1,0:T(8,128)(2,1)S(1)}, u32[]{:S(2)}, u32[]{:S(2)}) %collective-permute-start.2) | collective-permute-done | bytes 294944 | tf_op jit(solution)/shard_map/ppermute | solution.py:227
  39.6 7.0 %collective-permute-done.3 = bf16[288,512]{1,0:T(8,128)(2,1)S(1)} collective-permute-done((bf16[288,512]{1,0:T(8,128)(2,1)S(1)}, bf16[288,512]{1,0:T(8,128)(2,1)S(1)}, u32[]{:S(2)}, u32[]{:S(2)}) %collective-permute-start.3) | collective-permute-done | bytes 294944 | tf_op jit(solution)/shard_map/ppermute | solution.py:227
  46.7 4.8 %collective-permute-start.7 = (bf16[288,512]{1,0:T(8,128)(2,1)S(1)}, bf16[288,512]{1,0:T(8,128)(2,1)S(1)}, u32[]{:S(2)}, u32[]{:S(2)}) collective-permute-start(bf16[288,512]{1,0:T(8,128)(2,1)S(1)} %add.34.refs_0_), channel_id=1, source_target_pairs={{0,2},{1,3},{2,0},{3,1},{4,6},{5,7},{6,4},{7,5},{8,10},{9,11},{10,... | collective-permute-start | bytes 884744 | tf_op jit(solution)/shard_map/ppermute | solution.py:237
  51.5 2.7 %collective-permute-start.4 = (bf16[288,512]{1,0:T(8,128)(2,1)S(1)}, bf16[288,512]{1,0:T(8,128)(2,1)S(1)}, u32[]{:S(2)}, u32[]{:S(2)}) collective-permute-start(bf16[288,512]{1,0:T(8,128)(2,1)S(1)} %add.34.refs_0_), channel_id=1, source_target_pairs={{0,4},{1,5},{2,6},{3,7},{4,0},{5,1},{6,2},{7,3},{8,12},{9,13},{10,... | collective-permute-start | bytes 884744 | tf_op jit(solution)/shard_map/ppermute | solution.py:237
  54.2 2.6 %collective-permute-done.7.refs_4_ = bf16[288,512]{1,0:T(8,128)(2,1)S(1)} collective-permute-done((bf16[288,512]{1,0:T(8,128)(2,1)S(1)}, bf16[288,512]{1,0:T(8,128)(2,1)S(1)}, u32[]{:S(2)}, u32[]{:S(2)}) %collective-permute-start.7) | collective-permute-done | bytes 294944 | tf_op jit(solution)/shard_map/ppermute | solution.py:237
  56.8 2.4 %collective-permute-start.9 = (bf16[288,512]{1,0:T(8,128)(2,1)S(1)}, bf16[288,512]{1,0:T(8,128)(2,1)S(1)}, u32[]{:S(2)}, u32[]{:S(2)}) collective-permute-start(bf16[288,512]{1,0:T(8,128)(2,1)S(1)} %collective-permute-done.7.refs_4_), channel_id=1, source_target_pairs={{0,12},{1,13},{2,14},{3,15},{4,8},{5,9},{6,10},{7,11},{8,4},{9,5},... | collective-permute-start | bytes 884744 | tf_op jit(solution)/shard_map/ppermute | solution.py:237
  59.2 4.7 %collective-permute-start.5 = (bf16[288,512]{1,0:T(8,128)(2,1)S(1)}, bf16[288,512]{1,0:T(8,128)(2,1)S(1)}, u32[]{:S(2)}, u32[]{:S(2)}) collective-permute-start(bf16[288,512]{1,0:T(8,128)(2,1)S(1)} %add.34.refs_0_), channel_id=1, source_target_pairs={{0,12},{1,13},{2,14},{3,15},{4,8},{5,9},{6,10},{7,11},{8,4},{9,5},... | collective-permute-start | bytes 884744 | tf_op jit(solution)/shard_map/ppermute | solution.py:237
  65.8 2.6 %collective-permute-start.6 = (bf16[288,512]{1,0:T(8,128)(2,1)S(1)}, bf16[288,512]{1,0:T(8,128)(2,1)S(1)}, u32[]{:S(2)}, u32[]{:S(2)}) collective-permute-start(bf16[288,512]{1,0:T(8,128)(2,1)S(1)} %collective-permute-done.4.refs_1_), channel_id=1, source_target_pairs={{0,12},{1,13},{2,14},{3,15},{4,8},{5,9},{6,10},{7,11},{8,4},{9,5},... | collective-permute-start | bytes 884744 | tf_op jit(solution)/shard_map/ppermute | solution.py:237
  69.2 2.4 %collective-permute-start.10 = (bf16[288,512]{1,0:T(8,128)(2,1)S(1)}, bf16[288,512]{1,0:T(8,128)(2,1)S(1)}, u32[]{:S(2)}, u32[]{:S(2)}) collective-permute-start(bf16[288,512]{1,0:T(8,128)(2,1)S(1)} %collective-permute-done.9.refs_6_), channel_id=1, source_target_pairs={{0,4},{1,5},{2,6},{3,7},{4,0},{5,1},{6,2},{7,3},{8,12},{9,13},{10,... | collective-permute-start | bytes 884744 | tf_op jit(solution)/shard_map/ppermute | solution.py:237
  71.6 2.9 %collective-permute-done.5.refs_2_ = bf16[288,512]{1,0:T(8,128)(2,1)S(1)} collective-permute-done((bf16[288,512]{1,0:T(8,128)(2,1)S(1)}, bf16[288,512]{1,0:T(8,128)(2,1)S(1)}, u32[]{:S(2)}, u32[]{:S(2)}) %collective-permute-start.5) | collective-permute-done | bytes 294944 | tf_op jit(solution)/shard_map/ppermute | solution.py:237
  74.6 3.2 %collective-permute-done.6.refs_3_ = bf16[288,512]{1,0:T(8,128)(2,1)S(1)} collective-permute-done((bf16[288,512]{1,0:T(8,128)(2,1)S(1)}, bf16[288,512]{1,0:T(8,128)(2,1)S(1)}, u32[]{:S(2)}, u32[]{:S(2)}) %collective-permute-start.6) | collective-permute-done | bytes 294944 | tf_op jit(solution)/shard_map/ppermute | solution.py:237
  77.8 2.4 %shard_map.98 = (f32[384,512]{1,0:T(8,128)S(1)}, f32[384,512]{1,0:T(8,128)S(1)}) custom-call(bf16[8,288,256]{2,1,0:T(8,128)(2,1)S(1)} %get-tuple-element.24.own, bf16[8,288,256]{2,1,0:T(8,128)(2,1)S(1)} %collective-permute-done.away, bf16[288,512]{1,0:T(8,128)(2,1)S(1)} %add.34.refs_0_, bf16[288,512]{1,0:T(8,128)(2,1)S(1)} %collective-permute-done.4.refs_1_, ...), custom_call_target="tpu_custom_call" | custom-call | flops 1207959552 | bytes 6291456 | tf_op jit(solution)/shard_map/pallas_call | solution.py:42
  84.4 2.3 %shard_map.100 = (bf16[512,128]{1,0:T(8,128)(2,1)}, bf16[384,512]{1,0:T(8,128)(2,1)S(1)}, f32[256,512]{1,0:T(8,128)S(1)}) custom-call(f32[384,512]{1,0:T(8,128)S(1)} %get-tuple-element.29.kept, f32[384,512]{1,0:T(8,128)S(1)} %collective-permute-done.11.got, f32[64,512]{1,0:T(8,128)S(1)} %get-tuple-element.31.cosine, f32[64,512]{1,0:T(8,128)S(1)} %get-tuple-element.32.sine, ...), custom_call_target="tpu_custom_call" | custom-call | flops 469762048 | bytes 3031040 | tf_op jit(solution)/shard_map/pallas_call | solution.py:42
  86.7 2.4 %collective-permute-start.12 = (bf16[384,512]{1,0:T(8,128)(2,1)S(1)}, bf16[384,512]{1,0:T(8,128)(2,1)S(1)}, u32[]{:S(2)}, u32[]{:S(2)}) collective-permute-start(bf16[384,512]{1,0:T(8,128)(2,1)S(1)} %get-tuple-element.36.sent), channel_id=1, source_target_pairs={{0,1},{1,0},{2,3},{3,2},{4,5},{5,4},{6,7},{7,6},{8,9},{9,8},{10,11... | collective-permute-start | bytes 1179656 | tf_op jit(solution)/shard_map/ppermute | solution.py:237
  91.8 2.9 %collective-permute-start.17 = (bf16[288,512]{1,0:T(8,128)(2,1)S(1)}, bf16[288,512]{1,0:T(8,128)(2,1)S(1)}, u32[]{:S(2)}, u32[]{:S(2)}) collective-permute-start(bf16[288,512]{1,0:T(8,128)(2,1)S(1)} %get-tuple-element.45), channel_id=1, source_target_pairs={{0,4},{1,5},{2,6},{3,7},{4,0},{5,1},{6,2},{7,3},{8,12},{9,13},{10,... | collective-permute-start | bytes 884744 | tf_op jit(solution)/shard_map/ppermute | solution.py:237
  94.7 4.1 %collective-permute-start.14 = (bf16[288,512]{1,0:T(8,128)(2,1)S(1)}, bf16[288,512]{1,0:T(8,128)(2,1)S(1)}, u32[]{:S(2)}, u32[]{:S(2)}) collective-permute-start(bf16[288,512]{1,0:T(8,128)(2,1)S(1)} %get-tuple-element.41), channel_id=1, source_target_pairs={{0,12},{1,13},{2,14},{3,15},{4,8},{5,9},{6,10},{7,11},{8,4},{9,5},... | collective-permute-start | bytes 884744 | tf_op jit(solution)/shard_map/ppermute | solution.py:237
  100.8 2.2 %collective-permute-done.17 = bf16[288,512]{1,0:T(8,128)(2,1)S(1)} collective-permute-done((bf16[288,512]{1,0:T(8,128)(2,1)S(1)}, bf16[288,512]{1,0:T(8,128)(2,1)S(1)}, u32[]{:S(2)}, u32[]{:S(2)}) %collective-permute-start.17) | collective-permute-done | bytes 294944 | tf_op jit(solution)/shard_map/ppermute | solution.py:237
  103.1 4.2 %collective-permute-start.18 = (bf16[288,512]{1,0:T(8,128)(2,1)S(1)}, bf16[288,512]{1,0:T(8,128)(2,1)S(1)}, u32[]{:S(2)}, u32[]{:S(2)}) collective-permute-start(bf16[288,512]{1,0:T(8,128)(2,1)S(1)} %add_convert_fusion.2), channel_id=1, source_target_pairs={{0,12},{1,13},{2,14},{3,15},{4,8},{5,9},{6,10},{7,11},{8,4},{9,5},... | collective-permute-start | bytes 884744 | tf_op jit(solution)/shard_map/ppermute | solution.py:237
  107.3 2.8 %collective-permute-start.13 = (bf16[288,512]{1,0:T(8,128)(2,1)S(1)}, bf16[288,512]{1,0:T(8,128)(2,1)S(1)}, u32[]{:S(2)}, u32[]{:S(2)}) collective-permute-start(bf16[288,512]{1,0:T(8,128)(2,1)S(1)} %get-tuple-element.39), channel_id=1, source_target_pairs={{0,12},{1,13},{2,14},{3,15},{4,8},{5,9},{6,10},{7,11},{8,4},{9,5},... | collective-permute-start | bytes 884744 | tf_op jit(solution)/shard_map/ppermute | solution.py:237
  112.5 3.6 %collective-permute-done.18 = bf16[288,512]{1,0:T(8,128)(2,1)S(1)} collective-permute-done((bf16[288,512]{1,0:T(8,128)(2,1)S(1)}, bf16[288,512]{1,0:T(8,128)(2,1)S(1)}, u32[]{:S(2)}, u32[]{:S(2)}) %collective-permute-start.18) | collective-permute-done | bytes 294944 | tf_op jit(solution)/shard_map/ppermute | solution.py:237
  116.2 4.8 %collective-permute-start.19 = (bf16[288,512]{1,0:T(8,128)(2,1)S(1)}, bf16[288,512]{1,0:T(8,128)(2,1)S(1)}, u32[]{:S(2)}, u32[]{:S(2)}) collective-permute-start(bf16[288,512]{1,0:T(8,128)(2,1)S(1)} %add_convert_fusion.1), channel_id=1, source_target_pairs={{0,2},{1,3},{2,0},{3,1},{4,6},{5,7},{6,4},{7,5},{8,10},{9,11},{10,... | collective-permute-start | bytes 884744 | tf_op jit(solution)/shard_map/ppermute | solution.py:237
  121.1 5.3 %collective-permute-done.19 = bf16[288,512]{1,0:T(8,128)(2,1)S(1)} collective-permute-done((bf16[288,512]{1,0:T(8,128)(2,1)S(1)}, bf16[288,512]{1,0:T(8,128)(2,1)S(1)}, u32[]{:S(2)}, u32[]{:S(2)}) %collective-permute-start.19) | collective-permute-done | bytes 294944 | tf_op jit(solution)/shard_map/ppermute | solution.py:237
  126.5 3.1 %collective-permute-start.20 = (bf16[288,512]{1,0:T(8,128)(2,1)S(1)}, bf16[288,512]{1,0:T(8,128)(2,1)S(1)}, u32[]{:S(2)}, u32[]{:S(2)}) collective-permute-start(bf16[288,512]{1,0:T(8,128)(2,1)S(1)} %add_convert_fusion.refs_0_), channel_id=1, source_target_pairs={{0,496},{16,0},{32,16},{48,32},{64,48},{80,64},{96,80},{112,96},{1... | collective-permute-start | bytes 884744 | tf_op jit(solution)/shard_map/ppermute | solution.py:227
  129.7 6.0 %collective-permute-done.20.refs_1_ = bf16[288,512]{1,0:T(8,128)(2,1)S(1)} collective-permute-done((bf16[288,512]{1,0:T(8,128)(2,1)S(1)}, bf16[288,512]{1,0:T(8,128)(2,1)S(1)}, u32[]{:S(2)}, u32[]{:S(2)}) %collective-permute-start.20) | collective-permute-done | bytes 294944 | tf_op jit(solution)/shard_map/ppermute | solution.py:227
  135.7 4.7 %collective-permute-start.21 = (bf16[288,512]{1,0:T(8,128)(2,1)S(1)}, bf16[288,512]{1,0:T(8,128)(2,1)S(1)}, u32[]{:S(2)}, u32[]{:S(2)}) collective-permute-start(bf16[288,512]{1,0:T(8,128)(2,1)S(1)} %collective-permute-done.20.refs_1_), channel_id=1, source_target_pairs={{0,496},{16,0},{32,16},{48,32},{64,48},{80,64},{96,80},{112,96},{1... | collective-permute-start | bytes 884744 | tf_op jit(solution)/shard_map/ppermute | solution.py:227
  140.4 5.5 %collective-permute-done.21.refs_2_ = bf16[288,512]{1,0:T(8,128)(2,1)S(1)} collective-permute-done((bf16[288,512]{1,0:T(8,128)(2,1)S(1)}, bf16[288,512]{1,0:T(8,128)(2,1)S(1)}, u32[]{:S(2)}, u32[]{:S(2)}) %collective-permute-start.21) | collective-permute-done | bytes 294944 | tf_op jit(solution)/shard_map/ppermute | solution.py:227
  146.0 5.7 %collective-permute-start.22 = (bf16[288,384]{1,0:T(8,128)(2,1)S(1)}, bf16[288,384]{1,0:T(8,128)(2,1)S(1)}, u32[]{:S(2)}, u32[]{:S(2)}) collective-permute-start(bf16[288,384]{1,0:T(8,128)(2,1)S(1)} %slice.4), channel_id=1, source_target_pairs={{0,496},{16,0},{32,16},{48,32},{64,48},{80,64},{96,80},{112,96},{1... | collective-permute-start | bytes 663560 | tf_op jit(solution)/shard_map/ppermute | solution.py:227
  151.7 3.4 %collective-permute-done.22.refs_3_ = bf16[288,384]{1,0:T(8,128)(2,1)S(1)} collective-permute-done((bf16[288,384]{1,0:T(8,128)(2,1)S(1)}, bf16[288,384]{1,0:T(8,128)(2,1)S(1)}, u32[]{:S(2)}, u32[]{:S(2)}) %collective-permute-start.22) | collective-permute-done | bytes 221216 | tf_op jit(solution)/shard_map/ppermute | solution.py:227
  155.1 3.2 %shard_map.102 = bf16[1536,288]{1,0:T(8,128)(2,1)S(1)} custom-call(s32[128,2]{1,0:T(8,128)S(1)} %copy.10.tokens, s32[128]{0:T(128)S(1)} %copy-done.3, bf16[288,512]{1,0:T(8,128)(2,1)S(1)} %add_convert_fusion.refs_0_, bf16[288,512]{1,0:T(8,128)(2,1)S(1)} %collective-permute-done.20.refs_1_, bf16[288,512]{1,0:T(8,128)(2,1)S(1)} %collective-permute-done.21.refs_2_, ...), custom_call_target="tpu_custom_call" | custom-call | flops 603979776 | bytes 1992192 | tf_op jit(solution)/shard_map/pallas_call | solution.py:42
  (46 shorter events, 26.5 us)
Async XLA Ops:
  0.6 2.5 %copy-start.3 = (s32[128]{0:T(128)S(1)}, s32[128]{0:T(128)}, u32[]{:S(2)}) copy-start(s32[128]{0:T(128)} %target.7) | copy-start | bytes 1540
  5.1 17.8 %collective-permute-start.1 = (bf16[288,384]{1,0:T(8,128)(2,1)S(1)}, bf16[288,384]{1,0:T(8,128)(2,1)S(1)}, u32[]{:S(2)}, u32[]{:S(2)}) collective-permute-start(bf16[288,384]{1,0:T(8,128)(2,1)S(1)} %shard_map.96), channel_id=1, source_target_pairs={{0,16},{16,32},{32,48},{48,64},{64,80},{80,96},{96,112},{112,128},... | collective-permute-start | bytes 663560 | tf_op jit(solution)/shard_map/ppermute | solution.py:227
  8.9 28.3 %copy-start.1 = (bf16[4608,128]{1,0:T(8,128)(2,1)S(1)}, bf16[4608,128]{1,0:T(8,128)(2,1)}, u32[]{:S(2)}) copy-start(bf16[4608,128]{1,0:T(8,128)(2,1)} %param.10) | copy-start | bytes 3538948
  11.3 26.0 %copy-start = (bf16[4608,128]{1,0:T(8,128)(2,1)S(1)}, bf16[4608,128]{1,0:T(8,128)(2,1)}, u32[]{:S(2)}) copy-start(bf16[4608,128]{1,0:T(8,128)(2,1)} %param.9) | copy-start | bytes 3538948
  23.0 12.2 %collective-permute-start.2 = (bf16[288,512]{1,0:T(8,128)(2,1)S(1)}, bf16[288,512]{1,0:T(8,128)(2,1)S(1)}, u32[]{:S(2)}, u32[]{:S(2)}) collective-permute-start(bf16[288,512]{1,0:T(8,128)(2,1)S(1)} %pad_add_fusion), channel_id=1, source_target_pairs={{0,16},{16,32},{32,48},{48,64},{64,80},{80,96},{96,112},{112,128},... | collective-permute-start | bytes 884744 | tf_op jit(solution)/shard_map/ppermute | solution.py:227
  35.3 11.3 %collective-permute-start.3 = (bf16[288,512]{1,0:T(8,128)(2,1)S(1)}, bf16[288,512]{1,0:T(8,128)(2,1)S(1)}, u32[]{:S(2)}, u32[]{:S(2)}) collective-permute-start(bf16[288,512]{1,0:T(8,128)(2,1)S(1)} %add.33), channel_id=1, source_target_pairs={{0,16},{16,32},{32,48},{48,64},{64,80},{80,96},{96,112},{112,128},... | collective-permute-start | bytes 884744 | tf_op jit(solution)/shard_map/ppermute | solution.py:227
  37.7 36.9 %collective-permute-start = (bf16[8,288,256]{2,1,0:T(8,128)(2,1)S(1)}, bf16[8,288,256]{2,1,0:T(8,128)(2,1)S(1)}, u32[]{:S(2)}, u32[]{:S(2)}) collective-permute-start(bf16[8,288,256]{2,1,0:T(8,128)(2,1)S(1)} %get-tuple-element.25), channel_id=1, source_target_pairs={{0,1},{1,0},{2,3},{3,2},{4,5},{5,4},{6,7},{7,6},{8,9},{9,8},{10,11... | collective-permute-start | bytes 3538952 | tf_op jit(solution)/shard_map/ppermute | solution.py:237
  46.7 10.1 %collective-permute-start.7 = (bf16[288,512]{1,0:T(8,128)(2,1)S(1)}, bf16[288,512]{1,0:T(8,128)(2,1)S(1)}, u32[]{:S(2)}, u32[]{:S(2)}) collective-permute-start(bf16[288,512]{1,0:T(8,128)(2,1)S(1)} %add.34.refs_0_), channel_id=1, source_target_pairs={{0,2},{1,3},{2,0},{3,1},{4,6},{5,7},{6,4},{7,5},{8,10},{9,11},{10,... | collective-permute-start | bytes 884744 | tf_op jit(solution)/shard_map/ppermute | solution.py:237
  51.5 14.3 %collective-permute-start.4 = (bf16[288,512]{1,0:T(8,128)(2,1)S(1)}, bf16[288,512]{1,0:T(8,128)(2,1)S(1)}, u32[]{:S(2)}, u32[]{:S(2)}) collective-permute-start(bf16[288,512]{1,0:T(8,128)(2,1)S(1)} %add.34.refs_0_), channel_id=1, source_target_pairs={{0,4},{1,5},{2,6},{3,7},{4,0},{5,1},{6,2},{7,3},{8,12},{9,13},{10,... | collective-permute-start | bytes 884744 | tf_op jit(solution)/shard_map/ppermute | solution.py:237
  56.8 12.4 %collective-permute-start.9 = (bf16[288,512]{1,0:T(8,128)(2,1)S(1)}, bf16[288,512]{1,0:T(8,128)(2,1)S(1)}, u32[]{:S(2)}, u32[]{:S(2)}) collective-permute-start(bf16[288,512]{1,0:T(8,128)(2,1)S(1)} %collective-permute-done.7.refs_4_), channel_id=1, source_target_pairs={{0,12},{1,13},{2,14},{3,15},{4,8},{5,9},{6,10},{7,11},{8,4},{9,5},... | collective-permute-start | bytes 884744 | tf_op jit(solution)/shard_map/ppermute | solution.py:237
  59.2 15.4 %collective-permute-start.5 = (bf16[288,512]{1,0:T(8,128)(2,1)S(1)}, bf16[288,512]{1,0:T(8,128)(2,1)S(1)}, u32[]{:S(2)}, u32[]{:S(2)}) collective-permute-start(bf16[288,512]{1,0:T(8,128)(2,1)S(1)} %add.34.refs_0_), channel_id=1, source_target_pairs={{0,12},{1,13},{2,14},{3,15},{4,8},{5,9},{6,10},{7,11},{8,4},{9,5},... | collective-permute-start | bytes 884744 | tf_op jit(solution)/shard_map/ppermute | solution.py:237
  63.8 10.7 %collective-permute-start.8 = (bf16[288,512]{1,0:T(8,128)(2,1)S(1)}, bf16[288,512]{1,0:T(8,128)(2,1)S(1)}, u32[]{:S(2)}, u32[]{:S(2)}) collective-permute-start(bf16[288,512]{1,0:T(8,128)(2,1)S(1)} %collective-permute-done.7.refs_4_), channel_id=1, source_target_pairs={{0,4},{1,5},{2,6},{3,7},{4,0},{5,1},{6,2},{7,3},{8,12},{9,13},{10,... | collective-permute-start | bytes 884744 | tf_op jit(solution)/shard_map/ppermute | solution.py:237
  65.8 11.9 %collective-permute-start.6 = (bf16[288,512]{1,0:T(8,128)(2,1)S(1)}, bf16[288,512]{1,0:T(8,128)(2,1)S(1)}, u32[]{:S(2)}, u32[]{:S(2)}) collective-permute-start(bf16[288,512]{1,0:T(8,128)(2,1)S(1)} %collective-permute-done.4.refs_1_), channel_id=1, source_target_pairs={{0,12},{1,13},{2,14},{3,15},{4,8},{5,9},{6,10},{7,11},{8,4},{9,5},... | collective-permute-start | bytes 884744 | tf_op jit(solution)/shard_map/ppermute | solution.py:237
  69.2 8.6 %collective-permute-start.10 = (bf16[288,512]{1,0:T(8,128)(2,1)S(1)}, bf16[288,512]{1,0:T(8,128)(2,1)S(1)}, u32[]{:S(2)}, u32[]{:S(2)}) collective-permute-start(bf16[288,512]{1,0:T(8,128)(2,1)S(1)} %collective-permute-done.9.refs_6_), channel_id=1, source_target_pairs={{0,4},{1,5},{2,6},{3,7},{4,0},{5,1},{6,2},{7,3},{8,12},{9,13},{10,... | collective-permute-start | bytes 884744 | tf_op jit(solution)/shard_map/ppermute | solution.py:237
  77.8 4.3 %copy-start.5 = (f32[64]{0:T(128)S(1)}, f32[64]{0:T(128)}, u32[]{:S(2)}) copy-start(f32[64]{0:T(128)} %constant.5.clone) | copy-start | bytes 772
  77.8 4.4 %copy-start.2 = (bf16[512,128]{1,0:T(8,128)(2,1)S(1)}, bf16[512,128]{1,0:T(8,128)(2,1)}, u32[]{:S(2)}) copy-start(bf16[512,128]{1,0:T(8,128)(2,1)} %grad.1) | copy-start | bytes 393220
  77.8 4.4 %copy-start.4 = (f32[128]{0:T(128)S(1)}, f32[128]{0:T(128)}, u32[]{:S(2)}) copy-start(f32[128]{0:T(128)} %margins.1) | copy-start | bytes 1540
  80.2 4.2 %collective-permute-start.11 = (f32[384,512]{1,0:T(8,128)S(1)}, f32[384,512]{1,0:T(8,128)S(1)}, u32[]{:S(2)}, u32[]{:S(2)}) collective-permute-start(f32[384,512]{1,0:T(8,128)S(1)} %get-tuple-element.30), channel_id=1, source_target_pairs={{0,1},{1,0},{2,3},{3,2},{4,5},{5,4},{6,7},{7,6},{8,9},{9,8},{10,11... | collective-permute-start | bytes 2359304 | tf_op jit(solution)/shard_map/ppermute | solution.py:237
  86.7 3.7 %collective-permute-start.12 = (bf16[384,512]{1,0:T(8,128)(2,1)S(1)}, bf16[384,512]{1,0:T(8,128)(2,1)S(1)}, u32[]{:S(2)}, u32[]{:S(2)}) collective-permute-start(bf16[384,512]{1,0:T(8,128)(2,1)S(1)} %get-tuple-element.36.sent), channel_id=1, source_target_pairs={{0,1},{1,0},{2,3},{3,2},{4,5},{5,4},{6,7},{7,6},{8,9},{9,8},{10,11... | collective-permute-start | bytes 1179656 | tf_op jit(solution)/shard_map/ppermute | solution.py:237
  91.8 11.2 %collective-permute-start.17 = (bf16[288,512]{1,0:T(8,128)(2,1)S(1)}, bf16[288,512]{1,0:T(8,128)(2,1)S(1)}, u32[]{:S(2)}, u32[]{:S(2)}) collective-permute-start(bf16[288,512]{1,0:T(8,128)(2,1)S(1)} %get-tuple-element.45), channel_id=1, source_target_pairs={{0,4},{1,5},{2,6},{3,7},{4,0},{5,1},{6,2},{7,3},{8,12},{9,13},{10,... | collective-permute-start | bytes 884744 | tf_op jit(solution)/shard_map/ppermute | solution.py:237
  94.7 15.4 %collective-permute-start.14 = (bf16[288,512]{1,0:T(8,128)(2,1)S(1)}, bf16[288,512]{1,0:T(8,128)(2,1)S(1)}, u32[]{:S(2)}, u32[]{:S(2)}) collective-permute-start(bf16[288,512]{1,0:T(8,128)(2,1)S(1)} %get-tuple-element.41), channel_id=1, source_target_pairs={{0,12},{1,13},{2,14},{3,15},{4,8},{5,9},{6,10},{7,11},{8,4},{9,5},... | collective-permute-start | bytes 884744 | tf_op jit(solution)/shard_map/ppermute | solution.py:237
  98.8 13.7 %collective-permute-start.16 = (bf16[288,512]{1,0:T(8,128)(2,1)S(1)}, bf16[288,512]{1,0:T(8,128)(2,1)S(1)}, u32[]{:S(2)}, u32[]{:S(2)}) collective-permute-start(bf16[288,512]{1,0:T(8,128)(2,1)S(1)} %get-tuple-element.43), channel_id=1, source_target_pairs={{0,4},{1,5},{2,6},{3,7},{4,0},{5,1},{6,2},{7,3},{8,12},{9,13},{10,... | collective-permute-start | bytes 884744 | tf_op jit(solution)/shard_map/ppermute | solution.py:237
  103.1 13.0 %collective-permute-start.18 = (bf16[288,512]{1,0:T(8,128)(2,1)S(1)}, bf16[288,512]{1,0:T(8,128)(2,1)S(1)}, u32[]{:S(2)}, u32[]{:S(2)}) collective-permute-start(bf16[288,512]{1,0:T(8,128)(2,1)S(1)} %add_convert_fusion.2), channel_id=1, source_target_pairs={{0,12},{1,13},{2,14},{3,15},{4,8},{5,9},{6,10},{7,11},{8,4},{9,5},... | collective-permute-start | bytes 884744 | tf_op jit(solution)/shard_map/ppermute | solution.py:237
  107.3 13.8 %collective-permute-start.13 = (bf16[288,512]{1,0:T(8,128)(2,1)S(1)}, bf16[288,512]{1,0:T(8,128)(2,1)S(1)}, u32[]{:S(2)}, u32[]{:S(2)}) collective-permute-start(bf16[288,512]{1,0:T(8,128)(2,1)S(1)} %get-tuple-element.39), channel_id=1, source_target_pairs={{0,12},{1,13},{2,14},{3,15},{4,8},{5,9},{6,10},{7,11},{8,4},{9,5},... | collective-permute-start | bytes 884744 | tf_op jit(solution)/shard_map/ppermute | solution.py:237
  110.2 10.8 %collective-permute-start.15 = (bf16[288,512]{1,0:T(8,128)(2,1)S(1)}, bf16[288,512]{1,0:T(8,128)(2,1)S(1)}, u32[]{:S(2)}, u32[]{:S(2)}) collective-permute-start(bf16[288,512]{1,0:T(8,128)(2,1)S(1)} %add_convert_fusion.3), channel_id=1, source_target_pairs={{0,4},{1,5},{2,6},{3,7},{4,0},{5,1},{6,2},{7,3},{8,12},{9,13},{10,... | collective-permute-start | bytes 884744 | tf_op jit(solution)/shard_map/ppermute | solution.py:237
  116.2 10.1 %collective-permute-start.19 = (bf16[288,512]{1,0:T(8,128)(2,1)S(1)}, bf16[288,512]{1,0:T(8,128)(2,1)S(1)}, u32[]{:S(2)}, u32[]{:S(2)}) collective-permute-start(bf16[288,512]{1,0:T(8,128)(2,1)S(1)} %add_convert_fusion.1), channel_id=1, source_target_pairs={{0,2},{1,3},{2,0},{3,1},{4,6},{5,7},{6,4},{7,5},{8,10},{9,11},{10,... | collective-permute-start | bytes 884744 | tf_op jit(solution)/shard_map/ppermute | solution.py:237
  126.5 9.2 %collective-permute-start.20 = (bf16[288,512]{1,0:T(8,128)(2,1)S(1)}, bf16[288,512]{1,0:T(8,128)(2,1)S(1)}, u32[]{:S(2)}, u32[]{:S(2)}) collective-permute-start(bf16[288,512]{1,0:T(8,128)(2,1)S(1)} %add_convert_fusion.refs_0_), channel_id=1, source_target_pairs={{0,496},{16,0},{32,16},{48,32},{64,48},{80,64},{96,80},{112,96},{1... | collective-permute-start | bytes 884744 | tf_op jit(solution)/shard_map/ppermute | solution.py:227
  135.7 10.2 %collective-permute-start.21 = (bf16[288,512]{1,0:T(8,128)(2,1)S(1)}, bf16[288,512]{1,0:T(8,128)(2,1)S(1)}, u32[]{:S(2)}, u32[]{:S(2)}) collective-permute-start(bf16[288,512]{1,0:T(8,128)(2,1)S(1)} %collective-permute-done.20.refs_1_), channel_id=1, source_target_pairs={{0,496},{16,0},{32,16},{48,32},{64,48},{80,64},{96,80},{112,96},{1... | collective-permute-start | bytes 884744 | tf_op jit(solution)/shard_map/ppermute | solution.py:227
  146.0 9.1 %collective-permute-start.22 = (bf16[288,384]{1,0:T(8,128)(2,1)S(1)}, bf16[288,384]{1,0:T(8,128)(2,1)S(1)}, u32[]{:S(2)}, u32[]{:S(2)}) collective-permute-start(bf16[288,384]{1,0:T(8,128)(2,1)S(1)} %slice.4), channel_id=1, source_target_pairs={{0,496},{16,0},{32,16},{48,32},{64,48},{80,64},{96,80},{112,96},{1... | collective-permute-start | bytes 663560 | tf_op jit(solution)/shard_map/ppermute | solution.py:227

commit v2 on v1

--- a/solution.py
+++ b/solution.py
@@ -60,7 +60,7 @@
     for p in range(SPREAD):
         i = home * SPREAD + p
         hit = target[i] == replica
-        c, r = tokens[i, 0], tokens[i, 1]
+        c, r = tokens[0, i], tokens[1, i]
         start = jnp.where(hit, running, start)
         chosen = jnp.where(hit, c, chosen)
         rejected = jnp.where(hit, r, rejected)
@@ -84,23 +84,42 @@
 
 
 def window_of(start):
-    first = jnp.minimum((start // 16) * 16, HOME - WINDOW)
-    return pl.multiple_of(first, 16)
+    first = jnp.minimum((start // 128) * 128, HOME - WINDOW)
+    return pl.multiple_of(first, 128)
+
+
+def pack_one(replicas, offset, tokens, target, home, out, wait=None):
+    replica = lax.axis_index("dp")
+    start, size, place = outgoing(tokens, target, replicas, replica, offset)
+    first = window_of(start)
+    columns = out.shape[1]
+    column = lax.broadcasted_iota(jnp.int32, (1, columns), 1) + RECV - columns
+    live = (column >= place) & (column < place + size)
+    source = jnp.where(live, column - place + start - first, -1)
+    row = lax.broadcasted_iota(jnp.int32, (WINDOW, columns), 0)
+    pick = jnp.where(row == source, 1.0, 0.0).astype(BF16)
+    if wait is not None:
+        wait()
+    out[...] = dot(home[:, pl.ds(first, WINDOW)], pick, NN).astype(BF16)
+
+
+def pack_first_kernel(replicas, tokens, target, home, out, tokens_in, target_in, home_in, sems):
+    copies = [
+        pltpu.make_async_copy(source, place, sems.at[i])
+        for i, (source, place) in enumerate(
+            ((tokens, tokens_in), (target, target_in), (home, home_in))
+        )
+    ]
+    for copy in copies:
+        copy.start()
+    copies[0].wait()
+    copies[1].wait()
+    pack_one(replicas, SPREAD - 1, tokens_in, target_in, home_in, out, copies[2].wait)
 
 
 def pack_kernel(replicas, offsets, tokens, target, home, *outs):
-    replica = lax.axis_index("dp")
     for offset, out in zip(offsets, outs):
-        start, size, place = outgoing(tokens, target, replicas, replica, offset)
-        first = window_of(start)
-        skip = RECV - out.shape[1]
-        column = lax.broadcasted_iota(jnp.int32, (1, out.shape[1]), 1) + skip
-        live = (column >= place) & (column < place + size)
-        source = jnp.where(live, column - place + start - first, -1)
-        row = lax.broadcasted_iota(jnp.int32, (WINDOW, out.shape[1]), 0)
-        pick = (row == source).astype(F32).astype(BF16)
-        rows = home[pl.ds(first, WINDOW), :]
-        out[...] = dot(rows, pick, TN).astype(BF16)
+        pack_one(replicas, offset, tokens, target, home, out)
 
 
 def weights_kernel(q, kv, own, away):
@@ -110,6 +129,12 @@
         own[block, :, HEAD:] = kv[block, core]
         away[block, :, :HEAD] = q[block, 1 - core]
         away[block, :, HEAD:] = kv[block, 1 - core]
+
+
+def turned_kernel(own, away, out):
+    for block in range(own.shape[0]):
+        out[block, : 2 * HEAD] = own[block].astype(F32).T.astype(BF16)
+        out[block, 2 * HEAD :] = away[block].astype(F32).T.astype(BF16)
 
 
 def tables_kernel(replicas, tokens, target, margins, frequency, grad, cosine, sine, begin, upstream):
@@ -144,18 +169,26 @@
     return (x, near, far, across)[relative % 4] * 2 + (y if relative < 4 else 1 - y)
 
 
-def project_kernel(own, away, *refs):
+def partial_products(turned, pieces, numbers):
+    total = None
+    for relative, piece in zip(numbers, pieces):
+        term = dot(turned[block_index(relative)], piece[...], NN)
+        total = term if total is None else total + term
+    return total
+
+
+def project_kernel(numbers, turned, *refs):
+    pieces, out = refs[:-1], refs[-1]
+    out[...] = partial_products(turned, pieces, numbers)
+
+
+def project_last_kernel(numbers, turned, before, *refs):
     pieces, (keep, send) = refs[:-2], refs[-2:]
-    mine = jnp.zeros((2 * HEAD, RECV), F32)
-    other = jnp.zeros((2 * HEAD, RECV), F32)
-    for relative, piece in enumerate(pieces):
-        block = block_index(relative)
-        mine = mine + dot(own[block], piece[...], TN)
-        other = other + dot(away[block], piece[...], TN)
-    keep[: 2 * HEAD] = mine
-    keep[2 * HEAD :] = other[HEAD:]
-    send[: 2 * HEAD] = other
-    send[2 * HEAD :] = mine[HEAD:]
+    total = before[...] + partial_products(turned, pieces, numbers)
+    keep[: 2 * HEAD] = total[: 2 * HEAD]
+    keep[2 * HEAD :] = total[3 * HEAD :]
+    send[: 2 * HEAD] = total[2 * HEAD :].astype(BF16)
+    send[2 * HEAD :] = total[HEAD : 2 * HEAD].astype(BF16)
 
 
 def turn(value, cosine, sine):
@@ -164,9 +197,10 @@
 
 
 def attention_kernel(kept, got, cosine, sine, begin, upstream, attended, send, held):
-    first_core = lax.rem(lax.axis_index("mp"), 2) == 0
+    core = lax.rem(lax.axis_index("mp"), 2)
+    first_core = core == 0
     cos, sin = cosine[...], sine[...]
-    total = kept[...] + got[...]
+    total = kept[...] + got[1 - core].astype(F32)
     own, other = total[HEAD : 2 * HEAD], total[2 * HEAD :]
     query = (QUERY_SCALE * turn(total[:HEAD], cos, sin)).astype(BF16)
     key = turn(jnp.where(first_core, own, other), cos, sin).astype(BF16)
@@ -195,31 +229,53 @@
     held[HEAD:] = dother
 
 
-def spread_kernel(own, away, sent, held, got, *outs):
+def gradients(sent, held, both):
+    got = both.at[1 - lax.rem(lax.axis_index("mp"), 2)]
     down = (held[:HEAD] + got[2 * HEAD :].astype(F32)).astype(BF16)
     dother = (held[HEAD:] + got[HEAD : 2 * HEAD].astype(F32)).astype(BF16)
     mine = jnp.concatenate([sent[:HEAD], down], axis=0)
     other = jnp.concatenate([got[:HEAD], dother], axis=0)
-    for relative, out in enumerate(outs):
+    return mine, other
+
+
+def spread_kernel(numbers, own, away, sent, held, got, *outs):
+    mine, other = gradients(sent, held, got)
+    for relative, out in zip(numbers, outs):
         block = block_index(relative)
         out[...] = (dot(own[block], mine, NN) + dot(away[block], other, NN)).astype(BF16)
 
 
+def unpack_one(replicas, offset, tokens, target, piece):
+    replica = lax.axis_index("dp")
+    start, size, place = outgoing(tokens, target, replicas, replica, offset)
+    first = window_of(start)
+    columns = piece.shape[1]
+    column = lax.broadcasted_iota(jnp.int32, (columns, 1), 0) + RECV - columns
+    live = (column >= place) & (column < place + size)
+    dest = jnp.where(live, column - place + start - first, -1)
+    spot = lax.broadcasted_iota(jnp.int32, (columns, WINDOW), 1)
+    pick = jnp.where(spot == dest, 1.0, 0.0).astype(BF16)
+    return first, dot(piece[...], pick, NN)
+
+
 def unpack_kernel(replicas, tokens, target, *refs):
-    pieces, (home, total) = refs[:-2], refs[-2:]
+    pieces, (home, last) = refs[:-2], refs[-2:]
+    home[...] = jnp.zeros_like(home)
+    for offset, piece in enumerate(pieces):
+        first, back = unpack_one(replicas, offset, tokens, target, piece)
+        window = home[:, pl.ds(first, WINDOW)]
+        home[:, pl.ds(first, WINDOW)] = (window.astype(F32) + back).astype(BF16)
     replica = lax.axis_index("dp")
-    total[...] = jnp.zeros_like(total)
-    for offset, piece in enumerate(pieces):
-        start, size, place = outgoing(tokens, target, replicas, replica, offset)
-        first = window_of(start)
-        skip = RECV - piece.shape[1]
-        row = lax.broadcasted_iota(jnp.int32, (WINDOW, piece.shape[1]), 0)
-        column = lax.broadcasted_iota(jnp.int32, (1, piece.shape[1]), 1) + skip
-        live = (column >= place) & (column < place + size)
-        source = jnp.where(live, column - place + start - first, -1)
-        pick = (row == source).astype(F32).astype(BF16)
-        total[pl.ds(first, WINDOW), :] += dot(pick, piece[...], NT)
-    home[...] = total[...].astype(BF16)
+    start, _, _ = outgoing(tokens, target, replicas, replica, SPREAD - 1)
+    last[...] = home[:, pl.ds(window_of(start), WINDOW)]
+
+
+def unpack_last_kernel(replicas, tokens, target, window, piece, home, out, whole, sem):
+    first, back = unpack_one(replicas, SPREAD - 1, tokens, target, piece)
+    whole[...] = (window[...].astype(F32) + back).astype(BF16)
+    copy = pltpu.make_async_copy(whole, out.at[:, pl.ds(first, WINDOW)], sem)
+    copy.start()
+    copy.wait()
 
 
 def along(value, steps):
@@ -241,6 +297,12 @@
     return swap(value, lambda x, y, core: (x, y, 1 - core))
 
 
+def of_cores(value):
+    count = lax.axis_size("mp")
+    groups = [[place, place + 1] for place in range(0, count, 2)]
+    return lax.all_gather(value, "mp", axis_index_groups=groups)
+
+
 def to_y(value):
     return swap(value, lambda x, y, core: (x, 1 - y, core))
 
@@ -251,27 +313,60 @@
 
 def to_far(value):
     return swap(value, lambda x, y, core: (3 - x, y, core))
+
+
+def plus(*terms):
+    return sum(t.astype(F32) for t in terms).astype(BF16)
 
 
 def body(tokens_home, q_weight, kv_weight, pair_tokens, pair_target, margins, grad_attended):
     replicas = lax.axis_size("dp")
     blocks = lax.axis_size("mp") // 2
     width = tokens_home.shape[1]
-    table = (pair_tokens, pair_target)
-
-    def pack(offsets):
-        outs = [sds((width, CAP if o == SPREAD - 1 else RECV), BF16) for o in offsets]
-        return call(
-            functools.partial(pack_kernel, replicas, offsets),
-            outs,
-            [SMEM, SMEM, VMEM],
-            (*table, tokens_home),
-            2 * len(offsets) * width * WINDOW * RECV,
-        )
-
-    (third,) = pack((3,))
+    table = (pair_tokens.T, pair_target)
+    home = tokens_home.T
+
+    third = pl.pallas_call(
+        functools.partial(pack_first_kernel, replicas),
+        out_shape=sds((width, CAP), BF16),
+        in_specs=[pl.BlockSpec(memory_space=pl.ANY)] * 3,
+        out_specs=VMEM,
+        scratch_shapes=[
+            pltpu.SMEM(table[0].shape, jnp.int32),
+            pltpu.SMEM(table[1].shape, jnp.int32),
+            pltpu.VMEM(home.shape, BF16),
+            pltpu.SemaphoreType.DMA((3,)),
+        ],
+        compiler_params=pltpu.CompilerParams(vmem_limit_bytes=60 << 20),
+        cost_estimate=pl.CostEstimate(
+            flops=2 * width * WINDOW * CAP, bytes_accessed=2 * width * HOME, transcendentals=0
+        ),
+    )(*table, home)
     bucket = along(third, 1)
-    second, first, zeroth = pack((2, 1, 0))
+    (first,) = call(
+        functools.partial(pack_kernel, replicas, (1,)),
+        [sds((width, RECV), BF16)],
+        [SMEM, SMEM, VMEM],
+        (*table, home),
+        2 * width * WINDOW * RECV,
+    )
+    first = along(first, 1)
+    second, zeroth = call(
+        functools.partial(pack_kernel, replicas, (2, 0)),
+        [sds((width, RECV), BF16)] * 2,
+        [SMEM, SMEM, VMEM],
+        (*table, home),
+        4 * width * WINDOW * RECV,
+    )
+    frequency = np.exp(-np.log(ROPE_BASE) * np.arange(HALF) / HALF).astype(np.float32)
+    frequency = jnp.asarray(np.broadcast_to(frequency[:, None], (HALF, HEAD)))
+    tables = call(
+        functools.partial(tables_kernel, replicas),
+        [sds((HALF, RECV), F32), sds((HALF, RECV), F32), sds((8, RECV), jnp.int32), sds((HEAD, RECV), BF16)],
+        [SMEM, SMEM, SMEM, VMEM, VMEM],
+        (*table, margins, frequency, grad_attended),
+        1000,
+    )
     own_w, away_w = call(
         weights_kernel,
         [sds((blocks, width, 2 * HEAD), BF16)] * 2,
@@ -280,55 +375,59 @@
         1000,
     )
     other_w = to_core(away_w)
-    frequency = np.exp(-np.log(ROPE_BASE) * np.arange(HALF) / HALF).astype(np.float32)
-    frequency = jnp.asarray(np.broadcast_to(frequency[:, None], (HALF, HEAD)))
-    cosine, sine, begin, upstream = call(
-        functools.partial(tables_kernel, replicas),
-        [sds((HALF, RECV), F32), sds((HALF, RECV), F32), sds((8, RECV), jnp.int32), sds((HEAD, RECV), BF16)],
-        [SMEM, SMEM, SMEM, VMEM, VMEM],
-        (*table, margins, frequency, grad_attended),
+    bucket = jnp.pad(bucket, ((0, 0), (TAIL, 0))) + second
+    bucket, tables, own_w = lax.optimization_barrier((bucket, tables, own_w))
+    (turned,) = call(
+        turned_kernel,
+        [sds((blocks, 4 * HEAD, width), BF16)],
+        [VMEM, VMEM],
+        (own_w, other_w),
         1000,
     )
-    bucket = jnp.pad(bucket, ((0, 0), (TAIL, 0))) + second
-    bucket = along(bucket, 1) + first
-    moved = along(bucket, 1) + zeroth
-
-    other_y = to_y(moved)
-    near = to_near(moved)
-    far = to_far(moved)
+    mine = along(bucket, 2) + first + zeroth
+
+    mine_y = to_y(mine)
+    near = to_near(mine)
+    far = to_far(mine)
+    far_y = to_far(mine_y)
+    near_y = to_near(mine_y)
     across = to_far(near)
-    far_y = to_far(other_y)
-    near_y = to_near(other_y)
     across_y = to_near(far_y)
-    pieces = (moved, near, far, across, other_y, near_y, far_y, across_y)
+    (before,) = call(
+        functools.partial(project_kernel, (0, 1, 4, 6)),
+        [sds((4 * HEAD, RECV), F32)],
+        [VMEM] * 5,
+        (turned, mine, near, mine_y, far_y),
+        blocks * width * 4 * HEAD * RECV,
+    )
     keep, send = call(
-        project_kernel,
-        [sds((3 * HEAD, RECV), F32)] * 2,
-        [VMEM] * 10,
-        (own_w, other_w, *pieces),
-        2 * blocks * width * 4 * HEAD * RECV,
-    )
-    got = to_core(send)
+        functools.partial(project_last_kernel, (2, 3, 5, 7)),
+        [sds((3 * HEAD, RECV), F32), sds((3 * HEAD, RECV), BF16)],
+        [VMEM] * 6,
+        (turned, before, far, across, near_y, across_y),
+        blocks * width * 4 * HEAD * RECV,
+    )
+    got = of_cores(send)
     attended, send, held = call(
         attention_kernel,
         [sds((RECV, HEAD), BF16), sds((3 * HEAD, RECV), BF16), sds((2 * HEAD, RECV), F32)],
         [VMEM] * 6,
-        (keep, got, cosine, sine, begin, upstream),
+        (keep, got, *tables),
         14 * HEAD * RECV * RECV,
     )
-    got = to_core(send)
-    parts = call(
-        spread_kernel,
-        [sds((width, RECV), BF16)] * 8,
-        [VMEM] * 5,
-        (own_w, other_w, send, held, got),
-        2 * blocks * width * 4 * HEAD * RECV,
-    )
-    mine, near, far, across, mine_y, near_y, far_y, across_y = parts
-
-    def plus(*terms):
-        return sum(t.astype(F32) for t in terms).astype(BF16)
-
+    got = of_cores(send)
+
+    def spread(numbers):
+        return call(
+            functools.partial(spread_kernel, numbers),
+            [sds((width, RECV), BF16)] * len(numbers),
+            [VMEM] * 5,
+            (own_w, other_w, send, held, got),
+            len(numbers) * width * 8 * HEAD * RECV,
+        )
+
+    across_y, far, near_y, across = spread((7, 2, 5, 3))
+    mine, near, mine_y, far_y = spread((0, 1, 4, 6))
     forward_y = plus(far_y, to_near(across_y))
     forward = plus(near, to_far(across))
     here_y = plus(mine_y, to_near(near_y), to_far(forward_y))
@@ -337,15 +436,26 @@
     back1 = along(here, -1)
     back2 = along(back1, -1)
     back3 = along(back2[:, TAIL:], -1)
-    (grad_home,) = call(
+    most, window = call(
         functools.partial(unpack_kernel, replicas),
-        [sds((HOME, width), BF16)],
-        [SMEM, SMEM] + [VMEM] * 4,
-        (*table, here, back1, back2, back3),
-        2 * SPREAD * width * WINDOW * RECV,
-        scratch=[pltpu.VMEM((HOME, width), F32)],
-    )
-    return (attended, grad_home)
+        [sds((width, HOME), BF16), sds((width, WINDOW), BF16)],
+        [SMEM, SMEM, VMEM, VMEM, VMEM],
+        (*table, here, back1, back2),
+        6 * width * WINDOW * RECV,
+    )
+    grad_home = pl.pallas_call(
+        functools.partial(unpack_last_kernel, replicas),
+        out_shape=sds((width, HOME), BF16),
+        in_specs=[SMEM, SMEM, VMEM, VMEM, pl.BlockSpec(memory_space=pl.ANY)],
+        out_specs=pl.BlockSpec(memory_space=pl.ANY),
+        scratch_shapes=[pltpu.VMEM((width, WINDOW), BF16), pltpu.SemaphoreType.DMA],
+        input_output_aliases={4: 0},
+        compiler_params=pltpu.CompilerParams(vmem_limit_bytes=24 << 20),
+        cost_estimate=pl.CostEstimate(
+            flops=2 * width * WINDOW * CAP, bytes_accessed=4 * width * WINDOW, transcendentals=0
+        ),
+    )(*table, window, back3, most)
+    return (attended, grad_home.T)
 
 
 def solution(mesh):

time: 163 us -> 152 us (0.933); the launches traced: 160 us -> 152 us
  waiting for transfers between devices: 65.9 us -> 54.6 us
  blocking collectives: 0 us -> 4.72 us
    ppermute x6, waiting for transfers between devices: 43.9 us -> 32.6 us  [along(): lax.ppermute(value, 'dp', [(s, (s + steps) % count) for s in range(count)])]
    ppermute x17 -> x15, starting transfers between devices: 50.8 us -> 44.6 us  [swap(): return lax.ppermute(value, 'mp', pairs)]
    all_gather x0 -> x2, blocking collectives: none -> 4.72 us  [of_cores(): return lax.all_gather(value, 'mp', axis_index_groups=groups)]
    ppermute x6, starting transfers between devices: 21.2 us -> 25.8 us  [along(): lax.ppermute(value, 'dp', [(s, (s + steps) % count) for s in range(count)])]
    pallas_call x0 -> x2, Pallas kernels: none -> 4.03 us  [the longest x1 2.33 us: body(): pl.pallas_call(functools.partial(pack_first_kernel, replicas), out_shape=...]
    pallas_call x8 -> x11, Pallas kernels: 16.2 us -> 13.1 us  [call(): pl.pallas_call(kernel, out_shape=outs, in_specs=in_specs, out_specs=[VMEM...]
    unnamed x15 -> x20, local copies, waits for them, and re-layouts: 3.8 us -> 3.02 us
    ppermute x17 -> x15, waiting for transfers between devices: 22 us -> 22 us  [swap(): return lax.ppermute(value, 'mp', pairs)]
  transfers between devices with their start and end apart: 23 -> 21, of which waited for: 15 -> 13; matrix products, arithmetic and copies ran while one was open for 0% -> 0% of each run, Pallas kernels for 3% -> 6%
where the time goes in v2:
time: 152 us
  starting transfers between devices  70.4 us (46%)
  waiting for transfers between devices  54.6 us (36%)
  Pallas kernels  17.2 us (11%)
  blocking collectives  4.72 us (3%)
  local copies, waits for them, and re-layouts  3.11 us (2%)
    ppermute x15, starting transfers between devices, swap(): return lax.ppermute(value, 'mp', pairs)  44.6 us
    ppermute x6, waiting for transfers between devices, along(): lax.ppermute(value, 'dp', [(s, (s + steps) % count) for s in range(count)])  32.6 us
    ppermute x6, starting transfers between devices, along(): lax.ppermute(value, 'dp', [(s, (s + steps) % count) for s in range(count)])  25.8 us
    ppermute x15, waiting for transfers between devices, swap(): return lax.ppermute(value, 'mp', pairs)  22 us
    pallas_call x11, Pallas kernels, call(): pl.pallas_call(kernel, out_shape=outs, in_specs=in_specs, out_specs=[VMEM...  13.1 us
    all_gather x2, blocking collectives, of_cores(): return lax.all_gather(value, 'mp', axis_index_groups=groups)  4.72 us
  transfers between devices with their start and end apart: 21, of which 13 were waited for; matrix products, arithmetic and copies ran while one was open for 0% of the time, Pallas kernels for 6%

profile of v2, /device:TPU:6, one launch (start us, length us, event | category | flops | bytes accessed | tf_op | source)
XLA Modules:
  0.0 151.5 jit_solution(12279744846408235405)
XLA Ops:
  0.6 2.3 %shard_map.95 = bf16[288,384]{1,0:T(8,128)(2,1)} custom-call(s32[2,128]{1,0:T(2,128)} %bitcast.15, s32[128]{0:T(128)} %target.11, bf16[288,1536]{1,0:T(8,128)(2,1)} %bitcast.9), custom_call_target="tpu_custom_call" | custom-call | flops 113246208 | bytes 884736 | tf_op jit(solution)/shard_map/pallas_call | solution.py:329
  3.0 3.8 %collective-permute-start = (bf16[288,384]{1,0:T(8,128)(2,1)}, bf16[288,384]{1,0:T(8,128)(2,1)S(1)}, u32[]{:S(2)}, u32[]{:S(2)}) collective-permute-start(bf16[288,384]{1,0:T(8,128)(2,1)} %shard_map.95), channel_id=1, source_target_pairs={{0,16},{16,32},{32,48},{48,64},{64,80},{80,96},{96,112},{112,128},... | collective-permute-start | bytes 663560 | tf_op jit(solution)/shard_map/ppermute | solution.py:283
  9.1 3.8 %collective-permute-start.3 = (bf16[288,512]{1,0:T(8,128)(2,1)S(1)}, bf16[288,512]{1,0:T(8,128)(2,1)S(1)}, u32[]{:S(2)}, u32[]{:S(2)}) collective-permute-start(bf16[288,512]{1,0:T(8,128)(2,1)S(1)} %shard_map.100), channel_id=1, source_target_pairs={{0,16},{16,32},{32,48},{48,64},{64,80},{80,96},{96,112},{112,128},... | collective-permute-start | bytes 884744 | tf_op jit(solution)/shard_map/ppermute | solution.py:283
  17.4 4.4 %collective-permute-done = bf16[288,384]{1,0:T(8,128)(2,1)S(1)} collective-permute-done((bf16[288,384]{1,0:T(8,128)(2,1)}, bf16[288,384]{1,0:T(8,128)(2,1)S(1)}, u32[]{:S(2)}, u32[]{:S(2)}) %collective-permute-start) | collective-permute-done | bytes 221216 | tf_op jit(solution)/shard_map/ppermute | solution.py:283
  21.8 2.1 %collective-permute-start.2 = (bf16[288,512]{1,0:T(8,128)(2,1)S(1)}, bf16[288,512]{1,0:T(8,128)(2,1)S(1)}, u32[]{:S(2)}, u32[]{:S(2)}) collective-permute-start(bf16[288,512]{1,0:T(8,128)(2,1)S(1)} %pad_add_fusion), channel_id=1, source_target_pairs={{0,32},{16,48},{32,64},{48,80},{64,96},{80,112},{96,128},{112,144}... | collective-permute-start | bytes 884744 | tf_op jit(solution)/shard_map/ppermute | solution.py:283
  25.8 2.1 %collective-permute-done.3 = bf16[288,512]{1,0:T(8,128)(2,1)S(1)} collective-permute-done((bf16[288,512]{1,0:T(8,128)(2,1)S(1)}, bf16[288,512]{1,0:T(8,128)(2,1)S(1)}, u32[]{:S(2)}, u32[]{:S(2)}) %collective-permute-start.3) | collective-permute-done | bytes 294944 | tf_op jit(solution)/shard_map/ppermute | solution.py:283
  27.9 10.7 %collective-permute-done.2 = bf16[288,512]{1,0:T(8,128)(2,1)S(1)} collective-permute-done((bf16[288,512]{1,0:T(8,128)(2,1)S(1)}, bf16[288,512]{1,0:T(8,128)(2,1)S(1)}, u32[]{:S(2)}, u32[]{:S(2)}) %collective-permute-start.2) | collective-permute-done | bytes 294944 | tf_op jit(solution)/shard_map/ppermute | solution.py:283
  38.7 4.8 %collective-permute-start.5 = (bf16[288,512]{1,0:T(8,128)(2,1)S(1)}, bf16[288,512]{1,0:T(8,128)(2,1)S(1)}, u32[]{:S(2)}, u32[]{:S(2)}) collective-permute-start(bf16[288,512]{1,0:T(8,128)(2,1)S(1)} %add_add_fusion.refs_0_), channel_id=1, source_target_pairs={{0,2},{1,3},{2,0},{3,1},{4,6},{5,7},{6,4},{7,5},{8,10},{9,11},{10,... | collective-permute-start | bytes 884744 | tf_op jit(solution)/shard_map/ppermute | solution.py:293
  43.5 2.8 %collective-permute-start.4 = (bf16[288,512]{1,0:T(8,128)(2,1)S(1)}, bf16[288,512]{1,0:T(8,128)(2,1)S(1)}, u32[]{:S(2)}, u32[]{:S(2)}) collective-permute-start(bf16[288,512]{1,0:T(8,128)(2,1)S(1)} %add_add_fusion.refs_0_), channel_id=1, source_target_pairs={{0,4},{1,5},{2,6},{3,7},{4,0},{5,1},{6,2},{7,3},{8,12},{9,13},{10,... | collective-permute-start | bytes 884744 | tf_op jit(solution)/shard_map/ppermute | solution.py:293
  46.2 3.2 %collective-permute-done.5.refs_2_ = bf16[288,512]{1,0:T(8,128)(2,1)S(1)} collective-permute-done((bf16[288,512]{1,0:T(8,128)(2,1)S(1)}, bf16[288,512]{1,0:T(8,128)(2,1)S(1)}, u32[]{:S(2)}, u32[]{:S(2)}) %collective-permute-start.5) | collective-permute-done | bytes 294944 | tf_op jit(solution)/shard_map/ppermute | solution.py:293
  49.4 2.1 %collective-permute-start.6 = (bf16[288,512]{1,0:T(8,128)(2,1)S(1)}, bf16[288,512]{1,0:T(8,128)(2,1)S(1)}, u32[]{:S(2)}, u32[]{:S(2)}) collective-permute-start(bf16[288,512]{1,0:T(8,128)(2,1)S(1)} %collective-permute-done.5.refs_2_), channel_id=1, source_target_pairs={{0,12},{1,13},{2,14},{3,15},{4,8},{5,9},{6,10},{7,11},{8,4},{9,5},... | collective-permute-start | bytes 884744 | tf_op jit(solution)/shard_map/ppermute | solution.py:293
  51.5 5.0 %collective-permute-start.7 = (bf16[288,512]{1,0:T(8,128)(2,1)S(1)}, bf16[288,512]{1,0:T(8,128)(2,1)S(1)}, u32[]{:S(2)}, u32[]{:S(2)}) collective-permute-start(bf16[288,512]{1,0:T(8,128)(2,1)S(1)} %add_add_fusion.refs_0_), channel_id=1, source_target_pairs={{0,12},{1,13},{2,14},{3,15},{4,8},{5,9},{6,10},{7,11},{8,4},{9,5},... | collective-permute-start | bytes 884744 | tf_op jit(solution)/shard_map/ppermute | solution.py:293
  58.4 2.7 %collective-permute-start.8 = (bf16[288,512]{1,0:T(8,128)(2,1)S(1)}, bf16[288,512]{1,0:T(8,128)(2,1)S(1)}, u32[]{:S(2)}, u32[]{:S(2)}) collective-permute-start(bf16[288,512]{1,0:T(8,128)(2,1)S(1)} %collective-permute-done.4.refs_1_), channel_id=1, source_target_pairs={{0,12},{1,13},{2,14},{3,15},{4,8},{5,9},{6,10},{7,11},{8,4},{9,5},... | collective-permute-start | bytes 884744 | tf_op jit(solution)/shard_map/ppermute | solution.py:293
  68.4 3.2 %collective-permute-done.8.refs_1_ = bf16[288,512]{1,0:T(8,128)(2,1)S(1)} collective-permute-done((bf16[288,512]{1,0:T(8,128)(2,1)S(1)}, bf16[288,512]{1,0:T(8,128)(2,1)S(1)}, u32[]{:S(2)}, u32[]{:S(2)}) %collective-permute-start.8) | collective-permute-done | bytes 294944 | tf_op jit(solution)/shard_map/ppermute | solution.py:293
  72.9 2.4 %all-gather = bf16[768,512]{1,0:T(8,128)(2,1)S(1)} all-gather(bf16[384,512]{1,0:T(8,128)(2,1)S(1)} %get-tuple-element.42), channel_id=2, replica_groups={{0,1},{2,3},{4,5},{6,7},{8,9},{10,11},{12,13},{14,15},{16,17},{18,19},{..., dimensions={0}, use_global_device_ids=true | all-gather | bytes 1179648 | tf_op jit(solution)/shard_map/all_gather | solution.py:303
  75.2 2.3 %shard_map.103 = (bf16[512,128]{1,0:T(8,128)(2,1)}, bf16[384,512]{1,0:T(8,128)(2,1)S(1)}, f32[256,512]{1,0:T(8,128)S(1)}) custom-call(f32[384,512]{1,0:T(8,128)S(1)} %get-tuple-element.41.kept, bf16[2,384,512]{2,1,0:T(8,128)(2,1)S(1)} %bitcast.12, f32[64,512]{1,0:T(8,128)S(1)} %get-tuple-element.43.cosine, f32[64,512]{1,0:T(8,128)S(1)} %get-tuple-element.44.sine, ...), custom_call_target="tpu_custom_call" | custom-call | flops 469762048 | bytes 3031040 | tf_op jit(solution)/shard_map/pallas_call | solution.py:42
  77.5 2.4 %all-gather.1 = bf16[768,512]{1,0:T(8,128)(2,1)S(1)} all-gather(bf16[384,512]{1,0:T(8,128)(2,1)S(1)} %get-tuple-element.48.sent), channel_id=3, replica_groups={{0,1},{2,3},{4,5},{6,7},{8,9},{10,11},{12,13},{14,15},{16,17},{18,19},{..., dimensions={0}, use_global_device_ids=true | all-gather | bytes 1179648 | tf_op jit(solution)/shard_map/all_gather | solution.py:303
  80.6 1.9 %collective-permute-start.15 = (bf16[288,512]{1,0:T(8,128)(2,1)S(1)}, bf16[288,512]{1,0:T(8,128)(2,1)S(1)}, u32[]{:S(2)}, u32[]{:S(2)}) collective-permute-start(bf16[288,512]{1,0:T(8,128)(2,1)S(1)} %get-tuple-element.57), channel_id=1, source_target_pairs={{0,4},{1,5},{2,6},{3,7},{4,0},{5,1},{6,2},{7,3},{8,12},{9,13},{10,... | collective-permute-start | bytes 884744 | tf_op jit(solution)/shard_map/ppermute | solution.py:293
  82.6 3.9 %collective-permute-start.12 = (bf16[288,512]{1,0:T(8,128)(2,1)S(1)}, bf16[288,512]{1,0:T(8,128)(2,1)S(1)}, u32[]{:S(2)}, u32[]{:S(2)}) collective-permute-start(bf16[288,512]{1,0:T(8,128)(2,1)S(1)} %get-tuple-element.53), channel_id=1, source_target_pairs={{0,12},{1,13},{2,14},{3,15},{4,8},{5,9},{6,10},{7,11},{8,4},{9,5},... | collective-permute-start | bytes 884744 | tf_op jit(solution)/shard_map/ppermute | solution.py:293
  86.5 1.9 %collective-permute-start.14 = (bf16[288,512]{1,0:T(8,128)(2,1)S(1)}, bf16[288,512]{1,0:T(8,128)(2,1)S(1)}, u32[]{:S(2)}, u32[]{:S(2)}) collective-permute-start(bf16[288,512]{1,0:T(8,128)(2,1)S(1)} %get-tuple-element.55), channel_id=1, source_target_pairs={{0,4},{1,5},{2,6},{3,7},{4,0},{5,1},{6,2},{7,3},{8,12},{9,13},{10,... | collective-permute-start | bytes 884744 | tf_op jit(solution)/shard_map/ppermute | solution.py:293
  89.2 3.2 %collective-permute-done.15 = bf16[288,512]{1,0:T(8,128)(2,1)S(1)} collective-permute-done((bf16[288,512]{1,0:T(8,128)(2,1)S(1)}, bf16[288,512]{1,0:T(8,128)(2,1)S(1)}, u32[]{:S(2)}, u32[]{:S(2)}) %collective-permute-start.15) | collective-permute-done | bytes 294944 | tf_op jit(solution)/shard_map/ppermute | solution.py:293
  92.5 1.9 %collective-permute-start.16 = (bf16[288,512]{1,0:T(8,128)(2,1)S(1)}, bf16[288,512]{1,0:T(8,128)(2,1)S(1)}, u32[]{:S(2)}, u32[]{:S(2)}) collective-permute-start(bf16[288,512]{1,0:T(8,128)(2,1)S(1)} %add_convert_fusion.2), channel_id=1, source_target_pairs={{0,12},{1,13},{2,14},{3,15},{4,8},{5,9},{6,10},{7,11},{8,4},{9,5},... | collective-permute-start | bytes 884744 | tf_op jit(solution)/shard_map/ppermute | solution.py:293
  94.4 5.1 %collective-permute-start.11 = (bf16[288,512]{1,0:T(8,128)(2,1)S(1)}, bf16[288,512]{1,0:T(8,128)(2,1)S(1)}, u32[]{:S(2)}, u32[]{:S(2)}) collective-permute-start(bf16[288,512]{1,0:T(8,128)(2,1)S(1)} %get-tuple-element.51), channel_id=1, source_target_pairs={{0,12},{1,13},{2,14},{3,15},{4,8},{5,9},{6,10},{7,11},{8,4},{9,5},... | collective-permute-start | bytes 884744 | tf_op jit(solution)/shard_map/ppermute | solution.py:293
  101.6 3.9 %collective-permute-done.16 = bf16[288,512]{1,0:T(8,128)(2,1)S(1)} collective-permute-done((bf16[288,512]{1,0:T(8,128)(2,1)S(1)}, bf16[288,512]{1,0:T(8,128)(2,1)S(1)}, u32[]{:S(2)}, u32[]{:S(2)}) %collective-permute-start.16) | collective-permute-done | bytes 294944 | tf_op jit(solution)/shard_map/ppermute | solution.py:293
  105.6 4.8 %collective-permute-start.17 = (bf16[288,512]{1,0:T(8,128)(2,1)S(1)}, bf16[288,512]{1,0:T(8,128)(2,1)S(1)}, u32[]{:S(2)}, u32[]{:S(2)}) collective-permute-start(bf16[288,512]{1,0:T(8,128)(2,1)S(1)} %add_convert_fusion.1), channel_id=1, source_target_pairs={{0,2},{1,3},{2,0},{3,1},{4,6},{5,7},{6,4},{7,5},{8,10},{9,11},{10,... | collective-permute-start | bytes 884744 | tf_op jit(solution)/shard_map/ppermute | solution.py:293
  110.5 5.3 %collective-permute-done.17 = bf16[288,512]{1,0:T(8,128)(2,1)S(1)} collective-permute-done((bf16[288,512]{1,0:T(8,128)(2,1)S(1)}, bf16[288,512]{1,0:T(8,128)(2,1)S(1)}, u32[]{:S(2)}, u32[]{:S(2)}) %collective-permute-start.17) | collective-permute-done | bytes 294944 | tf_op jit(solution)/shard_map/ppermute | solution.py:293
  115.9 6.8 %collective-permute-start.18 = (bf16[288,512]{1,0:T(8,128)(2,1)S(1)}, bf16[288,512]{1,0:T(8,128)(2,1)S(1)}, u32[]{:S(2)}, u32[]{:S(2)}) collective-permute-start(bf16[288,512]{1,0:T(8,128)(2,1)S(1)} %add_convert_fusion.refs_0_), channel_id=1, source_target_pairs={{0,496},{16,0},{32,16},{48,32},{64,48},{80,64},{96,80},{112,96},{1... | collective-permute-start | bytes 884744 | tf_op jit(solution)/shard_map/ppermute | solution.py:283
  122.7 7.4 %collective-permute-done.18.refs_1_ = bf16[288,512]{1,0:T(8,128)(2,1)S(1)} collective-permute-done((bf16[288,512]{1,0:T(8,128)(2,1)S(1)}, bf16[288,512]{1,0:T(8,128)(2,1)S(1)}, u32[]{:S(2)}, u32[]{:S(2)}) %collective-permute-start.18) | collective-permute-done | bytes 294944 | tf_op jit(solution)/shard_map/ppermute | solution.py:283
  130.1 3.9 %collective-permute-start.19 = (bf16[288,512]{1,0:T(8,128)(2,1)S(1)}, bf16[288,512]{1,0:T(8,128)(2,1)S(1)}, u32[]{:S(2)}, u32[]{:S(2)}) collective-permute-start(bf16[288,512]{1,0:T(8,128)(2,1)S(1)} %collective-permute-done.18.refs_1_), channel_id=1, source_target_pairs={{0,496},{16,0},{32,16},{48,32},{64,48},{80,64},{96,80},{112,96},{1... | collective-permute-start | bytes 884744 | tf_op jit(solution)/shard_map/ppermute | solution.py:283
  134.0 6.9 %collective-permute-done.19.refs_2_ = bf16[288,512]{1,0:T(8,128)(2,1)S(1)} collective-permute-done((bf16[288,512]{1,0:T(8,128)(2,1)S(1)}, bf16[288,512]{1,0:T(8,128)(2,1)S(1)}, u32[]{:S(2)}, u32[]{:S(2)}) %collective-permute-start.19) | collective-permute-done | bytes 294944 | tf_op jit(solution)/shard_map/ppermute | solution.py:283
  140.9 5.5 %collective-permute-start.20 = (bf16[288,384]{1,0:T(8,128)(2,1)S(1)}, bf16[288,384]{1,0:T(8,128)(2,1)S(1)}, u32[]{:S(2)}, u32[]{:S(2)}) collective-permute-start(bf16[288,384]{1,0:T(8,128)(2,1)S(1)} %slice.4), channel_id=1, source_target_pairs={{0,496},{16,0},{32,16},{48,32},{64,48},{80,64},{96,80},{112,96},{1... | collective-permute-start | bytes 663560 | tf_op jit(solution)/shard_map/ppermute | solution.py:283
  146.4 2.4 %shard_map.106 = (bf16[288,1536]{1,0:T(8,128)(2,1)}, bf16[288,512]{1,0:T(8,128)(2,1)S(1)}) custom-call(s32[2,128]{1,0:T(2,128)S(1)} %bitcast.19, s32[128]{0:T(128)S(1)} %copy-done.7, bf16[288,512]{1,0:T(8,128)(2,1)S(1)} %add_convert_fusion.refs_0_, bf16[288,512]{1,0:T(8,128)(2,1)S(1)} %collective-permute-done.18.refs_1_, ...), custom_call_target="tpu_custom_call" | custom-call | flops 452984832 | bytes 2065920 | tf_op jit(solution)/shard_map/pallas_call | solution.py:42
  (53 shorter events, 25.8 us)
Async XLA Ops:
  0.6 6.2 %copy-start = (bf16[1536,288]{0,1:T(8,128)(2,1)S(1)}, bf16[1536,288]{0,1:T(8,128)(2,1)}, u32[]{:S(2)}) copy-start(bf16[1536,288]{0,1:T(8,128)(2,1)} %param.8) | copy-start | bytes 2654212
  0.6 12.3 %copy-start.1 = (bf16[4608,128]{1,0:T(8,128)(2,1)S(1)}, bf16[4608,128]{1,0:T(8,128)(2,1)}, u32[]{:S(2)}) copy-start(bf16[4608,128]{1,0:T(8,128)(2,1)} %param.9) | copy-start | bytes 3538948
  3.0 18.7 %collective-permute-start = (bf16[288,384]{1,0:T(8,128)(2,1)}, bf16[288,384]{1,0:T(8,128)(2,1)S(1)}, u32[]{:S(2)}, u32[]{:S(2)}) collective-permute-start(bf16[288,384]{1,0:T(8,128)(2,1)} %shard_map.95), channel_id=1, source_target_pairs={{0,16},{16,32},{32,48},{48,64},{64,80},{80,96},{96,112},{112,128},... | collective-permute-start | bytes 663560 | tf_op jit(solution)/shard_map/ppermute | solution.py:283
  6.8 0.7 copy-start.4
  7.5 0.7 copy-start.6
  9.1 18.8 %collective-permute-start.3 = (bf16[288,512]{1,0:T(8,128)(2,1)S(1)}, bf16[288,512]{1,0:T(8,128)(2,1)S(1)}, u32[]{:S(2)}, u32[]{:S(2)}) collective-permute-start(bf16[288,512]{1,0:T(8,128)(2,1)S(1)} %shard_map.100), channel_id=1, source_target_pairs={{0,16},{16,32},{32,48},{48,64},{64,80},{80,96},{96,112},{112,128},... | collective-permute-start | bytes 884744 | tf_op jit(solution)/shard_map/ppermute | solution.py:283
  12.9 1.3 copy-start.2
  14.2 0.7 copy-start.9
  14.2 0.9 copy-start.3
  14.2 0.9 copy-start.5
  14.2 0.9 copy-start.7
  14.2 0.9 copy-start.8
  21.8 16.8 %collective-permute-start.2 = (bf16[288,512]{1,0:T(8,128)(2,1)S(1)}, bf16[288,512]{1,0:T(8,128)(2,1)S(1)}, u32[]{:S(2)}, u32[]{:S(2)}) collective-permute-start(bf16[288,512]{1,0:T(8,128)(2,1)S(1)} %pad_add_fusion), channel_id=1, source_target_pairs={{0,32},{16,48},{32,64},{48,80},{64,96},{80,112},{96,128},{112,144}... | collective-permute-start | bytes 884744 | tf_op jit(solution)/shard_map/ppermute | solution.py:283
  23.8 40.5 %collective-permute-start.1 = (bf16[8,288,256]{2,1,0:T(8,128)(2,1)S(1)}, bf16[8,288,256]{2,1,0:T(8,128)(2,1)S(1)}, u32[]{:S(2)}, u32[]{:S(2)}) collective-permute-start(bf16[8,288,256]{2,1,0:T(8,128)(2,1)S(1)} %get-tuple-element.38), channel_id=1, source_target_pairs={{0,1},{1,0},{2,3},{3,2},{4,5},{5,4},{6,7},{7,6},{8,9},{9,8},{10,11... | collective-permute-start | bytes 3538952 | tf_op jit(solution)/shard_map/ppermute | solution.py:293
  38.7 10.8 %collective-permute-start.5 = (bf16[288,512]{1,0:T(8,128)(2,1)S(1)}, bf16[288,512]{1,0:T(8,128)(2,1)S(1)}, u32[]{:S(2)}, u32[]{:S(2)}) collective-permute-start(bf16[288,512]{1,0:T(8,128)(2,1)S(1)} %add_add_fusion.refs_0_), channel_id=1, source_target_pairs={{0,2},{1,3},{2,0},{3,1},{4,6},{5,7},{6,4},{7,5},{8,10},{9,11},{10,... | collective-permute-start | bytes 884744 | tf_op jit(solution)/shard_map/ppermute | solution.py:293
  43.5 14.9 %collective-permute-start.4 = (bf16[288,512]{1,0:T(8,128)(2,1)S(1)}, bf16[288,512]{1,0:T(8,128)(2,1)S(1)}, u32[]{:S(2)}, u32[]{:S(2)}) collective-permute-start(bf16[288,512]{1,0:T(8,128)(2,1)S(1)} %add_add_fusion.refs_0_), channel_id=1, source_target_pairs={{0,4},{1,5},{2,6},{3,7},{4,0},{5,1},{6,2},{7,3},{8,12},{9,13},{10,... | collective-permute-start | bytes 884744 | tf_op jit(solution)/shard_map/ppermute | solution.py:293
  49.4 13.0 %collective-permute-start.6 = (bf16[288,512]{1,0:T(8,128)(2,1)S(1)}, bf16[288,512]{1,0:T(8,128)(2,1)S(1)}, u32[]{:S(2)}, u32[]{:S(2)}) collective-permute-start(bf16[288,512]{1,0:T(8,128)(2,1)S(1)} %collective-permute-done.5.refs_2_), channel_id=1, source_target_pairs={{0,12},{1,13},{2,14},{3,15},{4,8},{5,9},{6,10},{7,11},{8,4},{9,5},... | collective-permute-start | bytes 884744 | tf_op jit(solution)/shard_map/ppermute | solution.py:293
  51.5 16.9 %collective-permute-start.7 = (bf16[288,512]{1,0:T(8,128)(2,1)S(1)}, bf16[288,512]{1,0:T(8,128)(2,1)S(1)}, u32[]{:S(2)}, u32[]{:S(2)}) collective-permute-start(bf16[288,512]{1,0:T(8,128)(2,1)S(1)} %add_add_fusion.refs_0_), channel_id=1, source_target_pairs={{0,12},{1,13},{2,14},{3,15},{4,8},{5,9},{6,10},{7,11},{8,4},{9,5},... | collective-permute-start | bytes 884744 | tf_op jit(solution)/shard_map/ppermute | solution.py:293
  56.5 12.0 %collective-permute-start.9 = (bf16[288,512]{1,0:T(8,128)(2,1)S(1)}, bf16[288,512]{1,0:T(8,128)(2,1)S(1)}, u32[]{:S(2)}, u32[]{:S(2)}) collective-permute-start(bf16[288,512]{1,0:T(8,128)(2,1)S(1)} %collective-permute-done.5.refs_2_), channel_id=1, source_target_pairs={{0,4},{1,5},{2,6},{3,7},{4,0},{5,1},{6,2},{7,3},{8,12},{9,13},{10,... | collective-permute-start | bytes 884744 | tf_op jit(solution)/shard_map/ppermute | solution.py:293
  58.4 13.2 %collective-permute-start.8 = (bf16[288,512]{1,0:T(8,128)(2,1)S(1)}, bf16[288,512]{1,0:T(8,128)(2,1)S(1)}, u32[]{:S(2)}, u32[]{:S(2)}) collective-permute-start(bf16[288,512]{1,0:T(8,128)(2,1)S(1)} %collective-permute-done.4.refs_1_), channel_id=1, source_target_pairs={{0,12},{1,13},{2,14},{3,15},{4,8},{5,9},{6,10},{7,11},{8,4},{9,5},... | collective-permute-start | bytes 884744 | tf_op jit(solution)/shard_map/ppermute | solution.py:293
  62.5 9.1 %collective-permute-start.10 = (bf16[288,512]{1,0:T(8,128)(2,1)S(1)}, bf16[288,512]{1,0:T(8,128)(2,1)S(1)}, u32[]{:S(2)}, u32[]{:S(2)}) collective-permute-start(bf16[288,512]{1,0:T(8,128)(2,1)S(1)} %collective-permute-done.6.refs_3_), channel_id=1, source_target_pairs={{0,4},{1,5},{2,6},{3,7},{4,0},{5,1},{6,2},{7,3},{8,12},{9,13},{10,... | collective-permute-start | bytes 884744 | tf_op jit(solution)/shard_map/ppermute | solution.py:293
  80.6 11.7 %collective-permute-start.15 = (bf16[288,512]{1,0:T(8,128)(2,1)S(1)}, bf16[288,512]{1,0:T(8,128)(2,1)S(1)}, u32[]{:S(2)}, u32[]{:S(2)}) collective-permute-start(bf16[288,512]{1,0:T(8,128)(2,1)S(1)} %get-tuple-element.57), channel_id=1, source_target_pairs={{0,4},{1,5},{2,6},{3,7},{4,0},{5,1},{6,2},{7,3},{8,12},{9,13},{10,... | collective-permute-start | bytes 884744 | tf_op jit(solution)/shard_map/ppermute | solution.py:293
  82.6 17.0 %collective-permute-start.12 = (bf16[288,512]{1,0:T(8,128)(2,1)S(1)}, bf16[288,512]{1,0:T(8,128)(2,1)S(1)}, u32[]{:S(2)}, u32[]{:S(2)}) collective-permute-start(bf16[288,512]{1,0:T(8,128)(2,1)S(1)} %get-tuple-element.53), channel_id=1, source_target_pairs={{0,12},{1,13},{2,14},{3,15},{4,8},{5,9},{6,10},{7,11},{8,4},{9,5},... | collective-permute-start | bytes 884744 | tf_op jit(solution)/shard_map/ppermute | solution.py:293
  86.5 15.1 %collective-permute-start.14 = (bf16[288,512]{1,0:T(8,128)(2,1)S(1)}, bf16[288,512]{1,0:T(8,128)(2,1)S(1)}, u32[]{:S(2)}, u32[]{:S(2)}) collective-permute-start(bf16[288,512]{1,0:T(8,128)(2,1)S(1)} %get-tuple-element.55), channel_id=1, source_target_pairs={{0,4},{1,5},{2,6},{3,7},{4,0},{5,1},{6,2},{7,3},{8,12},{9,13},{10,... | collective-permute-start | bytes 884744 | tf_op jit(solution)/shard_map/ppermute | solution.py:293
  92.5 13.0 %collective-permute-start.16 = (bf16[288,512]{1,0:T(8,128)(2,1)S(1)}, bf16[288,512]{1,0:T(8,128)(2,1)S(1)}, u32[]{:S(2)}, u32[]{:S(2)}) collective-permute-start(bf16[288,512]{1,0:T(8,128)(2,1)S(1)} %add_convert_fusion.2), channel_id=1, source_target_pairs={{0,12},{1,13},{2,14},{3,15},{4,8},{5,9},{6,10},{7,11},{8,4},{9,5},... | collective-permute-start | bytes 884744 | tf_op jit(solution)/shard_map/ppermute | solution.py:293
  94.4 16.1 %collective-permute-start.11 = (bf16[288,512]{1,0:T(8,128)(2,1)S(1)}, bf16[288,512]{1,0:T(8,128)(2,1)S(1)}, u32[]{:S(2)}, u32[]{:S(2)}) collective-permute-start(bf16[288,512]{1,0:T(8,128)(2,1)S(1)} %get-tuple-element.51), channel_id=1, source_target_pairs={{0,12},{1,13},{2,14},{3,15},{4,8},{5,9},{6,10},{7,11},{8,4},{9,5},... | collective-permute-start | bytes 884744 | tf_op jit(solution)/shard_map/ppermute | solution.py:293
  99.6 10.8 %collective-permute-start.13 = (bf16[288,512]{1,0:T(8,128)(2,1)S(1)}, bf16[288,512]{1,0:T(8,128)(2,1)S(1)}, u32[]{:S(2)}, u32[]{:S(2)}) collective-permute-start(bf16[288,512]{1,0:T(8,128)(2,1)S(1)} %add_convert_fusion.3), channel_id=1, source_target_pairs={{0,4},{1,5},{2,6},{3,7},{4,0},{5,1},{6,2},{7,3},{8,12},{9,13},{10,... | collective-permute-start | bytes 884744 | tf_op jit(solution)/shard_map/ppermute | solution.py:293
  105.6 10.1 %collective-permute-start.17 = (bf16[288,512]{1,0:T(8,128)(2,1)S(1)}, bf16[288,512]{1,0:T(8,128)(2,1)S(1)}, u32[]{:S(2)}, u32[]{:S(2)}) collective-permute-start(bf16[288,512]{1,0:T(8,128)(2,1)S(1)} %add_convert_fusion.1), channel_id=1, source_target_pairs={{0,2},{1,3},{2,0},{3,1},{4,6},{5,7},{6,4},{7,5},{8,10},{9,11},{10,... | collective-permute-start | bytes 884744 | tf_op jit(solution)/shard_map/ppermute | solution.py:293
  115.9 14.2 %collective-permute-start.18 = (bf16[288,512]{1,0:T(8,128)(2,1)S(1)}, bf16[288,512]{1,0:T(8,128)(2,1)S(1)}, u32[]{:S(2)}, u32[]{:S(2)}) collective-permute-start(bf16[288,512]{1,0:T(8,128)(2,1)S(1)} %add_convert_fusion.refs_0_), channel_id=1, source_target_pairs={{0,496},{16,0},{32,16},{48,32},{64,48},{80,64},{96,80},{112,96},{1... | collective-permute-start | bytes 884744 | tf_op jit(solution)/shard_map/ppermute | solution.py:283
  130.1 10.8 %collective-permute-start.19 = (bf16[288,512]{1,0:T(8,128)(2,1)S(1)}, bf16[288,512]{1,0:T(8,128)(2,1)S(1)}, u32[]{:S(2)}, u32[]{:S(2)}) collective-permute-start(bf16[288,512]{1,0:T(8,128)(2,1)S(1)} %collective-permute-done.18.refs_1_), channel_id=1, source_target_pairs={{0,496},{16,0},{32,16},{48,32},{64,48},{80,64},{96,80},{112,96},{1... | collective-permute-start | bytes 884744 | tf_op jit(solution)/shard_map/ppermute | solution.py:283
  140.9 8.9 %collective-permute-start.20 = (bf16[288,384]{1,0:T(8,128)(2,1)S(1)}, bf16[288,384]{1,0:T(8,128)(2,1)S(1)}, u32[]{:S(2)}, u32[]{:S(2)}) collective-permute-start(bf16[288,384]{1,0:T(8,128)(2,1)S(1)} %slice.4), channel_id=1, source_target_pairs={{0,496},{16,0},{32,16},{48,32},{64,48},{80,64},{96,80},{112,96},{1... | collective-permute-start | bytes 663560 | tf_op jit(solution)/shard_map/ppermute | solution.py:283

commit v3 on v2

--- a/solution.py
+++ b/solution.py
@@ -433,8 +433,8 @@
     here_y = plus(mine_y, to_near(near_y), to_far(forward_y))
     here = plus(mine, to_far(far), to_near(forward), to_y(here_y))
 
+    back2 = along(here, -2)
     back1 = along(here, -1)
-    back2 = along(back1, -1)
     back3 = along(back2[:, TAIL:], -1)
     most, window = call(
         functools.partial(unpack_kernel, replicas),

time: 152 us -> 145 us (0.954)
  waiting for transfers between devices: 54.6 us -> 41.8 us
  starting transfers between devices: 70.4 us -> 76.1 us
    ppermute x6, waiting for transfers between devices: 32.6 us -> 20.8 us  [along(): lax.ppermute(value, 'dp', [(s, (s + steps) % count) for s in range(count)])]
    ppermute x6, starting transfers between devices: 25.8 us -> 31.1 us  [along(): lax.ppermute(value, 'dp', [(s, (s + steps) % count) for s in range(count)])]
  transfers between devices with their start and end apart: 21 -> 21, of which waited for: 13 -> 12; matrix products, arithmetic and copies ran while one was open for 0% -> 0% of each run, Pallas kernels for 6% -> 6%
where the time goes in v3:
time: 145 us; the launch traced here: 144 us
  starting transfers between devices  76.1 us (52%)
  waiting for transfers between devices  41.8 us (29%)
  Pallas kernels  17.1 us (12%)
  blocking collectives  4.72 us (3%)
  local copies, waits for them, and re-layouts  3.11 us (2%)
    ppermute x15, starting transfers between devices, swap(): return lax.ppermute(value, 'mp', pairs)  44.9 us
    ppermute x6, starting transfers between devices, along(): lax.ppermute(value, 'dp', [(s, (s + steps) % count) for s in range(count)])  31.1 us
    ppermute x15, waiting for transfers between devices, swap(): return lax.ppermute(value, 'mp', pairs)  21.1 us
    ppermute x6, waiting for transfers between devices, along(): lax.ppermute(value, 'dp', [(s, (s + steps) % count) for s in range(count)])  20.8 us
    pallas_call x11, Pallas kernels, call(): pl.pallas_call(kernel, out_shape=outs, in_specs=in_specs, out_specs=[VMEM...  13.1 us
    all_gather x2, blocking collectives, of_cores(): return lax.all_gather(value, 'mp', axis_index_groups=groups)  4.72 us
    unnamed x20, local copies, waits for them, and re-layouts  3.02 us
  transfers between devices with their start and end apart: 21, of which 12 were waited for; matrix products, arithmetic and copies ran while one was open for 0% of the time, Pallas kernels for 6%

profile of v3, /device:TPU:6, one launch (start us, length us, event | category | flops | bytes accessed | tf_op | source)
XLA Modules:
  0.0 144.4 jit_solution(3046126524185643599)
XLA Ops:
  0.6 2.3 %shard_map.95 = bf16[288,384]{1,0:T(8,128)(2,1)} custom-call(s32[2,128]{1,0:T(2,128)} %bitcast.15, s32[128]{0:T(128)} %target.11, bf16[288,1536]{1,0:T(8,128)(2,1)} %bitcast.9), custom_call_target="tpu_custom_call" | custom-call | flops 113246208 | bytes 884736 | tf_op jit(solution)/shard_map/pallas_call | solution.py:329
  3.0 3.8 %collective-permute-start = (bf16[288,384]{1,0:T(8,128)(2,1)}, bf16[288,384]{1,0:T(8,128)(2,1)S(1)}, u32[]{:S(2)}, u32[]{:S(2)}) collective-permute-start(bf16[288,384]{1,0:T(8,128)(2,1)} %shard_map.95), channel_id=1, source_target_pairs={{0,16},{16,32},{32,48},{48,64},{64,80},{80,96},{96,112},{112,128},... | collective-permute-start | bytes 663560 | tf_op jit(solution)/shard_map/ppermute | solution.py:283
  9.1 3.8 %collective-permute-start.3 = (bf16[288,512]{1,0:T(8,128)(2,1)S(1)}, bf16[288,512]{1,0:T(8,128)(2,1)S(1)}, u32[]{:S(2)}, u32[]{:S(2)}) collective-permute-start(bf16[288,512]{1,0:T(8,128)(2,1)S(1)} %shard_map.100), channel_id=1, source_target_pairs={{0,16},{16,32},{32,48},{48,64},{64,80},{80,96},{96,112},{112,128},... | collective-permute-start | bytes 884744 | tf_op jit(solution)/shard_map/ppermute | solution.py:283
  17.4 4.3 %collective-permute-done = bf16[288,384]{1,0:T(8,128)(2,1)S(1)} collective-permute-done((bf16[288,384]{1,0:T(8,128)(2,1)}, bf16[288,384]{1,0:T(8,128)(2,1)S(1)}, u32[]{:S(2)}, u32[]{:S(2)}) %collective-permute-start) | collective-permute-done | bytes 221216 | tf_op jit(solution)/shard_map/ppermute | solution.py:283
  21.8 2.1 %collective-permute-start.2 = (bf16[288,512]{1,0:T(8,128)(2,1)S(1)}, bf16[288,512]{1,0:T(8,128)(2,1)S(1)}, u32[]{:S(2)}, u32[]{:S(2)}) collective-permute-start(bf16[288,512]{1,0:T(8,128)(2,1)S(1)} %pad_add_fusion), channel_id=1, source_target_pairs={{0,32},{16,48},{32,64},{48,80},{64,96},{80,112},{96,128},{112,144}... | collective-permute-start | bytes 884744 | tf_op jit(solution)/shard_map/ppermute | solution.py:283
  23.8 1.9 %collective-permute-start.1 = (bf16[8,288,256]{2,1,0:T(8,128)(2,1)S(1)}, bf16[8,288,256]{2,1,0:T(8,128)(2,1)S(1)}, u32[]{:S(2)}, u32[]{:S(2)}) collective-permute-start(bf16[8,288,256]{2,1,0:T(8,128)(2,1)S(1)} %get-tuple-element.38), channel_id=1, source_target_pairs={{0,1},{1,0},{2,3},{3,2},{4,5},{5,4},{6,7},{7,6},{8,9},{9,8},{10,11... | collective-permute-start | bytes 3538952 | tf_op jit(solution)/shard_map/ppermute | solution.py:293
  25.8 2.1 %collective-permute-done.3 = bf16[288,512]{1,0:T(8,128)(2,1)S(1)} collective-permute-done((bf16[288,512]{1,0:T(8,128)(2,1)S(1)}, bf16[288,512]{1,0:T(8,128)(2,1)S(1)}, u32[]{:S(2)}, u32[]{:S(2)}) %collective-permute-start.3) | collective-permute-done | bytes 294944 | tf_op jit(solution)/shard_map/ppermute | solution.py:283
  27.9 10.7 %collective-permute-done.2 = bf16[288,512]{1,0:T(8,128)(2,1)S(1)} collective-permute-done((bf16[288,512]{1,0:T(8,128)(2,1)S(1)}, bf16[288,512]{1,0:T(8,128)(2,1)S(1)}, u32[]{:S(2)}, u32[]{:S(2)}) %collective-permute-start.2) | collective-permute-done | bytes 294944 | tf_op jit(solution)/shard_map/ppermute | solution.py:283
  38.6 4.8 %collective-permute-start.5 = (bf16[288,512]{1,0:T(8,128)(2,1)S(1)}, bf16[288,512]{1,0:T(8,128)(2,1)S(1)}, u32[]{:S(2)}, u32[]{:S(2)}) collective-permute-start(bf16[288,512]{1,0:T(8,128)(2,1)S(1)} %add_add_fusion.refs_0_), channel_id=1, source_target_pairs={{0,2},{1,3},{2,0},{3,1},{4,6},{5,7},{6,4},{7,5},{8,10},{9,11},{10,... | collective-permute-start | bytes 884744 | tf_op jit(solution)/shard_map/ppermute | solution.py:293
  43.4 2.7 %collective-permute-start.4 = (bf16[288,512]{1,0:T(8,128)(2,1)S(1)}, bf16[288,512]{1,0:T(8,128)(2,1)S(1)}, u32[]{:S(2)}, u32[]{:S(2)}) collective-permute-start(bf16[288,512]{1,0:T(8,128)(2,1)S(1)} %add_add_fusion.refs_0_), channel_id=1, source_target_pairs={{0,4},{1,5},{2,6},{3,7},{4,0},{5,1},{6,2},{7,3},{8,12},{9,13},{10,... | collective-permute-start | bytes 884744 | tf_op jit(solution)/shard_map/ppermute | solution.py:293
  46.2 3.0 %collective-permute-done.5.refs_2_ = bf16[288,512]{1,0:T(8,128)(2,1)S(1)} collective-permute-done((bf16[288,512]{1,0:T(8,128)(2,1)S(1)}, bf16[288,512]{1,0:T(8,128)(2,1)S(1)}, u32[]{:S(2)}, u32[]{:S(2)}) %collective-permute-start.5) | collective-permute-done | bytes 294944 | tf_op jit(solution)/shard_map/ppermute | solution.py:293
  49.1 2.4 %collective-permute-start.6 = (bf16[288,512]{1,0:T(8,128)(2,1)S(1)}, bf16[288,512]{1,0:T(8,128)(2,1)S(1)}, u32[]{:S(2)}, u32[]{:S(2)}) collective-permute-start(bf16[288,512]{1,0:T(8,128)(2,1)S(1)} %collective-permute-done.5.refs_2_), channel_id=1, source_target_pairs={{0,12},{1,13},{2,14},{3,15},{4,8},{5,9},{6,10},{7,11},{8,4},{9,5},... | collective-permute-start | bytes 884744 | tf_op jit(solution)/shard_map/ppermute | solution.py:293
  51.5 4.7 %collective-permute-start.7 = (bf16[288,512]{1,0:T(8,128)(2,1)S(1)}, bf16[288,512]{1,0:T(8,128)(2,1)S(1)}, u32[]{:S(2)}, u32[]{:S(2)}) collective-permute-start(bf16[288,512]{1,0:T(8,128)(2,1)S(1)} %add_add_fusion.refs_0_), channel_id=1, source_target_pairs={{0,12},{1,13},{2,14},{3,15},{4,8},{5,9},{6,10},{7,11},{8,4},{9,5},... | collective-permute-start | bytes 884744 | tf_op jit(solution)/shard_map/ppermute | solution.py:293
  58.1 2.7 %collective-permute-start.8 = (bf16[288,512]{1,0:T(8,128)(2,1)S(1)}, bf16[288,512]{1,0:T(8,128)(2,1)S(1)}, u32[]{:S(2)}, u32[]{:S(2)}) collective-permute-start(bf16[288,512]{1,0:T(8,128)(2,1)S(1)} %collective-permute-done.4.refs_1_), channel_id=1, source_target_pairs={{0,12},{1,13},{2,14},{3,15},{4,8},{5,9},{6,10},{7,11},{8,4},{9,5},... | collective-permute-start | bytes 884744 | tf_op jit(solution)/shard_map/ppermute | solution.py:293
  67.9 3.2 %collective-permute-done.8.refs_1_ = bf16[288,512]{1,0:T(8,128)(2,1)S(1)} collective-permute-done((bf16[288,512]{1,0:T(8,128)(2,1)S(1)}, bf16[288,512]{1,0:T(8,128)(2,1)S(1)}, u32[]{:S(2)}, u32[]{:S(2)}) %collective-permute-start.8) | collective-permute-done | bytes 294944 | tf_op jit(solution)/shard_map/ppermute | solution.py:293
  72.3 2.4 %all-gather = bf16[768,512]{1,0:T(8,128)(2,1)S(1)} all-gather(bf16[384,512]{1,0:T(8,128)(2,1)S(1)} %get-tuple-element.42), channel_id=2, replica_groups={{0,1},{2,3},{4,5},{6,7},{8,9},{10,11},{12,13},{14,15},{16,17},{18,19},{..., dimensions={0}, use_global_device_ids=true | all-gather | bytes 1179648 | tf_op jit(solution)/shard_map/all_gather | solution.py:303
  74.7 2.3 %shard_map.103 = (bf16[512,128]{1,0:T(8,128)(2,1)}, bf16[384,512]{1,0:T(8,128)(2,1)S(1)}, f32[256,512]{1,0:T(8,128)S(1)}) custom-call(f32[384,512]{1,0:T(8,128)S(1)} %get-tuple-element.41.kept, bf16[2,384,512]{2,1,0:T(8,128)(2,1)S(1)} %bitcast.12, f32[64,512]{1,0:T(8,128)S(1)} %get-tuple-element.43.cosine, f32[64,512]{1,0:T(8,128)S(1)} %get-tuple-element.44.sine, ...), custom_call_target="tpu_custom_call" | custom-call | flops 469762048 | bytes 3031040 | tf_op jit(solution)/shard_map/pallas_call | solution.py:42
  77.0 2.4 %all-gather.1 = bf16[768,512]{1,0:T(8,128)(2,1)S(1)} all-gather(bf16[384,512]{1,0:T(8,128)(2,1)S(1)} %get-tuple-element.48.sent), channel_id=3, replica_groups={{0,1},{2,3},{4,5},{6,7},{8,9},{10,11},{12,13},{14,15},{16,17},{18,19},{..., dimensions={0}, use_global_device_ids=true | all-gather | bytes 1179648 | tf_op jit(solution)/shard_map/all_gather | solution.py:303
  80.1 2.0 %collective-permute-start.15 = (bf16[288,512]{1,0:T(8,128)(2,1)S(1)}, bf16[288,512]{1,0:T(8,128)(2,1)S(1)}, u32[]{:S(2)}, u32[]{:S(2)}) collective-permute-start(bf16[288,512]{1,0:T(8,128)(2,1)S(1)} %get-tuple-element.57), channel_id=1, source_target_pairs={{0,4},{1,5},{2,6},{3,7},{4,0},{5,1},{6,2},{7,3},{8,12},{9,13},{10,... | collective-permute-start | bytes 884744 | tf_op jit(solution)/shard_map/ppermute | solution.py:293
  82.1 4.1 %collective-permute-start.12 = (bf16[288,512]{1,0:T(8,128)(2,1)S(1)}, bf16[288,512]{1,0:T(8,128)(2,1)S(1)}, u32[]{:S(2)}, u32[]{:S(2)}) collective-permute-start(bf16[288,512]{1,0:T(8,128)(2,1)S(1)} %get-tuple-element.53), channel_id=1, source_target_pairs={{0,12},{1,13},{2,14},{3,15},{4,8},{5,9},{6,10},{7,11},{8,4},{9,5},... | collective-permute-start | bytes 884744 | tf_op jit(solution)/shard_map/ppermute | solution.py:293
  86.2 2.1 %collective-permute-start.14 = (bf16[288,512]{1,0:T(8,128)(2,1)S(1)}, bf16[288,512]{1,0:T(8,128)(2,1)S(1)}, u32[]{:S(2)}, u32[]{:S(2)}) collective-permute-start(bf16[288,512]{1,0:T(8,128)(2,1)S(1)} %get-tuple-element.55), channel_id=1, source_target_pairs={{0,4},{1,5},{2,6},{3,7},{4,0},{5,1},{6,2},{7,3},{8,12},{9,13},{10,... | collective-permute-start | bytes 884744 | tf_op jit(solution)/shard_map/ppermute | solution.py:293
  89.1 2.7 %collective-permute-done.15 = bf16[288,512]{1,0:T(8,128)(2,1)S(1)} collective-permute-done((bf16[288,512]{1,0:T(8,128)(2,1)S(1)}, bf16[288,512]{1,0:T(8,128)(2,1)S(1)}, u32[]{:S(2)}, u32[]{:S(2)}) %collective-permute-start.15) | collective-permute-done | bytes 294944 | tf_op jit(solution)/shard_map/ppermute | solution.py:293
  91.8 2.7 %collective-permute-start.16 = (bf16[288,512]{1,0:T(8,128)(2,1)S(1)}, bf16[288,512]{1,0:T(8,128)(2,1)S(1)}, u32[]{:S(2)}, u32[]{:S(2)}) collective-permute-start(bf16[288,512]{1,0:T(8,128)(2,1)S(1)} %add_convert_fusion.2), channel_id=1, source_target_pairs={{0,12},{1,13},{2,14},{3,15},{4,8},{5,9},{6,10},{7,11},{8,4},{9,5},... | collective-permute-start | bytes 884744 | tf_op jit(solution)/shard_map/ppermute | solution.py:293
  94.5 4.4 %collective-permute-start.11 = (bf16[288,512]{1,0:T(8,128)(2,1)S(1)}, bf16[288,512]{1,0:T(8,128)(2,1)S(1)}, u32[]{:S(2)}, u32[]{:S(2)}) collective-permute-start(bf16[288,512]{1,0:T(8,128)(2,1)S(1)} %get-tuple-element.51), channel_id=1, source_target_pairs={{0,12},{1,13},{2,14},{3,15},{4,8},{5,9},{6,10},{7,11},{8,4},{9,5},... | collective-permute-start | bytes 884744 | tf_op jit(solution)/shard_map/ppermute | solution.py:293
  99.0 1.9 %collective-permute-start.13 = (bf16[288,512]{1,0:T(8,128)(2,1)S(1)}, bf16[288,512]{1,0:T(8,128)(2,1)S(1)}, u32[]{:S(2)}, u32[]{:S(2)}) collective-permute-start(bf16[288,512]{1,0:T(8,128)(2,1)S(1)} %add_convert_fusion.3), channel_id=1, source_target_pairs={{0,4},{1,5},{2,6},{3,7},{4,0},{5,1},{6,2},{7,3},{8,12},{9,13},{10,... | collective-permute-start | bytes 884744 | tf_op jit(solution)/shard_map/ppermute | solution.py:293
  100.9 3.9 %collective-permute-done.16 = bf16[288,512]{1,0:T(8,128)(2,1)S(1)} collective-permute-done((bf16[288,512]{1,0:T(8,128)(2,1)S(1)}, bf16[288,512]{1,0:T(8,128)(2,1)S(1)}, u32[]{:S(2)}, u32[]{:S(2)}) %collective-permute-start.16) | collective-permute-done | bytes 294944 | tf_op jit(solution)/shard_map/ppermute | solution.py:293
  105.0 4.8 %collective-permute-start.17 = (bf16[288,512]{1,0:T(8,128)(2,1)S(1)}, bf16[288,512]{1,0:T(8,128)(2,1)S(1)}, u32[]{:S(2)}, u32[]{:S(2)}) collective-permute-start(bf16[288,512]{1,0:T(8,128)(2,1)S(1)} %add_convert_fusion.1), channel_id=1, source_target_pairs={{0,2},{1,3},{2,0},{3,1},{4,6},{5,7},{6,4},{7,5},{8,10},{9,11},{10,... | collective-permute-start | bytes 884744 | tf_op jit(solution)/shard_map/ppermute | solution.py:293
  109.8 5.3 %collective-permute-done.17 = bf16[288,512]{1,0:T(8,128)(2,1)S(1)} collective-permute-done((bf16[288,512]{1,0:T(8,128)(2,1)S(1)}, bf16[288,512]{1,0:T(8,128)(2,1)S(1)}, u32[]{:S(2)}, u32[]{:S(2)}) %collective-permute-start.17) | collective-permute-done | bytes 294944 | tf_op jit(solution)/shard_map/ppermute | solution.py:293
  117.2 11.3 %collective-permute-start.18 = (bf16[288,512]{1,0:T(8,128)(2,1)S(1)}, bf16[288,512]{1,0:T(8,128)(2,1)S(1)}, u32[]{:S(2)}, u32[]{:S(2)}) collective-permute-start(bf16[288,512]{1,0:T(8,128)(2,1)S(1)} %add_convert_fusion.refs_0_), channel_id=1, source_target_pairs={{0,496},{16,0},{32,16},{48,32},{64,48},{80,64},{96,80},{112,96},{1... | collective-permute-start | bytes 884744 | tf_op jit(solution)/shard_map/ppermute | solution.py:283
  128.5 2.5 %collective-permute-done.19.refs_2_ = bf16[288,512]{1,0:T(8,128)(2,1)S(1)} collective-permute-done((bf16[288,512]{1,0:T(8,128)(2,1)S(1)}, bf16[288,512]{1,0:T(8,128)(2,1)S(1)}, u32[]{:S(2)}, u32[]{:S(2)}) %collective-permute-start.19) | collective-permute-done | bytes 294944 | tf_op jit(solution)/shard_map/ppermute | solution.py:283
  131.1 8.2 %collective-permute-start.20 = (bf16[288,384]{1,0:T(8,128)(2,1)S(1)}, bf16[288,384]{1,0:T(8,128)(2,1)S(1)}, u32[]{:S(2)}, u32[]{:S(2)}) collective-permute-start(bf16[288,384]{1,0:T(8,128)(2,1)S(1)} %slice.4), channel_id=1, source_target_pairs={{0,496},{16,0},{32,16},{48,32},{64,48},{80,64},{96,80},{112,96},{1... | collective-permute-start | bytes 663560 | tf_op jit(solution)/shard_map/ppermute | solution.py:283
  139.3 2.4 %shard_map.106 = (bf16[288,1536]{1,0:T(8,128)(2,1)}, bf16[288,512]{1,0:T(8,128)(2,1)S(1)}) custom-call(s32[2,128]{1,0:T(2,128)S(1)} %bitcast.19, s32[128]{0:T(128)S(1)} %copy-done.7, bf16[288,512]{1,0:T(8,128)(2,1)S(1)} %add_convert_fusion.refs_0_, bf16[288,512]{1,0:T(8,128)(2,1)S(1)} %collective-permute-done.18.refs_1_, ...), custom_call_target="tpu_custom_call" | custom-call | flops 452984832 | bytes 2065920 | tf_op jit(solution)/shard_map/pallas_call | solution.py:42
  (53 shorter events, 23.7 us)
Async XLA Ops:
  0.6 6.2 %copy-start = (bf16[1536,288]{0,1:T(8,128)(2,1)S(1)}, bf16[1536,288]{0,1:T(8,128)(2,1)}, u32[]{:S(2)}) copy-start(bf16[1536,288]{0,1:T(8,128)(2,1)} %param.8) | copy-start | bytes 2654212
  0.6 12.3 %copy-start.1 = (bf16[4608,128]{1,0:T(8,128)(2,1)S(1)}, bf16[4608,128]{1,0:T(8,128)(2,1)}, u32[]{:S(2)}) copy-start(bf16[4608,128]{1,0:T(8,128)(2,1)} %param.9) | copy-start | bytes 3538948
  3.0 18.7 %collective-permute-start = (bf16[288,384]{1,0:T(8,128)(2,1)}, bf16[288,384]{1,0:T(8,128)(2,1)S(1)}, u32[]{:S(2)}, u32[]{:S(2)}) collective-permute-start(bf16[288,384]{1,0:T(8,128)(2,1)} %shard_map.95), channel_id=1, source_target_pairs={{0,16},{16,32},{32,48},{48,64},{64,80},{80,96},{96,112},{112,128},... | collective-permute-start | bytes 663560 | tf_op jit(solution)/shard_map/ppermute | solution.py:283
  6.8 0.7 copy-start.4
  7.5 0.7 copy-start.6
  9.1 18.8 %collective-permute-start.3 = (bf16[288,512]{1,0:T(8,128)(2,1)S(1)}, bf16[288,512]{1,0:T(8,128)(2,1)S(1)}, u32[]{:S(2)}, u32[]{:S(2)}) collective-permute-start(bf16[288,512]{1,0:T(8,128)(2,1)S(1)} %shard_map.100), channel_id=1, source_target_pairs={{0,16},{16,32},{32,48},{48,64},{64,80},{80,96},{96,112},{112,128},... | collective-permute-start | bytes 884744 | tf_op jit(solution)/shard_map/ppermute | solution.py:283
  12.9 1.3 copy-start.2
  14.2 0.7 copy-start.9
  14.2 0.9 copy-start.3
  14.2 0.9 copy-start.5
  14.2 0.9 copy-start.7
  14.2 0.9 copy-start.8
  21.8 16.8 %collective-permute-start.2 = (bf16[288,512]{1,0:T(8,128)(2,1)S(1)}, bf16[288,512]{1,0:T(8,128)(2,1)S(1)}, u32[]{:S(2)}, u32[]{:S(2)}) collective-permute-start(bf16[288,512]{1,0:T(8,128)(2,1)S(1)} %pad_add_fusion), channel_id=1, source_target_pairs={{0,32},{16,48},{32,64},{48,80},{64,96},{80,112},{96,128},{112,144}... | collective-permute-start | bytes 884744 | tf_op jit(solution)/shard_map/ppermute | solution.py:283
  23.8 40.2 %collective-permute-start.1 = (bf16[8,288,256]{2,1,0:T(8,128)(2,1)S(1)}, bf16[8,288,256]{2,1,0:T(8,128)(2,1)S(1)}, u32[]{:S(2)}, u32[]{:S(2)}) collective-permute-start(bf16[8,288,256]{2,1,0:T(8,128)(2,1)S(1)} %get-tuple-element.38), channel_id=1, source_target_pairs={{0,1},{1,0},{2,3},{3,2},{4,5},{5,4},{6,7},{7,6},{8,9},{9,8},{10,11... | collective-permute-start | bytes 3538952 | tf_op jit(solution)/shard_map/ppermute | solution.py:293
  38.6 10.5 %collective-permute-start.5 = (bf16[288,512]{1,0:T(8,128)(2,1)S(1)}, bf16[288,512]{1,0:T(8,128)(2,1)S(1)}, u32[]{:S(2)}, u32[]{:S(2)}) collective-permute-start(bf16[288,512]{1,0:T(8,128)(2,1)S(1)} %add_add_fusion.refs_0_), channel_id=1, source_target_pairs={{0,2},{1,3},{2,0},{3,1},{4,6},{5,7},{6,4},{7,5},{8,10},{9,11},{10,... | collective-permute-start | bytes 884744 | tf_op jit(solution)/shard_map/ppermute | solution.py:293
  43.4 14.7 %collective-permute-start.4 = (bf16[288,512]{1,0:T(8,128)(2,1)S(1)}, bf16[288,512]{1,0:T(8,128)(2,1)S(1)}, u32[]{:S(2)}, u32[]{:S(2)}) collective-permute-start(bf16[288,512]{1,0:T(8,128)(2,1)S(1)} %add_add_fusion.refs_0_), channel_id=1, source_target_pairs={{0,4},{1,5},{2,6},{3,7},{4,0},{5,1},{6,2},{7,3},{8,12},{9,13},{10,... | collective-permute-start | bytes 884744 | tf_op jit(solution)/shard_map/ppermute | solution.py:293
  49.1 13.0 %collective-permute-start.6 = (bf16[288,512]{1,0:T(8,128)(2,1)S(1)}, bf16[288,512]{1,0:T(8,128)(2,1)S(1)}, u32[]{:S(2)}, u32[]{:S(2)}) collective-permute-start(bf16[288,512]{1,0:T(8,128)(2,1)S(1)} %collective-permute-done.5.refs_2_), channel_id=1, source_target_pairs={{0,12},{1,13},{2,14},{3,15},{4,8},{5,9},{6,10},{7,11},{8,4},{9,5},... | collective-permute-start | bytes 884744 | tf_op jit(solution)/shard_map/ppermute | solution.py:293
  51.5 16.4 %collective-permute-start.7 = (bf16[288,512]{1,0:T(8,128)(2,1)S(1)}, bf16[288,512]{1,0:T(8,128)(2,1)S(1)}, u32[]{:S(2)}, u32[]{:S(2)}) collective-permute-start(bf16[288,512]{1,0:T(8,128)(2,1)S(1)} %add_add_fusion.refs_0_), channel_id=1, source_target_pairs={{0,12},{1,13},{2,14},{3,15},{4,8},{5,9},{6,10},{7,11},{8,4},{9,5},... | collective-permute-start | bytes 884744 | tf_op jit(solution)/shard_map/ppermute | solution.py:293
  56.2 11.7 %collective-permute-start.9 = (bf16[288,512]{1,0:T(8,128)(2,1)S(1)}, bf16[288,512]{1,0:T(8,128)(2,1)S(1)}, u32[]{:S(2)}, u32[]{:S(2)}) collective-permute-start(bf16[288,512]{1,0:T(8,128)(2,1)S(1)} %collective-permute-done.5.refs_2_), channel_id=1, source_target_pairs={{0,4},{1,5},{2,6},{3,7},{4,0},{5,1},{6,2},{7,3},{8,12},{9,13},{10,... | collective-permute-start | bytes 884744 | tf_op jit(solution)/shard_map/ppermute | solution.py:293
  58.1 12.9 %collective-permute-start.8 = (bf16[288,512]{1,0:T(8,128)(2,1)S(1)}, bf16[288,512]{1,0:T(8,128)(2,1)S(1)}, u32[]{:S(2)}, u32[]{:S(2)}) collective-permute-start(bf16[288,512]{1,0:T(8,128)(2,1)S(1)} %collective-permute-done.4.refs_1_), channel_id=1, source_target_pairs={{0,12},{1,13},{2,14},{3,15},{4,8},{5,9},{6,10},{7,11},{8,4},{9,5},... | collective-permute-start | bytes 884744 | tf_op jit(solution)/shard_map/ppermute | solution.py:293
  62.2 8.9 %collective-permute-start.10 = (bf16[288,512]{1,0:T(8,128)(2,1)S(1)}, bf16[288,512]{1,0:T(8,128)(2,1)S(1)}, u32[]{:S(2)}, u32[]{:S(2)}) collective-permute-start(bf16[288,512]{1,0:T(8,128)(2,1)S(1)} %collective-permute-done.6.refs_3_), channel_id=1, source_target_pairs={{0,4},{1,5},{2,6},{3,7},{4,0},{5,1},{6,2},{7,3},{8,12},{9,13},{10,... | collective-permute-start | bytes 884744 | tf_op jit(solution)/shard_map/ppermute | solution.py:293
  80.1 11.7 %collective-permute-start.15 = (bf16[288,512]{1,0:T(8,128)(2,1)S(1)}, bf16[288,512]{1,0:T(8,128)(2,1)S(1)}, u32[]{:S(2)}, u32[]{:S(2)}) collective-permute-start(bf16[288,512]{1,0:T(8,128)(2,1)S(1)} %get-tuple-element.57), channel_id=1, source_target_pairs={{0,4},{1,5},{2,6},{3,7},{4,0},{5,1},{6,2},{7,3},{8,12},{9,13},{10,... | collective-permute-start | bytes 884744 | tf_op jit(solution)/shard_map/ppermute | solution.py:293
  82.1 16.8 %collective-permute-start.12 = (bf16[288,512]{1,0:T(8,128)(2,1)S(1)}, bf16[288,512]{1,0:T(8,128)(2,1)S(1)}, u32[]{:S(2)}, u32[]{:S(2)}) collective-permute-start(bf16[288,512]{1,0:T(8,128)(2,1)S(1)} %get-tuple-element.53), channel_id=1, source_target_pairs={{0,12},{1,13},{2,14},{3,15},{4,8},{5,9},{6,10},{7,11},{8,4},{9,5},... | collective-permute-start | bytes 884744 | tf_op jit(solution)/shard_map/ppermute | solution.py:293
  86.2 14.7 %collective-permute-start.14 = (bf16[288,512]{1,0:T(8,128)(2,1)S(1)}, bf16[288,512]{1,0:T(8,128)(2,1)S(1)}, u32[]{:S(2)}, u32[]{:S(2)}) collective-permute-start(bf16[288,512]{1,0:T(8,128)(2,1)S(1)} %get-tuple-element.55), channel_id=1, source_target_pairs={{0,4},{1,5},{2,6},{3,7},{4,0},{5,1},{6,2},{7,3},{8,12},{9,13},{10,... | collective-permute-start | bytes 884744 | tf_op jit(solution)/shard_map/ppermute | solution.py:293
  91.8 13.0 %collective-permute-start.16 = (bf16[288,512]{1,0:T(8,128)(2,1)S(1)}, bf16[288,512]{1,0:T(8,128)(2,1)S(1)}, u32[]{:S(2)}, u32[]{:S(2)}) collective-permute-start(bf16[288,512]{1,0:T(8,128)(2,1)S(1)} %add_convert_fusion.2), channel_id=1, source_target_pairs={{0,12},{1,13},{2,14},{3,15},{4,8},{5,9},{6,10},{7,11},{8,4},{9,5},... | collective-permute-start | bytes 884744 | tf_op jit(solution)/shard_map/ppermute | solution.py:293
  94.5 15.3 %collective-permute-start.11 = (bf16[288,512]{1,0:T(8,128)(2,1)S(1)}, bf16[288,512]{1,0:T(8,128)(2,1)S(1)}, u32[]{:S(2)}, u32[]{:S(2)}) collective-permute-start(bf16[288,512]{1,0:T(8,128)(2,1)S(1)} %get-tuple-element.51), channel_id=1, source_target_pairs={{0,12},{1,13},{2,14},{3,15},{4,8},{5,9},{6,10},{7,11},{8,4},{9,5},... | collective-permute-start | bytes 884744 | tf_op jit(solution)/shard_map/ppermute | solution.py:293
  99.0 10.8 %collective-permute-start.13 = (bf16[288,512]{1,0:T(8,128)(2,1)S(1)}, bf16[288,512]{1,0:T(8,128)(2,1)S(1)}, u32[]{:S(2)}, u32[]{:S(2)}) collective-permute-start(bf16[288,512]{1,0:T(8,128)(2,1)S(1)} %add_convert_fusion.3), channel_id=1, source_target_pairs={{0,4},{1,5},{2,6},{3,7},{4,0},{5,1},{6,2},{7,3},{8,12},{9,13},{10,... | collective-permute-start | bytes 884744 | tf_op jit(solution)/shard_map/ppermute | solution.py:293
  105.0 10.1 %collective-permute-start.17 = (bf16[288,512]{1,0:T(8,128)(2,1)S(1)}, bf16[288,512]{1,0:T(8,128)(2,1)S(1)}, u32[]{:S(2)}, u32[]{:S(2)}) collective-permute-start(bf16[288,512]{1,0:T(8,128)(2,1)S(1)} %add_convert_fusion.1), channel_id=1, source_target_pairs={{0,2},{1,3},{2,0},{3,1},{4,6},{5,7},{6,4},{7,5},{8,10},{9,11},{10,... | collective-permute-start | bytes 884744 | tf_op jit(solution)/shard_map/ppermute | solution.py:293
  115.3 15.7 %collective-permute-start.19 = (bf16[288,512]{1,0:T(8,128)(2,1)S(1)}, bf16[288,512]{1,0:T(8,128)(2,1)S(1)}, u32[]{:S(2)}, u32[]{:S(2)}) collective-permute-start(bf16[288,512]{1,0:T(8,128)(2,1)S(1)} %add_convert_fusion.refs_0_), channel_id=1, source_target_pairs={{0,480},{16,496},{32,0},{48,16},{64,32},{80,48},{96,64},{112,80},{... | collective-permute-start | bytes 884744 | tf_op jit(solution)/shard_map/ppermute | solution.py:283
  117.2 22.1 %collective-permute-start.18 = (bf16[288,512]{1,0:T(8,128)(2,1)S(1)}, bf16[288,512]{1,0:T(8,128)(2,1)S(1)}, u32[]{:S(2)}, u32[]{:S(2)}) collective-permute-start(bf16[288,512]{1,0:T(8,128)(2,1)S(1)} %add_convert_fusion.refs_0_), channel_id=1, source_target_pairs={{0,496},{16,0},{32,16},{48,32},{64,48},{80,64},{96,80},{112,96},{1... | collective-permute-start | bytes 884744 | tf_op jit(solution)/shard_map/ppermute | solution.py:283
  131.1 11.7 %collective-permute-start.20 = (bf16[288,384]{1,0:T(8,128)(2,1)S(1)}, bf16[288,384]{1,0:T(8,128)(2,1)S(1)}, u32[]{:S(2)}, u32[]{:S(2)}) collective-permute-start(bf16[288,384]{1,0:T(8,128)(2,1)S(1)} %slice.4), channel_id=1, source_target_pairs={{0,496},{16,0},{32,16},{48,32},{64,48},{80,64},{96,80},{112,96},{1... | collective-permute-start | bytes 663560 | tf_op jit(solution)/shard_map/ppermute | solution.py:283

commit v4 on v3

--- a/solution.py
+++ b/solution.py
@@ -376,7 +376,6 @@
     )
     other_w = to_core(away_w)
     bucket = jnp.pad(bucket, ((0, 0), (TAIL, 0))) + second
-    bucket, tables, own_w = lax.optimization_barrier((bucket, tables, own_w))
     (turned,) = call(
         turned_kernel,
         [sds((blocks, 4 * HEAD, width), BF16)],

time: 145 us -> 144 us (level)
  local copies, waits for them, and re-layouts: 3.11 us -> 1.47 us
    ppermute x6, waiting for transfers between devices: 20.8 us -> 27.4 us  [along(): lax.ppermute(value, 'dp', [(s, (s + steps) % count) for s in range(count)])]
    ppermute x15, waiting for transfers between devices: 21.1 us -> 15.8 us  [swap(): return lax.ppermute(value, 'mp', pairs)]
    ppermute x6, starting transfers between devices: 31.1 us -> 27.9 us  [along(): lax.ppermute(value, 'dp', [(s, (s + steps) % count) for s in range(count)])]
    ppermute x15, starting transfers between devices: 44.9 us -> 47.1 us  [swap(): return lax.ppermute(value, 'mp', pairs)]
    unnamed x20, local copies, waits for them, and re-layouts: 3.02 us -> 1.38 us
where the time goes in v4:
time: 144 us; the launch traced here: 143 us
  starting transfers between devices  75.1 us (52%)
  waiting for transfers between devices  43.1 us (30%)
  Pallas kernels  17.1 us (12%)
  blocking collectives  4.72 us (3%)
  local copies, waits for them, and re-layouts  1.47 us (1%)
    ppermute x15, starting transfers between devices, swap(): return lax.ppermute(value, 'mp', pairs)  47.1 us
    ppermute x6, starting transfers between devices, along(): lax.ppermute(value, 'dp', [(s, (s + steps) % count) for s in range(count)])  27.9 us
    ppermute x6, waiting for transfers between devices, along(): lax.ppermute(value, 'dp', [(s, (s + steps) % count) for s in range(count)])  27.4 us
    ppermute x15, waiting for transfers between devices, swap(): return lax.ppermute(value, 'mp', pairs)  15.8 us
    pallas_call x11, Pallas kernels, call(): pl.pallas_call(kernel, out_shape=outs, in_specs=in_specs, out_specs=[VMEM...  13.1 us
    all_gather x2, blocking collectives, of_cores(): return lax.all_gather(value, 'mp', axis_index_groups=groups)  4.72 us
  transfers between devices with their start and end apart: 21, of which 12 were waited for; matrix products, arithmetic and copies ran while one was open for 0% of the time, Pallas kernels for 6%

profile of v4, /device:TPU:6, one launch (start us, length us, event | category | flops | bytes accessed | tf_op | source)
XLA Modules:
  0.0 143.1 jit_solution(15631549035005559401)
XLA Ops:
  0.6 2.3 %shard_map.97 = bf16[288,384]{1,0:T(8,128)(2,1)} custom-call(s32[2,128]{1,0:T(2,128)} %bitcast.15, s32[128]{0:T(128)} %target.11, bf16[288,1536]{1,0:T(8,128)(2,1)} %bitcast.9), custom_call_target="tpu_custom_call" | custom-call | flops 113246208 | bytes 884736 | tf_op jit(solution)/shard_map/pallas_call | solution.py:329
  2.9 3.8 %collective-permute-start.1 = (bf16[288,384]{1,0:T(8,128)(2,1)}, bf16[288,384]{1,0:T(8,128)(2,1)S(1)}, u32[]{:S(2)}, u32[]{:S(2)}) collective-permute-start(bf16[288,384]{1,0:T(8,128)(2,1)} %shard_map.97), channel_id=1, source_target_pairs={{0,16},{16,32},{32,48},{48,64},{64,80},{80,96},{96,112},{112,128},... | collective-permute-start | bytes 663560 | tf_op jit(solution)/shard_map/ppermute | solution.py:283
  9.0 4.0 %collective-permute-start.3 = (bf16[288,512]{1,0:T(8,128)(2,1)S(1)}, bf16[288,512]{1,0:T(8,128)(2,1)S(1)}, u32[]{:S(2)}, u32[]{:S(2)}) collective-permute-start(bf16[288,512]{1,0:T(8,128)(2,1)S(1)} %shard_map.99), channel_id=1, source_target_pairs={{0,16},{16,32},{32,48},{48,64},{64,80},{80,96},{96,112},{112,128},... | collective-permute-start | bytes 884744 | tf_op jit(solution)/shard_map/ppermute | solution.py:283
  14.1 7.4 %collective-permute-done.1 = bf16[288,384]{1,0:T(8,128)(2,1)S(1)} collective-permute-done((bf16[288,384]{1,0:T(8,128)(2,1)}, bf16[288,384]{1,0:T(8,128)(2,1)S(1)}, u32[]{:S(2)}, u32[]{:S(2)}) %collective-permute-start.1) | collective-permute-done | bytes 221216 | tf_op jit(solution)/shard_map/ppermute | solution.py:283
  21.6 1.9 %collective-permute-start.2 = (bf16[288,512]{1,0:T(8,128)(2,1)S(1)}, bf16[288,512]{1,0:T(8,128)(2,1)S(1)}, u32[]{:S(2)}, u32[]{:S(2)}) collective-permute-start(bf16[288,512]{1,0:T(8,128)(2,1)S(1)} %pad_add_fusion), channel_id=1, source_target_pairs={{0,32},{16,48},{32,64},{48,80},{64,96},{80,112},{96,128},{112,144}... | collective-permute-start | bytes 884744 | tf_op jit(solution)/shard_map/ppermute | solution.py:283
  24.0 2.1 %collective-permute-start = (bf16[8,288,256]{2,1,0:T(8,128)(2,1)S(1)}, bf16[8,288,256]{2,1,0:T(8,128)(2,1)S(1)}, u32[]{:S(2)}, u32[]{:S(2)}) collective-permute-start(bf16[8,288,256]{2,1,0:T(8,128)(2,1)S(1)} %get-tuple-element.26), channel_id=1, source_target_pairs={{0,1},{1,0},{2,3},{3,2},{4,5},{5,4},{6,7},{7,6},{8,9},{9,8},{10,11... | collective-permute-start | bytes 3538952 | tf_op jit(solution)/shard_map/ppermute | solution.py:293
  27.8 11.5 %collective-permute-done.2 = bf16[288,512]{1,0:T(8,128)(2,1)S(1)} collective-permute-done((bf16[288,512]{1,0:T(8,128)(2,1)S(1)}, bf16[288,512]{1,0:T(8,128)(2,1)S(1)}, u32[]{:S(2)}, u32[]{:S(2)}) %collective-permute-start.2) | collective-permute-done | bytes 294944 | tf_op jit(solution)/shard_map/ppermute | solution.py:283
  39.3 5.2 %collective-permute-start.5 = (bf16[288,512]{1,0:T(8,128)(2,1)S(1)}, bf16[288,512]{1,0:T(8,128)(2,1)S(1)}, u32[]{:S(2)}, u32[]{:S(2)}) collective-permute-start(bf16[288,512]{1,0:T(8,128)(2,1)S(1)} %add_add_fusion.refs_0_), channel_id=1, source_target_pairs={{0,2},{1,3},{2,0},{3,1},{4,6},{5,7},{6,4},{7,5},{8,10},{9,11},{10,... | collective-permute-start | bytes 884744 | tf_op jit(solution)/shard_map/ppermute | solution.py:293
  44.5 2.8 %collective-permute-start.4 = (bf16[288,512]{1,0:T(8,128)(2,1)S(1)}, bf16[288,512]{1,0:T(8,128)(2,1)S(1)}, u32[]{:S(2)}, u32[]{:S(2)}) collective-permute-start(bf16[288,512]{1,0:T(8,128)(2,1)S(1)} %add_add_fusion.refs_0_), channel_id=1, source_target_pairs={{0,4},{1,5},{2,6},{3,7},{4,0},{5,1},{6,2},{7,3},{8,12},{9,13},{10,... | collective-permute-start | bytes 884744 | tf_op jit(solution)/shard_map/ppermute | solution.py:293
  47.3 2.1 %collective-permute-done.5.refs_2_ = bf16[288,512]{1,0:T(8,128)(2,1)S(1)} collective-permute-done((bf16[288,512]{1,0:T(8,128)(2,1)S(1)}, bf16[288,512]{1,0:T(8,128)(2,1)S(1)}, u32[]{:S(2)}, u32[]{:S(2)}) %collective-permute-start.5) | collective-permute-done | bytes 294944 | tf_op jit(solution)/shard_map/ppermute | solution.py:293
  49.5 2.4 %collective-permute-start.6 = (bf16[288,512]{1,0:T(8,128)(2,1)S(1)}, bf16[288,512]{1,0:T(8,128)(2,1)S(1)}, u32[]{:S(2)}, u32[]{:S(2)}) collective-permute-start(bf16[288,512]{1,0:T(8,128)(2,1)S(1)} %collective-permute-done.5.refs_2_), channel_id=1, source_target_pairs={{0,12},{1,13},{2,14},{3,15},{4,8},{5,9},{6,10},{7,11},{8,4},{9,5},... | collective-permute-start | bytes 884744 | tf_op jit(solution)/shard_map/ppermute | solution.py:293
  51.8 4.7 %collective-permute-start.7 = (bf16[288,512]{1,0:T(8,128)(2,1)S(1)}, bf16[288,512]{1,0:T(8,128)(2,1)S(1)}, u32[]{:S(2)}, u32[]{:S(2)}) collective-permute-start(bf16[288,512]{1,0:T(8,128)(2,1)S(1)} %add_add_fusion.refs_0_), channel_id=1, source_target_pairs={{0,12},{1,13},{2,14},{3,15},{4,8},{5,9},{6,10},{7,11},{8,4},{9,5},... | collective-permute-start | bytes 884744 | tf_op jit(solution)/shard_map/ppermute | solution.py:293
  56.5 1.9 %collective-permute-start.9 = (bf16[288,512]{1,0:T(8,128)(2,1)S(1)}, bf16[288,512]{1,0:T(8,128)(2,1)S(1)}, u32[]{:S(2)}, u32[]{:S(2)}) collective-permute-start(bf16[288,512]{1,0:T(8,128)(2,1)S(1)} %collective-permute-done.5.refs_2_), channel_id=1, source_target_pairs={{0,4},{1,5},{2,6},{3,7},{4,0},{5,1},{6,2},{7,3},{8,12},{9,13},{10,... | collective-permute-start | bytes 884744 | tf_op jit(solution)/shard_map/ppermute | solution.py:293
  58.5 2.6 %collective-permute-start.8 = (bf16[288,512]{1,0:T(8,128)(2,1)S(1)}, bf16[288,512]{1,0:T(8,128)(2,1)S(1)}, u32[]{:S(2)}, u32[]{:S(2)}) collective-permute-start(bf16[288,512]{1,0:T(8,128)(2,1)S(1)} %collective-permute-done.4.refs_1_), channel_id=1, source_target_pairs={{0,12},{1,13},{2,14},{3,15},{4,8},{5,9},{6,10},{7,11},{8,4},{9,5},... | collective-permute-start | bytes 884744 | tf_op jit(solution)/shard_map/ppermute | solution.py:293
  61.9 2.5 %collective-permute-start.10 = (bf16[288,512]{1,0:T(8,128)(2,1)S(1)}, bf16[288,512]{1,0:T(8,128)(2,1)S(1)}, u32[]{:S(2)}, u32[]{:S(2)}) collective-permute-start(bf16[288,512]{1,0:T(8,128)(2,1)S(1)} %collective-permute-done.6.refs_3_), channel_id=1, source_target_pairs={{0,4},{1,5},{2,6},{3,7},{4,0},{5,1},{6,2},{7,3},{8,12},{9,13},{10,... | collective-permute-start | bytes 884744 | tf_op jit(solution)/shard_map/ppermute | solution.py:293
  67.7 2.7 %collective-permute-done.8.refs_1_ = bf16[288,512]{1,0:T(8,128)(2,1)S(1)} collective-permute-done((bf16[288,512]{1,0:T(8,128)(2,1)S(1)}, bf16[288,512]{1,0:T(8,128)(2,1)S(1)}, u32[]{:S(2)}, u32[]{:S(2)}) %collective-permute-start.8) | collective-permute-done | bytes 294944 | tf_op jit(solution)/shard_map/ppermute | solution.py:293
  71.7 2.4 %all-gather = bf16[768,512]{1,0:T(8,128)(2,1)S(1)} all-gather(bf16[384,512]{1,0:T(8,128)(2,1)S(1)} %get-tuple-element.30), channel_id=2, replica_groups={{0,1},{2,3},{4,5},{6,7},{8,9},{10,11},{12,13},{14,15},{16,17},{18,19},{..., dimensions={0}, use_global_device_ids=true | all-gather | bytes 1179648 | tf_op jit(solution)/shard_map/all_gather | solution.py:303
  74.1 2.3 %shard_map.103 = (bf16[512,128]{1,0:T(8,128)(2,1)}, bf16[384,512]{1,0:T(8,128)(2,1)S(1)}, f32[256,512]{1,0:T(8,128)S(1)}) custom-call(f32[384,512]{1,0:T(8,128)S(1)} %get-tuple-element.29.kept, bf16[2,384,512]{2,1,0:T(8,128)(2,1)S(1)} %bitcast.12, f32[64,512]{1,0:T(8,128)S(1)} %get-tuple-element.31.cosine, f32[64,512]{1,0:T(8,128)S(1)} %get-tuple-element.32.sine, ...), custom_call_target="tpu_custom_call" | custom-call | flops 469762048 | bytes 3031040 | tf_op jit(solution)/shard_map/pallas_call | solution.py:42
  76.3 2.4 %all-gather.1 = bf16[768,512]{1,0:T(8,128)(2,1)S(1)} all-gather(bf16[384,512]{1,0:T(8,128)(2,1)S(1)} %get-tuple-element.36.sent), channel_id=3, replica_groups={{0,1},{2,3},{4,5},{6,7},{8,9},{10,11},{12,13},{14,15},{16,17},{18,19},{..., dimensions={0}, use_global_device_ids=true | all-gather | bytes 1179648 | tf_op jit(solution)/shard_map/all_gather | solution.py:303
  79.5 2.9 %collective-permute-start.15 = (bf16[288,512]{1,0:T(8,128)(2,1)S(1)}, bf16[288,512]{1,0:T(8,128)(2,1)S(1)}, u32[]{:S(2)}, u32[]{:S(2)}) collective-permute-start(bf16[288,512]{1,0:T(8,128)(2,1)S(1)} %get-tuple-element.45), channel_id=1, source_target_pairs={{0,4},{1,5},{2,6},{3,7},{4,0},{5,1},{6,2},{7,3},{8,12},{9,13},{10,... | collective-permute-start | bytes 884744 | tf_op jit(solution)/shard_map/ppermute | solution.py:293
  82.4 4.1 %collective-permute-start.12 = (bf16[288,512]{1,0:T(8,128)(2,1)S(1)}, bf16[288,512]{1,0:T(8,128)(2,1)S(1)}, u32[]{:S(2)}, u32[]{:S(2)}) collective-permute-start(bf16[288,512]{1,0:T(8,128)(2,1)S(1)} %get-tuple-element.41), channel_id=1, source_target_pairs={{0,12},{1,13},{2,14},{3,15},{4,8},{5,9},{6,10},{7,11},{8,4},{9,5},... | collective-permute-start | bytes 884744 | tf_op jit(solution)/shard_map/ppermute | solution.py:293
  90.5 4.2 %collective-permute-start.16 = (bf16[288,512]{1,0:T(8,128)(2,1)S(1)}, bf16[288,512]{1,0:T(8,128)(2,1)S(1)}, u32[]{:S(2)}, u32[]{:S(2)}) collective-permute-start(bf16[288,512]{1,0:T(8,128)(2,1)S(1)} %add_convert_fusion.2), channel_id=1, source_target_pairs={{0,12},{1,13},{2,14},{3,15},{4,8},{5,9},{6,10},{7,11},{8,4},{9,5},... | collective-permute-start | bytes 884744 | tf_op jit(solution)/shard_map/ppermute | solution.py:293
  94.7 2.9 %collective-permute-start.11 = (bf16[288,512]{1,0:T(8,128)(2,1)S(1)}, bf16[288,512]{1,0:T(8,128)(2,1)S(1)}, u32[]{:S(2)}, u32[]{:S(2)}) collective-permute-start(bf16[288,512]{1,0:T(8,128)(2,1)S(1)} %get-tuple-element.39), channel_id=1, source_target_pairs={{0,12},{1,13},{2,14},{3,15},{4,8},{5,9},{6,10},{7,11},{8,4},{9,5},... | collective-permute-start | bytes 884744 | tf_op jit(solution)/shard_map/ppermute | solution.py:293
  97.7 2.2 %collective-permute-start.13 = (bf16[288,512]{1,0:T(8,128)(2,1)S(1)}, bf16[288,512]{1,0:T(8,128)(2,1)S(1)}, u32[]{:S(2)}, u32[]{:S(2)}) collective-permute-start(bf16[288,512]{1,0:T(8,128)(2,1)S(1)} %add_convert_fusion.3), channel_id=1, source_target_pairs={{0,4},{1,5},{2,6},{3,7},{4,0},{5,1},{6,2},{7,3},{8,12},{9,13},{10,... | collective-permute-start | bytes 884744 | tf_op jit(solution)/shard_map/ppermute | solution.py:293
  99.9 3.7 %collective-permute-done.16 = bf16[288,512]{1,0:T(8,128)(2,1)S(1)} collective-permute-done((bf16[288,512]{1,0:T(8,128)(2,1)S(1)}, bf16[288,512]{1,0:T(8,128)(2,1)S(1)}, u32[]{:S(2)}, u32[]{:S(2)}) %collective-permute-start.16) | collective-permute-done | bytes 294944 | tf_op jit(solution)/shard_map/ppermute | solution.py:293
  103.7 4.9 %collective-permute-start.17 = (bf16[288,512]{1,0:T(8,128)(2,1)S(1)}, bf16[288,512]{1,0:T(8,128)(2,1)S(1)}, u32[]{:S(2)}, u32[]{:S(2)}) collective-permute-start(bf16[288,512]{1,0:T(8,128)(2,1)S(1)} %add_convert_fusion.1), channel_id=1, source_target_pairs={{0,2},{1,3},{2,0},{3,1},{4,6},{5,7},{6,4},{7,5},{8,10},{9,11},{10,... | collective-permute-start | bytes 884744 | tf_op jit(solution)/shard_map/ppermute | solution.py:293
  108.6 5.2 %collective-permute-done.17 = bf16[288,512]{1,0:T(8,128)(2,1)S(1)} collective-permute-done((bf16[288,512]{1,0:T(8,128)(2,1)S(1)}, bf16[288,512]{1,0:T(8,128)(2,1)S(1)}, u32[]{:S(2)}, u32[]{:S(2)}) %collective-permute-start.17) | collective-permute-done | bytes 294944 | tf_op jit(solution)/shard_map/ppermute | solution.py:293
  114.0 2.7 %collective-permute-start.19 = (bf16[288,512]{1,0:T(8,128)(2,1)S(1)}, bf16[288,512]{1,0:T(8,128)(2,1)S(1)}, u32[]{:S(2)}, u32[]{:S(2)}) collective-permute-start(bf16[288,512]{1,0:T(8,128)(2,1)S(1)} %add_convert_fusion.refs_0_), channel_id=1, source_target_pairs={{0,480},{16,496},{32,0},{48,16},{64,32},{80,48},{96,64},{112,80},{... | collective-permute-start | bytes 884744 | tf_op jit(solution)/shard_map/ppermute | solution.py:283
  116.7 8.5 %collective-permute-start.18 = (bf16[288,512]{1,0:T(8,128)(2,1)S(1)}, bf16[288,512]{1,0:T(8,128)(2,1)S(1)}, u32[]{:S(2)}, u32[]{:S(2)}) collective-permute-start(bf16[288,512]{1,0:T(8,128)(2,1)S(1)} %add_convert_fusion.refs_0_), channel_id=1, source_target_pairs={{0,496},{16,0},{32,16},{48,32},{64,48},{80,64},{96,80},{112,96},{1... | collective-permute-start | bytes 884744 | tf_op jit(solution)/shard_map/ppermute | solution.py:283
  125.2 5.4 %collective-permute-done.19.refs_2_ = bf16[288,512]{1,0:T(8,128)(2,1)S(1)} collective-permute-done((bf16[288,512]{1,0:T(8,128)(2,1)S(1)}, bf16[288,512]{1,0:T(8,128)(2,1)S(1)}, u32[]{:S(2)}, u32[]{:S(2)}) %collective-permute-start.19) | collective-permute-done | bytes 294944 | tf_op jit(solution)/shard_map/ppermute | solution.py:283
  130.7 7.0 %collective-permute-start.20 = (bf16[288,384]{1,0:T(8,128)(2,1)S(1)}, bf16[288,384]{1,0:T(8,128)(2,1)S(1)}, u32[]{:S(2)}, u32[]{:S(2)}) collective-permute-start(bf16[288,384]{1,0:T(8,128)(2,1)S(1)} %slice.4), channel_id=1, source_target_pairs={{0,496},{16,0},{32,16},{48,32},{64,48},{80,64},{96,80},{112,96},{1... | collective-permute-start | bytes 663560 | tf_op jit(solution)/shard_map/ppermute | solution.py:283
  137.7 2.4 %shard_map.106 = (bf16[288,1536]{1,0:T(8,128)(2,1)}, bf16[288,512]{1,0:T(8,128)(2,1)S(1)}) custom-call(s32[2,128]{1,0:T(2,128)S(1)} %bitcast.19, s32[128]{0:T(128)S(1)} %copy-done.7, bf16[288,512]{1,0:T(8,128)(2,1)S(1)} %add_convert_fusion.refs_0_, bf16[288,512]{1,0:T(8,128)(2,1)S(1)} %collective-permute-done.18.refs_1_, ...), custom_call_target="tpu_custom_call" | custom-call | flops 452984832 | bytes 2065920 | tf_op jit(solution)/shard_map/pallas_call | solution.py:42
  (53 shorter events, 19.3 us)
Async XLA Ops:
  0.6 6.1 %copy-start = (bf16[1536,288]{0,1:T(8,128)(2,1)S(1)}, bf16[1536,288]{0,1:T(8,128)(2,1)}, u32[]{:S(2)}) copy-start(bf16[1536,288]{0,1:T(8,128)(2,1)} %param.8) | copy-start | bytes 2654212
  2.9 18.6 %collective-permute-start.1 = (bf16[288,384]{1,0:T(8,128)(2,1)}, bf16[288,384]{1,0:T(8,128)(2,1)S(1)}, u32[]{:S(2)}, u32[]{:S(2)}) collective-permute-start(bf16[288,384]{1,0:T(8,128)(2,1)} %shard_map.97), channel_id=1, source_target_pairs={{0,16},{16,32},{32,48},{48,64},{64,80},{80,96},{96,112},{112,128},... | collective-permute-start | bytes 663560 | tf_op jit(solution)/shard_map/ppermute | solution.py:283
  6.8 0.7 copy-start.4
  7.4 0.7 copy-start.6
  8.1 15.4 %copy-start.2 = (bf16[4608,128]{1,0:T(8,128)(2,1)S(1)}, bf16[4608,128]{1,0:T(8,128)(2,1)}, u32[]{:S(2)}) copy-start(bf16[4608,128]{1,0:T(8,128)(2,1)} %param.10) | copy-start | bytes 3538948
  9.0 14.5 %copy-start.1 = (bf16[4608,128]{1,0:T(8,128)(2,1)S(1)}, bf16[4608,128]{1,0:T(8,128)(2,1)}, u32[]{:S(2)}) copy-start(bf16[4608,128]{1,0:T(8,128)(2,1)} %param.9) | copy-start | bytes 3538948
  9.0 18.8 %collective-permute-start.3 = (bf16[288,512]{1,0:T(8,128)(2,1)S(1)}, bf16[288,512]{1,0:T(8,128)(2,1)S(1)}, u32[]{:S(2)}, u32[]{:S(2)}) collective-permute-start(bf16[288,512]{1,0:T(8,128)(2,1)S(1)} %shard_map.99), channel_id=1, source_target_pairs={{0,16},{16,32},{32,48},{48,64},{64,80},{80,96},{96,112},{112,128},... | collective-permute-start | bytes 884744 | tf_op jit(solution)/shard_map/ppermute | solution.py:283
  21.6 17.7 %collective-permute-start.2 = (bf16[288,512]{1,0:T(8,128)(2,1)S(1)}, bf16[288,512]{1,0:T(8,128)(2,1)S(1)}, u32[]{:S(2)}, u32[]{:S(2)}) collective-permute-start(bf16[288,512]{1,0:T(8,128)(2,1)S(1)} %pad_add_fusion), channel_id=1, source_target_pairs={{0,32},{16,48},{32,64},{48,80},{64,96},{80,112},{96,128},{112,144}... | collective-permute-start | bytes 884744 | tf_op jit(solution)/shard_map/ppermute | solution.py:283
  23.9 40.4 %copy-start.9 = (f32[64]{0:T(128)S(1)}, f32[64]{0:T(128)}, u32[]{:S(2)}) copy-start(f32[64]{0:T(128)} %constant.5.clone) | copy-start | bytes 772
  23.9 40.5 %copy-start.3 = (bf16[512,128]{1,0:T(8,128)(2,1)S(1)}, bf16[512,128]{1,0:T(8,128)(2,1)}, u32[]{:S(2)}) copy-start(bf16[512,128]{1,0:T(8,128)(2,1)} %grad.1) | copy-start | bytes 393220
  24.0 40.4 %copy-start.8 = (f32[128]{0:T(128)S(1)}, f32[128]{0:T(128)}, u32[]{:S(2)}) copy-start(f32[128]{0:T(128)} %margins.1) | copy-start | bytes 1540
  24.0 41.6 %collective-permute-start = (bf16[8,288,256]{2,1,0:T(8,128)(2,1)S(1)}, bf16[8,288,256]{2,1,0:T(8,128)(2,1)S(1)}, u32[]{:S(2)}, u32[]{:S(2)}) collective-permute-start(bf16[8,288,256]{2,1,0:T(8,128)(2,1)S(1)} %get-tuple-element.26), channel_id=1, source_target_pairs={{0,1},{1,0},{2,3},{3,2},{4,5},{5,4},{6,7},{7,6},{8,9},{9,8},{10,11... | collective-permute-start | bytes 3538952 | tf_op jit(solution)/shard_map/ppermute | solution.py:293
  39.3 10.1 %collective-permute-start.5 = (bf16[288,512]{1,0:T(8,128)(2,1)S(1)}, bf16[288,512]{1,0:T(8,128)(2,1)S(1)}, u32[]{:S(2)}, u32[]{:S(2)}) collective-permute-start(bf16[288,512]{1,0:T(8,128)(2,1)S(1)} %add_add_fusion.refs_0_), channel_id=1, source_target_pairs={{0,2},{1,3},{2,0},{3,1},{4,6},{5,7},{6,4},{7,5},{8,10},{9,11},{10,... | collective-permute-start | bytes 884744 | tf_op jit(solution)/shard_map/ppermute | solution.py:293
  44.5 13.9 %collective-permute-start.4 = (bf16[288,512]{1,0:T(8,128)(2,1)S(1)}, bf16[288,512]{1,0:T(8,128)(2,1)S(1)}, u32[]{:S(2)}, u32[]{:S(2)}) collective-permute-start(bf16[288,512]{1,0:T(8,128)(2,1)S(1)} %add_add_fusion.refs_0_), channel_id=1, source_target_pairs={{0,4},{1,5},{2,6},{3,7},{4,0},{5,1},{6,2},{7,3},{8,12},{9,13},{10,... | collective-permute-start | bytes 884744 | tf_op jit(solution)/shard_map/ppermute | solution.py:293
  49.5 12.4 %collective-permute-start.6 = (bf16[288,512]{1,0:T(8,128)(2,1)S(1)}, bf16[288,512]{1,0:T(8,128)(2,1)S(1)}, u32[]{:S(2)}, u32[]{:S(2)}) collective-permute-start(bf16[288,512]{1,0:T(8,128)(2,1)S(1)} %collective-permute-done.5.refs_2_), channel_id=1, source_target_pairs={{0,12},{1,13},{2,14},{3,15},{4,8},{5,9},{6,10},{7,11},{8,4},{9,5},... | collective-permute-start | bytes 884744 | tf_op jit(solution)/shard_map/ppermute | solution.py:293
  51.8 15.8 %collective-permute-start.7 = (bf16[288,512]{1,0:T(8,128)(2,1)S(1)}, bf16[288,512]{1,0:T(8,128)(2,1)S(1)}, u32[]{:S(2)}, u32[]{:S(2)}) collective-permute-start(bf16[288,512]{1,0:T(8,128)(2,1)S(1)} %add_add_fusion.refs_0_), channel_id=1, source_target_pairs={{0,12},{1,13},{2,14},{3,15},{4,8},{5,9},{6,10},{7,11},{8,4},{9,5},... | collective-permute-start | bytes 884744 | tf_op jit(solution)/shard_map/ppermute | solution.py:293
  56.5 11.2 %collective-permute-start.9 = (bf16[288,512]{1,0:T(8,128)(2,1)S(1)}, bf16[288,512]{1,0:T(8,128)(2,1)S(1)}, u32[]{:S(2)}, u32[]{:S(2)}) collective-permute-start(bf16[288,512]{1,0:T(8,128)(2,1)S(1)} %collective-permute-done.5.refs_2_), channel_id=1, source_target_pairs={{0,4},{1,5},{2,6},{3,7},{4,0},{5,1},{6,2},{7,3},{8,12},{9,13},{10,... | collective-permute-start | bytes 884744 | tf_op jit(solution)/shard_map/ppermute | solution.py:293
  58.5 11.9 %collective-permute-start.8 = (bf16[288,512]{1,0:T(8,128)(2,1)S(1)}, bf16[288,512]{1,0:T(8,128)(2,1)S(1)}, u32[]{:S(2)}, u32[]{:S(2)}) collective-permute-start(bf16[288,512]{1,0:T(8,128)(2,1)S(1)} %collective-permute-done.4.refs_1_), channel_id=1, source_target_pairs={{0,12},{1,13},{2,14},{3,15},{4,8},{5,9},{6,10},{7,11},{8,4},{9,5},... | collective-permute-start | bytes 884744 | tf_op jit(solution)/shard_map/ppermute | solution.py:293
  61.9 8.6 %collective-permute-start.10 = (bf16[288,512]{1,0:T(8,128)(2,1)S(1)}, bf16[288,512]{1,0:T(8,128)(2,1)S(1)}, u32[]{:S(2)}, u32[]{:S(2)}) collective-permute-start(bf16[288,512]{1,0:T(8,128)(2,1)S(1)} %collective-permute-done.6.refs_3_), channel_id=1, source_target_pairs={{0,4},{1,5},{2,6},{3,7},{4,0},{5,1},{6,2},{7,3},{8,12},{9,13},{10,... | collective-permute-start | bytes 884744 | tf_op jit(solution)/shard_map/ppermute | solution.py:293
  79.5 10.9 %collective-permute-start.15 = (bf16[288,512]{1,0:T(8,128)(2,1)S(1)}, bf16[288,512]{1,0:T(8,128)(2,1)S(1)}, u32[]{:S(2)}, u32[]{:S(2)}) collective-permute-start(bf16[288,512]{1,0:T(8,128)(2,1)S(1)} %get-tuple-element.45), channel_id=1, source_target_pairs={{0,4},{1,5},{2,6},{3,7},{4,0},{5,1},{6,2},{7,3},{8,12},{9,13},{10,... | collective-permute-start | bytes 884744 | tf_op jit(solution)/shard_map/ppermute | solution.py:293
  82.4 15.2 %collective-permute-start.12 = (bf16[288,512]{1,0:T(8,128)(2,1)S(1)}, bf16[288,512]{1,0:T(8,128)(2,1)S(1)}, u32[]{:S(2)}, u32[]{:S(2)}) collective-permute-start(bf16[288,512]{1,0:T(8,128)(2,1)S(1)} %get-tuple-element.41), channel_id=1, source_target_pairs={{0,12},{1,13},{2,14},{3,15},{4,8},{5,9},{6,10},{7,11},{8,4},{9,5},... | collective-permute-start | bytes 884744 | tf_op jit(solution)/shard_map/ppermute | solution.py:293
  86.5 13.4 %collective-permute-start.14 = (bf16[288,512]{1,0:T(8,128)(2,1)S(1)}, bf16[288,512]{1,0:T(8,128)(2,1)S(1)}, u32[]{:S(2)}, u32[]{:S(2)}) collective-permute-start(bf16[288,512]{1,0:T(8,128)(2,1)S(1)} %get-tuple-element.43), channel_id=1, source_target_pairs={{0,4},{1,5},{2,6},{3,7},{4,0},{5,1},{6,2},{7,3},{8,12},{9,13},{10,... | collective-permute-start | bytes 884744 | tf_op jit(solution)/shard_map/ppermute | solution.py:293
  90.5 13.0 %collective-permute-start.16 = (bf16[288,512]{1,0:T(8,128)(2,1)S(1)}, bf16[288,512]{1,0:T(8,128)(2,1)S(1)}, u32[]{:S(2)}, u32[]{:S(2)}) collective-permute-start(bf16[288,512]{1,0:T(8,128)(2,1)S(1)} %add_convert_fusion.2), channel_id=1, source_target_pairs={{0,12},{1,13},{2,14},{3,15},{4,8},{5,9},{6,10},{7,11},{8,4},{9,5},... | collective-permute-start | bytes 884744 | tf_op jit(solution)/shard_map/ppermute | solution.py:293
  94.7 13.9 %collective-permute-start.11 = (bf16[288,512]{1,0:T(8,128)(2,1)S(1)}, bf16[288,512]{1,0:T(8,128)(2,1)S(1)}, u32[]{:S(2)}, u32[]{:S(2)}) collective-permute-start(bf16[288,512]{1,0:T(8,128)(2,1)S(1)} %get-tuple-element.39), channel_id=1, source_target_pairs={{0,12},{1,13},{2,14},{3,15},{4,8},{5,9},{6,10},{7,11},{8,4},{9,5},... | collective-permute-start | bytes 884744 | tf_op jit(solution)/shard_map/ppermute | solution.py:293
  97.7 10.9 %collective-permute-start.13 = (bf16[288,512]{1,0:T(8,128)(2,1)S(1)}, bf16[288,512]{1,0:T(8,128)(2,1)S(1)}, u32[]{:S(2)}, u32[]{:S(2)}) collective-permute-start(bf16[288,512]{1,0:T(8,128)(2,1)S(1)} %add_convert_fusion.3), channel_id=1, source_target_pairs={{0,4},{1,5},{2,6},{3,7},{4,0},{5,1},{6,2},{7,3},{8,12},{9,13},{10,... | collective-permute-start | bytes 884744 | tf_op jit(solution)/shard_map/ppermute | solution.py:293
  103.7 34.0 %copy-start.5 = (s32[128,2]{0,1:T(2,128)S(1)}, s32[128,2]{0,1:T(2,128)}, u32[]{:S(2)}) copy-start(s32[128,2]{0,1:T(2,128)} %param.11) | copy-start | bytes 3076
  103.7 34.0 %copy-start.7 = (s32[128]{0:T(128)S(1)}, s32[128]{0:T(128)}, u32[]{:S(2)}) copy-start(s32[128]{0:T(128)} %target.11) | copy-start | bytes 1540
  103.7 10.1 %collective-permute-start.17 = (bf16[288,512]{1,0:T(8,128)(2,1)S(1)}, bf16[288,512]{1,0:T(8,128)(2,1)S(1)}, u32[]{:S(2)}, u32[]{:S(2)}) collective-permute-start(bf16[288,512]{1,0:T(8,128)(2,1)S(1)} %add_convert_fusion.1), channel_id=1, source_target_pairs={{0,2},{1,3},{2,0},{3,1},{4,6},{5,7},{6,4},{7,5},{8,10},{9,11},{10,... | collective-permute-start | bytes 884744 | tf_op jit(solution)/shard_map/ppermute | solution.py:293
  114.0 16.6 %collective-permute-start.19 = (bf16[288,512]{1,0:T(8,128)(2,1)S(1)}, bf16[288,512]{1,0:T(8,128)(2,1)S(1)}, u32[]{:S(2)}, u32[]{:S(2)}) collective-permute-start(bf16[288,512]{1,0:T(8,128)(2,1)S(1)} %add_convert_fusion.refs_0_), channel_id=1, source_target_pairs={{0,480},{16,496},{32,0},{48,16},{64,32},{80,48},{96,64},{112,80},{... | collective-permute-start | bytes 884744 | tf_op jit(solution)/shard_map/ppermute | solution.py:283
  116.7 21.0 %collective-permute-start.18 = (bf16[288,512]{1,0:T(8,128)(2,1)S(1)}, bf16[288,512]{1,0:T(8,128)(2,1)S(1)}, u32[]{:S(2)}, u32[]{:S(2)}) collective-permute-start(bf16[288,512]{1,0:T(8,128)(2,1)S(1)} %add_convert_fusion.refs_0_), channel_id=1, source_target_pairs={{0,496},{16,0},{32,16},{48,32},{64,48},{80,64},{96,80},{112,96},{1... | collective-permute-start | bytes 884744 | tf_op jit(solution)/shard_map/ppermute | solution.py:283
  130.7 10.7 %collective-permute-start.20 = (bf16[288,384]{1,0:T(8,128)(2,1)S(1)}, bf16[288,384]{1,0:T(8,128)(2,1)S(1)}, u32[]{:S(2)}, u32[]{:S(2)}) collective-permute-start(bf16[288,384]{1,0:T(8,128)(2,1)S(1)} %slice.4), channel_id=1, source_target_pairs={{0,496},{16,0},{32,16},{48,32},{64,48},{80,64},{96,80},{112,96},{1... | collective-permute-start | bytes 663560 | tf_op jit(solution)/shard_map/ppermute | solution.py:283
